TPU v7x, 1024 devices: a whole 4x4x32 slice. The times are simulated.
1024 devices in a mesh: outer: 32 (over x, z_lo), inner: 32 (over y, z_hi, core).
Axes of the slice: x: 4, y: 4, z: 32 (z_hi: 4, z_lo: 8; z = z_hi * 8 + z_lo), core: 2. Of those that a mesh axis runs over, the one named last changes fastest.
Arguments:
- out_grad: bfloat16 [196608, 8192], P(('outer', 'inner')), may hold values from -6 to 6
- hidden: bfloat16 [196608, 128], P(('outer', 'inner')), may hold values from -0.0546875 to 0.0546875
- weight: bfloat16 [128, 8192], P(None, 'inner'), may hold values from -0.0625 to 0.0625
- first_exponent: int32 [131072, 64], P(('outer', 'inner')), may hold values from -16 to -8
- second_exponent: int32 [4096, 64], P('outer', 'inner'), may hold values from -14 to -6
Outputs:
- hidden_grad: bfloat16 [196608, 128], P(('outer', 'inner'))
- weight_grad: float32 [128, 8192], P('outer', 'inner')
All inputs are finite; a program needn't handle non-finite values.
Results may differ from a plain program's by a relative error of at most 0.01.
Values may be sent and summed in bfloat16 or wider, within the bound.
No kernel may reach another device: no remote copies, remote signals or barrier semaphores. Data moves between devices by JAX's collectives and lax.ppermute only.
A program may use at most 32 MiB of HBM per device.

v0:
```python
import jax
import jax.numpy as jnp
from jax import lax
from jax.sharding import PartitionSpec as P


def quantize(values, exponents):
    shape = values.shape
    scale = jnp.exp2(exponents.astype(jnp.float32))[..., None]
    blocks = values.reshape(shape[:-1] + (shape[-1] // 128, 128))
    clipped = jnp.clip(blocks / scale, -448.0, 448.0).astype(jnp.bfloat16)
    return (clipped.astype(jnp.float32) * scale).astype(jnp.bfloat16).reshape(shape)


def per_device(out_grad, hidden, weight, first_exponent, second_exponent):
    hidden_grad = lax.dot_general(
        out_grad,
        lax.all_gather(weight, "inner", axis=1, tiled=True),
        (((1,), (1,)), ((), ())),
        preferred_element_type=jnp.float32,
    ).astype(jnp.bfloat16)
    local_grad = lax.dot_general(
        hidden, out_grad, (((0,), (0,)), ((), ())), preferred_element_type=jnp.float32
    )
    quantized = quantize(local_grad, first_exponent)
    inner_total = lax.psum_scatter(
        quantized.astype(jnp.float32), "inner", scatter_dimension=1, tiled=True
    )
    requantized = quantize(inner_total, second_exponent)
    weight_grad = lax.psum_scatter(
        requantized.astype(jnp.float32), "outer", scatter_dimension=0, tiled=True
    )
    return (hidden_grad, weight_grad)


def solution(mesh):
    in_specs = (
        P(("outer", "inner"), None),
        P(("outer", "inner"), None),
        P(None, "inner"),
        P(("outer", "inner"), None),
        P("outer", "inner"),
    )
    out_specs = (P(("outer", "inner"), None), P("outer", "inner"))
    return jax.shard_map(
        per_device, mesh=mesh, in_specs=in_specs, out_specs=out_specs, check_vma=False
    )
```

profile of v0, /device:TPU:1, one launch (start us, length us, event | category | flops | bytes accessed | tf_op | source)
XLA Modules:
  0.0 818.5 jit_solution(15247045358140615181)
XLA Ops:
  7.2 0.0 copy-start
  7.2 0.0 copy-start.2
  7.2 0.0 reduce-scatter.2.cloned.1.call-start
  7.2 0.9 multiply_exponential_fusion
  8.2 0.1 copy.9
  8.3 1.1 div.22
  9.4 0.0 copy-done
  9.4 0.0 copy-done.2
  9.4 5.1 fusion.5
  14.6 0.0 copy-start.1
  14.6 0.0 reduce-scatter.2.cloned.1.call-update
  14.6 0.0 all-gather.2.cloned.1.call-start
  14.6 0.7 all-gather.2.cloned.1.call-update
  15.3 0.0 all-reduce.3.cloned.1.call-start
  15.4 0.0 copy-done.1
  15.4 0.1 copy.10
  15.5 1.3 dynamic-slice
  17.5 233.5 %reduce-scatter.2.cloned.1.call-done = f32[128,256]{1,0:T(8,128)} async-done(((f32[128,8192]{1,0:T(8,128)}), f32[128,256]{1,0:T(8,128)}) %reduce-scatter.2.cloned.1.call-update) | async-done | bytes 131088 | tf_op jit(solution)/shard_map/reduce_scatter | solution.py:26
  250.9 0.2 div.25
  251.1 1.6 fusion.9
  252.7 0.0 all-reduce.3.cloned.1.call-update
  252.7 130.2 %all-gather.2.cloned.1.call-done = bf16[128,8192]{1,0:T(8,128)(2,1)} async-done(((bf16[128,256]{1,0:T(8,128)(2,1)}), bf16[128,8192]{1,0:T(8,128)(2,1)}) %all-gather.2.cloned.1.call-update) | async-done | bytes 2097168 | tf_op jit(solution)/shard_map/all_gather | solution.py:18
  382.9 3.2 convolution_convert_fusion
  386.1 424.6 %all-reduce.3.cloned.1.call-done = f32[128,256]{1,0:T(8,128)} async-done(((f32[128,256]{1,0:T(8,128)}), f32[128,256]{1,0:T(8,128)}) %all-reduce.3.cloned.1.call-update) | async-done | bytes 131088
  810.7 1.3 constant_dynamic-slice_fusion
  (1 shorter events, 0.0 us)
Async XLA Ops:
  7.2 2.2 copy-start
  7.2 2.2 copy-start.2
  7.2 243.8 %reduce-scatter.2.cloned.1.call-start = ((), (), s32[]{:S(2)}) async-start(), calls=%async_computation.2 | async-start | bytes 4325376 | tf_op jit(solution)/shard_map/reduce_scatter | solution.py:26
  14.6 0.8 copy-start.1
  14.6 368.3 %all-gather.2.cloned.1.call-start = ((), (), s32[]{:S(2)}) async-start(), calls=%async_computation.1 | async-start | bytes 2162688 | tf_op jit(solution)/shard_map/all_gather | solution.py:18
  15.3 795.3 %all-reduce.3.cloned.1.call-start = ((), (), s32[]{:S(2)}) async-start(), calls=%async_computation.3 | async-start | bytes 262144
Sparse Core Ops, SparseCore 0:
  14.7 236.1 reduce-scatter.1
  255.9 126.9 all-gather.1
  386.8 423.8 all-reduce.2
where the time goes:
time: 832 us; the launch traced here: 819 us
  waiting for transfers between devices  789 us (95%)
  between operations  14.5 us (2%)
  matrix products  8.33 us (1%)
    unnamed x4, waiting for transfers between devices  425 us
    reduce_scatter x1, waiting for transfers between devices, per_device(): lax.psum_scatter(quantized.astype(jnp.float32), 'inner', scatter_dimensio...  233 us
    all_gather x1, waiting for transfers between devices, per_device(): lax.all_gather(weight, 'inner', axis=1, tiled=True)  130 us
  transfers between devices with their start and end apart: 3, of which 3 were waited for; matrix products, arithmetic and copies ran while one was open for 1% of the time, Pallas kernels for 0%

commit v1 on v0

v1 whole, which is shorter than its diff:
```python
import jax
import jax.numpy as jnp
from jax import lax
from jax.experimental import pallas as pl
from jax.experimental.pallas import tpu as pltpu
from jax.sharding import Mesh, PartitionSpec as P

SIZES = {"x": 4, "zl": 8, "y": 4, "zh": 4, "c": 2}
AXES = tuple(SIZES)
OUTER = ("x", "zl")
LIMIT = 448.0


def shifted(value, axis, k):
    n = SIZES[axis]
    return lax.ppermute(value, axis, [(i, (i - k) % n) for i in range(n)])


def sent(value, axis, k):
    return shifted(value, axis, -k)


def grad_kernel(pos, hid, og_own, og_oth, e1, own, oth):
    j, c = pl.program_id(0), pos[0]
    bound = (jnp.left_shift(1, e1[...] + 16).astype(jnp.float32) * (LIMIT * 2.0**-16)).astype(jnp.bfloat16)
    rows = lax.broadcasted_iota(jnp.int32, (64, 256), 0)
    lanes = lax.broadcasted_iota(jnp.int32, (64, 256), 1) // 128
    for core, og, out in ((c, og_own, own), (1 - c, og_oth, oth)):
        pick = (rows == (2 * j + core) * 2 + lanes).astype(jnp.bfloat16)
        limit = jnp.dot(bound, pick, preferred_element_type=jnp.float32)
        local = lax.dot_general(hid[...], og[...], (((0,), (0,)), ((), ())), preferred_element_type=jnp.float32)
        out[0] = jnp.clip(local, -limit, limit).astype(jnp.bfloat16)


def local_grads(pos, hidden, out_grad, e1):
    block = jax.ShapeDtypeStruct((16, 128, 256), jnp.bfloat16)
    return pl.pallas_call(
        grad_kernel,
        grid_spec=pltpu.PrefetchScalarGridSpec(
            num_scalar_prefetch=1,
            grid=(16,),
            in_specs=[
                pl.BlockSpec((192, 128), lambda j, pos: (0, 0)),
                pl.BlockSpec((192, 256), lambda j, pos: (0, 2 * j + pos[0])),
                pl.BlockSpec((192, 256), lambda j, pos: (0, 2 * j + 1 - pos[0])),
                pl.BlockSpec((128, 64), lambda j, pos: (0, 0)),
            ],
            out_specs=[pl.BlockSpec((1, 128, 256), lambda j, pos: (j, 0, 0))] * 2,
        ),
        out_shape=[block, block],
        cost_estimate=pl.CostEstimate(flops=2 * 192 * 128 * 8192, bytes_accessed=5 << 20, transcendentals=0),
        name="local_grads",
    )(pos, hidden, out_grad, out_grad, e1)


def hidden_kernel(pos, og, own, oth, out, wide, total):
    c, x, zh = pos[0], pos[1], pos[3]
    step = pl.program_id(0)

    @pl.when(step == 0)
    def _():
        total[...] = jnp.zeros_like(total)

    acc = total[...]
    for kz in range(4):
        at = lax.rem(zh + kz, 4) * 512
        for side, (core, part) in enumerate(((c, own), (1 - c, oth))):
            slot = 2 * kz + side
            for kx in range(4):
                row = pl.multiple_of(lax.rem(x + kx, 4) * 32, 32)
                wide[slot, pl.ds(row, 32), :] = part[kx, 0, kz]
            cols = og[:, pl.ds(pl.multiple_of(at + core * 256, 256), 256)]
            acc += lax.dot_general(cols, wide[slot], (((1,), (1,)), ((), ())), preferred_element_type=jnp.float32)
    total[...] = acc

    @pl.when(step == 3)
    def _():
        out[...] = total[...].astype(jnp.bfloat16)


def hidden_grads(pos, out_grad, own, oth):
    part = pl.BlockSpec((4, 1, 4, 32, 256), lambda k, pos: (0, k, 0, 0, 0))
    return pl.pallas_call(
        hidden_kernel,
        grid_spec=pltpu.PrefetchScalarGridSpec(
            num_scalar_prefetch=1,
            grid=(4,),
            in_specs=[pl.BlockSpec((192, 2048), lambda k, pos: (0, lax.rem(pos[2] + k, 4))), part, part],
            out_specs=pl.BlockSpec((192, 128), lambda k, pos: (0, 0)),
            scratch_shapes=[pltpu.VMEM((8, 128, 256), jnp.bfloat16), pltpu.VMEM((192, 128), jnp.float32)],
        ),
        out_shape=jax.ShapeDtypeStruct((192, 128), jnp.bfloat16),
        cost_estimate=pl.CostEstimate(flops=2 * 192 * 128 * 8192, bytes_accessed=5 << 20, transcendentals=0),
        name="hidden_grads",
    )(pos, out_grad, own, oth)


def gather(value, axis):
    return jnp.stack([value] + [shifted(value, axis, k) for k in (1, 2, 3)])


def per_device(out_grad, hidden, weight, e1, e2):
    x, y, zh, c = (lax.axis_index(a) for a in ("x", "y", "zh", "c"))
    pos = jnp.stack([c, x, y, zh]).astype(jnp.int32)
    f32, bf16 = jnp.float32, jnp.bfloat16

    own, oth = local_grads(pos, hidden, out_grad, e1)
    got = shifted(oth, "c", 1)
    pair = (own.astype(f32) + got.astype(f32)).astype(bf16).reshape(4, 4, 128, 256)
    cols = lax.all_to_all(pair, "y", 0, 0, tiled=True)
    line = cols.astype(f32).sum(0).astype(bf16)
    group = lax.dynamic_index_in_dim(line, zh, 0, False).astype(f32)
    for k in (1, 2, 3):
        block = lax.dynamic_index_in_dim(line, lax.rem(zh + k, 4), 0, False)
        group = group + sent(block, "zh", k).astype(f32)
    limit = jnp.left_shift(1, e2 + 16).astype(f32) * (LIMIT * 2.0**-16)
    limit = jnp.repeat(limit, 128, axis=1)
    again = jnp.clip(group, -limit, limit).astype(bf16)
    rows = lax.all_to_all(again.reshape(SIZES["x"] * SIZES["zl"], -1, 256), OUTER, 0, 0, tiled=True)
    weight_grad = rows.astype(f32).sum(0)

    part = lax.dynamic_slice_in_dim(weight, x * 32, 32, 0)
    part = gather(part, "zh")
    part = gather(part, "y")
    part = gather(part, "x")
    hidden_grad = hidden_grads(pos, out_grad, part, shifted(part, "c", 1))
    return hidden_grad, weight_grad


def solution(mesh):
    fine = Mesh(mesh.devices.reshape(tuple(SIZES.values())), AXES)
    every, inner = P(AXES, None), ("y", "zh", "c")
    return jax.shard_map(
        per_device,
        mesh=fine,
        in_specs=(every, every, P(None, inner), every, P(OUTER, inner)),
        out_specs=(every, P(OUTER, inner)),
        check_vma=False,
    )
```

time: 832 us -> 175 us (0.21); the launches traced: 819 us -> 174 us
  waiting for transfers between devices: 789 us -> 48.4 us
  starting transfers between devices: 0.12 us -> 99.5 us
  Pallas kernels: 0 us -> 17.1 us
  between operations: 14.5 us -> 0.95 us
  matrix products: 8.33 us -> 0 us
    unnamed x4 -> x0, waiting for transfers between devices: 425 us -> none
    reduce_scatter x1 -> x0, waiting for transfers between devices: 233 us -> none  [per_device(): lax.psum_scatter(quantized.astype(jnp.float32), 'inner', scatter_dimensio...]
    all_gather x1 -> x0, waiting for transfers between devices: 130 us -> none  [per_device(): lax.all_gather(weight, 'inner', axis=1, tiled=True)]
    ppermute x0 -> x14, starting transfers between devices: none -> 91.5 us  [shifted(): return lax.ppermute(value, axis, [(i, (i - k) % n) for i in range(n)])]
    ppermute x0 -> x14, waiting for transfers between devices: none -> 43.2 us  [shifted(): return lax.ppermute(value, axis, [(i, (i - k) % n) for i in range(n)])]
    pallas_call x0 -> x2, Pallas kernels: none -> 17.1 us  [the longest x1 11.8 us: local_grads(): pl.pallas_call(grad_kernel, grid_spec=pltpu.PrefetchScalarGridSpec(num_sc...]
    dot_general x2 -> x0, matrix products: 8.33 us -> none  [the longest x1 5.15 us: per_device(): lax.dot_general(hidden, out_grad, (((0,), (0,)), ((), ())), preferred_ele...]
  transfers between devices with their start and end apart: 3 -> 16, of which waited for: 3 -> 7; matrix products, arithmetic and copies ran while one was open for 1% -> 2% of each run, Pallas kernels for 0% -> 3%
where the time goes in v1:
time: 175 us; the launch traced here: 174 us
  starting transfers between devices  99.5 us (57%)
  waiting for transfers between devices  48.4 us (28%)
  Pallas kernels  17.1 us (10%)
  other arithmetic  4.28 us (2%)
  local copies, waits for them, and re-layouts  3.5 us (2%)
    ppermute x14, starting transfers between devices, shifted(): return lax.ppermute(value, axis, [(i, (i - k) % n) for i in range(n)])  91.5 us
    ppermute x14, waiting for transfers between devices, shifted(): return lax.ppermute(value, axis, [(i, (i - k) % n) for i in range(n)])  43.2 us
    pallas_call x1, Pallas kernels, local_grads(): pl.pallas_call(grad_kernel, grid_spec=pltpu.PrefetchScalarGridSpec(num_sc...  11.8 us
    pallas_call x1, Pallas kernels, hidden_grads(): pl.pallas_call(hidden_kernel, grid_spec=pltpu.PrefetchScalarGridSpec(num_...  5.28 us
    all_to_all x1, waiting for transfers between devices, per_device(): lax.all_to_all(again.reshape(SIZES['x'] * SIZES['zl'], -1, 256), OUTER, 0...  5.22 us
    all_to_all x1, starting transfers between devices, per_device(): cols = lax.all_to_all(pair, 'y', 0, 0, tiled=True)  4.18 us
    all_to_all x1, starting transfers between devices, per_device(): lax.all_to_all(again.reshape(SIZES['x'] * SIZES['zl'], -1, 256), OUTER, 0...  3.86 us
  transfers between devices with their start and end apart: 16, of which 7 were waited for; matrix products, arithmetic and copies ran while one was open for 2% of the time, Pallas kernels for 3%

profile of v1, /device:TPU:1, one launch (start us, length us, event | category | flops | bytes accessed | tf_op | source)
XLA Modules:
  0.0 173.8 jit_solution(11251780238517998244)
XLA Ops:
  0.6 0.0 copy-start
  0.7 1.5 copy.18.e1
  2.2 0.7 pad_add_fusion.pos
  2.8 11.8 %local_grads.1 = (bf16[16,128,256]{2,1,0:T(8,128)(2,1)}, bf16[16,128,256]{2,1,0:T(8,128)(2,1)}) custom-call(s32[4]{0:T(128)} %pad_add_fusion.pos, bf16[192,128]{1,0:T(8,128)(2,1)} %hid.1, bf16[192,8192]{1,0:T(8,128)(2,1)} %og_oth.1, bf16[192,8192]{1,0:T(8,128)(2,1)} %og_oth.1, s32[128,64]{1,0:T(8,128)} %copy.18.e1), custom_call_target="tpu_custom_call" | custom-call | flops 402653184 | bytes 5242880 | tf_op jit(solution)/shard_map/local_grads/pallas_call | solution.py:37
  14.7 16.1 %collective-permute-start.10 = (bf16[16,128,256]{2,1,0:T(8,128)(2,1)}, bf16[16,128,256]{2,1,0:T(8,128)(2,1)S(1)}, u32[]{:S(2)}, u32[]{:S(2)}) collective-permute-start(bf16[16,128,256]{2,1,0:T(8,128)(2,1)} %get-tuple-element.5), channel_id=1, source_target_pairs={{0,1},{1,0},{2,3},{3,2},{4,5},{5,4},{6,7},{7,6},{8,9},{9,8},{10,11... | collective-permute-start | bytes 3145736 | tf_op jit(solution)/shard_map/ppermute | solution.py:16
  30.7 0.0 copy-done
  30.8 10.1 %collective-permute-start = (bf16[32,256]{1,0:T(8,128)(2,1)S(1)}, bf16[32,256]{1,0:T(8,128)(2,1)S(1)}, u32[]{:S(2)}, u32[]{:S(2)}) collective-permute-start(bf16[32,256]{1,0:T(8,128)(2,1)S(1)} %constant_dynamic-slice_fusion), channel_id=1, source_target_pairs={{0,6},{2,0},{4,2},{6,4},{1,7},{3,1},{5,3},{7,5},{8,14},{10,8},{12,... | collective-permute-start | bytes 49160 | tf_op jit(solution)/shard_map/ppermute | solution.py:16
  40.8 7.9 %collective-permute-start.1 = (bf16[32,256]{1,0:T(8,128)(2,1)S(1)}, bf16[32,256]{1,0:T(8,128)(2,1)S(1)}, u32[]{:S(2)}, u32[]{:S(2)}) collective-permute-start(bf16[32,256]{1,0:T(8,128)(2,1)S(1)} %constant_dynamic-slice_fusion), channel_id=1, source_target_pairs={{0,4},{2,6},{4,0},{6,2},{1,5},{3,7},{5,1},{7,3},{8,12},{10,14},{12... | collective-permute-start | bytes 49160 | tf_op jit(solution)/shard_map/ppermute | solution.py:16
  48.7 12.1 %collective-permute-start.2 = (bf16[32,256]{1,0:T(8,128)(2,1)S(1)}, bf16[32,256]{1,0:T(8,128)(2,1)S(1)}, u32[]{:S(2)}, u32[]{:S(2)}) collective-permute-start(bf16[32,256]{1,0:T(8,128)(2,1)S(1)} %constant_dynamic-slice_fusion), channel_id=1, source_target_pairs={{0,2},{2,4},{4,6},{6,0},{1,3},{3,5},{5,7},{7,1},{8,10},{10,12},{12... | collective-permute-start | bytes 49160 | tf_op jit(solution)/shard_map/ppermute | solution.py:16
  60.8 0.0 collective-permute-done.10
  60.8 2.5 %add_convert_fusion = bf16[16,128,256]{2,1,0:T(8,128)(2,1)} fusion(bf16[16,128,256]{2,1,0:T(8,128)(2,1)S(1)} %collective-permute-done.10, bf16[16,128,256]{2,1,0:T(8,128)(2,1)} %get-tuple-element.4), kind=kLoop, calls=%fused_computation | loop fusion | flops 2097152 | bytes 3145728 | tf_op jit(solution)/shard_map/convert_element_type | solution.py:109
  63.3 4.2 %all-to-all-start = ((bf16[4,4,128,256]{3,2,1,0:T(8,128)(2,1)}), bf16[4,4,128,256]{3,2,1,0:T(8,128)(2,1)S(1)}, u32[]{:S(2)}, u32[]{:S(2)}) async-start(bf16[4,4,128,256]{3,2,1,0:T(8,128)(2,1)} %bitcast.16), calls=%async_computation | async-start | bytes 2097152 | tf_op jit(solution)/shard_map/all_to_all | solution.py:110
  67.5 0.0 collective-permute-done
  67.5 0.0 collective-permute-done.1
  67.5 0.0 collective-permute-done.2
  67.6 4.9 %collective-permute-start.4 = (bf16[4,32,256]{2,1,0:T(8,128)(2,1)S(1)}, bf16[4,32,256]{2,1,0:T(8,128)(2,1)S(1)}, u32[]{:S(2)}, u32[]{:S(2)}) collective-permute-start(bf16[4,32,256]{2,1,0:T(8,128)(2,1)S(1)} %get-tuple-element.12), channel_id=1, source_target_pairs={{0,16},{8,24},{16,0},{24,8},{1,17},{9,25},{17,1},{25,9},{2,18},{10... | collective-permute-start | bytes 196616 | tf_op jit(solution)/shard_map/ppermute | solution.py:16
  72.5 2.2 %collective-permute-start.5 = (bf16[4,32,256]{2,1,0:T(8,128)(2,1)S(1)}, bf16[4,32,256]{2,1,0:T(8,128)(2,1)S(1)}, u32[]{:S(2)}, u32[]{:S(2)}) collective-permute-start(bf16[4,32,256]{2,1,0:T(8,128)(2,1)S(1)} %get-tuple-element.12), channel_id=1, source_target_pairs={{0,8},{8,16},{16,24},{24,0},{1,9},{9,17},{17,25},{25,1},{2,10},{10... | collective-permute-start | bytes 196616 | tf_op jit(solution)/shard_map/ppermute | solution.py:16
  74.7 4.3 %collective-permute-start.3 = (bf16[4,32,256]{2,1,0:T(8,128)(2,1)S(1)}, bf16[4,32,256]{2,1,0:T(8,128)(2,1)S(1)}, u32[]{:S(2)}, u32[]{:S(2)}) collective-permute-start(bf16[4,32,256]{2,1,0:T(8,128)(2,1)S(1)} %get-tuple-element.12), channel_id=1, source_target_pairs={{0,24},{8,0},{16,8},{24,16},{1,25},{9,1},{17,9},{25,17},{2,26},{10... | collective-permute-start | bytes 196616 | tf_op jit(solution)/shard_map/ppermute | solution.py:16
  79.0 4.0 %collective-permute-done.4 = bf16[4,32,256]{2,1,0:T(8,128)(2,1)S(1)} collective-permute-done((bf16[4,32,256]{2,1,0:T(8,128)(2,1)S(1)}, bf16[4,32,256]{2,1,0:T(8,128)(2,1)S(1)}, u32[]{:S(2)}, u32[]{:S(2)}) %collective-permute-start.4) | collective-permute-done | bytes 65568 | tf_op jit(solution)/shard_map/ppermute | solution.py:16
  83.0 1.2 collective-permute-done.5
  84.2 0.0 collective-permute-done.3
  84.2 0.0 copy-start.3
  84.2 4.4 %collective-permute-start.6 = (bf16[4,4,32,256]{3,2,1,0:T(8,128)(2,1)S(1)}, bf16[4,4,32,256]{3,2,1,0:T(8,128)(2,1)S(1)}, u32[]{:S(2)}, u32[]{:S(2)}) collective-permute-start(bf16[4,4,32,256]{3,2,1,0:T(8,128)(2,1)S(1)} %get-tuple-element.10), channel_id=1, source_target_pairs={{0,768},{256,0},{512,256},{768,512},{1,769},{257,1},{513,257},{769... | collective-permute-start | bytes 786440 | tf_op jit(solution)/shard_map/ppermute | solution.py:16
  88.6 2.4 %collective-permute-start.7 = (bf16[4,4,32,256]{3,2,1,0:T(8,128)(2,1)S(1)}, bf16[4,4,32,256]{3,2,1,0:T(8,128)(2,1)S(1)}, u32[]{:S(2)}, u32[]{:S(2)}) collective-permute-start(bf16[4,4,32,256]{3,2,1,0:T(8,128)(2,1)S(1)} %get-tuple-element.10), channel_id=1, source_target_pairs={{0,512},{256,768},{512,0},{768,256},{1,513},{257,769},{513,1},{769... | collective-permute-start | bytes 786440 | tf_op jit(solution)/shard_map/ppermute | solution.py:16
  91.1 2.5 %collective-permute-start.8 = (bf16[4,4,32,256]{3,2,1,0:T(8,128)(2,1)S(1)}, bf16[4,4,32,256]{3,2,1,0:T(8,128)(2,1)S(1)}, u32[]{:S(2)}, u32[]{:S(2)}) collective-permute-start(bf16[4,4,32,256]{3,2,1,0:T(8,128)(2,1)S(1)} %get-tuple-element.10), channel_id=1, source_target_pairs={{0,256},{256,512},{512,768},{768,0},{1,257},{257,513},{513,769},{7... | collective-permute-start | bytes 786440 | tf_op jit(solution)/shard_map/ppermute | solution.py:16
  93.6 0.0 collective-permute-done.6
  93.6 4.0 %collective-permute-done.7 = bf16[4,4,32,256]{3,2,1,0:T(8,128)(2,1)S(1)} collective-permute-done((bf16[4,4,32,256]{3,2,1,0:T(8,128)(2,1)S(1)}, bf16[4,4,32,256]{3,2,1,0:T(8,128)(2,1)S(1)}, u32[]{:S(2)}, u32[]{:S(2)}) %collective-permute-start.7) | collective-permute-done | bytes 262176 | tf_op jit(solution)/shard_map/ppermute | solution.py:16
  97.6 7.2 %collective-permute-done.8 = bf16[4,4,32,256]{3,2,1,0:T(8,128)(2,1)S(1)} collective-permute-done((bf16[4,4,32,256]{3,2,1,0:T(8,128)(2,1)S(1)}, bf16[4,4,32,256]{3,2,1,0:T(8,128)(2,1)S(1)}, u32[]{:S(2)}, u32[]{:S(2)}) %collective-permute-start.8) | collective-permute-done | bytes 262176 | tf_op jit(solution)/shard_map/ppermute | solution.py:16
  104.8 0.1 pad_maximum_fusion.own
  105.0 0.0 copy-start.1
  105.0 3.5 %collective-permute-start.9 = (bf16[4,4,4,32,256]{4,3,2,1,0:T(8,128)(2,1)S(1)}, bf16[4,4,4,32,256]{4,3,2,1,0:T(8,128)(2,1)S(1)}, u32[]{:S(2)}, u32[]{:S(2)}) collective-permute-start(bf16[4,4,4,32,256]{4,3,2,1,0:T(8,128)(2,1)S(1)} %pad_maximum_fusion.own), channel_id=1, source_target_pairs={{0,1},{1,0},{2,3},{3,2},{4,5},{5,4},{6,7},{7,6},{8,9},{9,8},{10,11... | collective-permute-start | bytes 3145736 | tf_op jit(solution)/shard_map/ppermute | solution.py:16
  108.5 0.0 all-to-all-done
  108.5 0.2 reduce_sum.21
  108.7 7.5 %collective-permute-start.11 = (bf16[128,256]{1,0:T(8,128)(2,1)S(1)}, bf16[128,256]{1,0:T(8,128)(2,1)S(1)}, u32[]{:S(2)}, u32[]{:S(2)}) collective-permute-start(bf16[128,256]{1,0:T(8,128)(2,1)S(1)} %get-tuple-element.6), channel_id=1, source_target_pairs={{0,2},{2,4},{4,6},{6,0},{1,3},{3,5},{5,7},{7,1},{8,10},{10,12},{12... | collective-permute-start | bytes 196616 | tf_op jit(solution)/shard_map/ppermute | solution.py:16
  116.3 7.9 %collective-permute-start.12 = (bf16[128,256]{1,0:T(8,128)(2,1)S(1)}, bf16[128,256]{1,0:T(8,128)(2,1)S(1)}, u32[]{:S(2)}, u32[]{:S(2)}) collective-permute-start(bf16[128,256]{1,0:T(8,128)(2,1)S(1)} %get-tuple-element.8), channel_id=1, source_target_pairs={{0,4},{2,6},{4,0},{6,2},{1,5},{3,7},{5,1},{7,3},{8,12},{10,14},{12... | collective-permute-start | bytes 196616 | tf_op jit(solution)/shard_map/ppermute | solution.py:16
  124.2 5.8 %collective-permute-start.13 = (bf16[128,256]{1,0:T(8,128)(2,1)S(1)}, bf16[128,256]{1,0:T(8,128)(2,1)S(1)}, u32[]{:S(2)}, u32[]{:S(2)}) collective-permute-start(bf16[128,256]{1,0:T(8,128)(2,1)S(1)} %get-tuple-element.7), channel_id=1, source_target_pairs={{0,6},{2,0},{4,2},{6,4},{1,7},{3,1},{5,3},{7,5},{8,14},{10,8},{12,... | collective-permute-start | bytes 196616 | tf_op jit(solution)/shard_map/ppermute | solution.py:16
  130.0 0.0 copy-done.3
  130.0 0.1 copy.17
  130.2 0.0 collective-permute-done.11
  130.2 9.7 %collective-permute-done.12 = bf16[128,256]{1,0:T(8,128)(2,1)S(1)} collective-permute-done((bf16[128,256]{1,0:T(8,128)(2,1)S(1)}, bf16[128,256]{1,0:T(8,128)(2,1)S(1)}, u32[]{:S(2)}, u32[]{:S(2)}) %collective-permute-start.12) | collective-permute-done | bytes 65568 | tf_op jit(solution)/shard_map/ppermute | solution.py:16
  139.9 17.0 %collective-permute-done.13 = bf16[128,256]{1,0:T(8,128)(2,1)S(1)} collective-permute-done((bf16[128,256]{1,0:T(8,128)(2,1)S(1)}, bf16[128,256]{1,0:T(8,128)(2,1)S(1)}, u32[]{:S(2)}, u32[]{:S(2)}) %collective-permute-start.13) | collective-permute-done | bytes 65568 | tf_op jit(solution)/shard_map/ppermute | solution.py:16
  156.9 0.2 broadcast_in_dim.3
  157.1 0.1 fusion.1
  157.1 0.7 reshape.17
  157.8 3.9 %all-to-all-start.1 = ((bf16[32,4,256]{2,1,0:T(4,128)(2,1)}), bf16[32,4,256]{2,1,0:T(4,128)(2,1)S(1)}, u32[]{:S(2)}, u32[]{:S(2)}) async-start(bf16[32,4,256]{2,1,0:T(4,128)(2,1)} %reshape.17), calls=%async_computation.1 | async-start | bytes 131072 | tf_op jit(solution)/shard_map/all_to_all | solution.py:119
  161.6 0.0 collective-permute-done.9.oth
  161.6 0.0 copy-done.1
  161.7 0.0 copy-start.2
  161.7 1.0 copy-done.2
  162.6 5.3 %hidden_grads.1 = bf16[192,128]{1,0:T(8,128)(2,1)} custom-call(s32[4]{0:T(128)} %pad_add_fusion.pos, bf16[192,8192]{1,0:T(8,128)(2,1)} %og_oth.1, bf16[4,4,4,32,256]{4,3,2,1,0:T(8,128)(2,1)} %copy-done.1, bf16[4,4,4,32,256]{4,3,2,1,0:T(8,128)(2,1)} %copy-done.2), custom_call_target="tpu_custom_call" | custom-call | flops 402653184 | bytes 5242880 | tf_op jit(solution)/shard_map/hidden_grads/pallas_call | solution.py:83
  167.9 5.2 %all-to-all-done.1 = bf16[32,4,256]{2,1,0:T(4,128)(2,1)S(1)} async-done(((bf16[32,4,256]{2,1,0:T(4,128)(2,1)}), bf16[32,4,256]{2,1,0:T(4,128)(2,1)S(1)}, u32[]{:S(2)}, u32[]{:S(2)}) %all-to-all-start.1) | async-done | bytes 65568 | tf_op jit(solution)/shard_map/all_to_all | solution.py:119
  173.1 0.6 convert_reduce_fusion
  (6 shorter events, 0.1 us)
Async XLA Ops:
  0.6 30.1 %copy-start = (bf16[128,256]{1,0:T(8,128)(2,1)S(1)}, bf16[128,256]{1,0:T(8,128)(2,1)}, u32[]{:S(2)}) copy-start(bf16[128,256]{1,0:T(8,128)(2,1)} %param.7) | copy-start | bytes 196612
  14.7 46.2 %collective-permute-start.10 = (bf16[16,128,256]{2,1,0:T(8,128)(2,1)}, bf16[16,128,256]{2,1,0:T(8,128)(2,1)S(1)}, u32[]{:S(2)}, u32[]{:S(2)}) collective-permute-start(bf16[16,128,256]{2,1,0:T(8,128)(2,1)} %get-tuple-element.5), channel_id=1, source_target_pairs={{0,1},{1,0},{2,3},{3,2},{4,5},{5,4},{6,7},{7,6},{8,9},{9,8},{10,11... | collective-permute-start | bytes 3145736 | tf_op jit(solution)/shard_map/ppermute | solution.py:16
  30.8 36.8 %collective-permute-start = (bf16[32,256]{1,0:T(8,128)(2,1)S(1)}, bf16[32,256]{1,0:T(8,128)(2,1)S(1)}, u32[]{:S(2)}, u32[]{:S(2)}) collective-permute-start(bf16[32,256]{1,0:T(8,128)(2,1)S(1)} %constant_dynamic-slice_fusion), channel_id=1, source_target_pairs={{0,6},{2,0},{4,2},{6,4},{1,7},{3,1},{5,3},{7,5},{8,14},{10,8},{12,... | collective-permute-start | bytes 49160 | tf_op jit(solution)/shard_map/ppermute | solution.py:16
  40.8 26.7 %collective-permute-start.1 = (bf16[32,256]{1,0:T(8,128)(2,1)S(1)}, bf16[32,256]{1,0:T(8,128)(2,1)S(1)}, u32[]{:S(2)}, u32[]{:S(2)}) collective-permute-start(bf16[32,256]{1,0:T(8,128)(2,1)S(1)} %constant_dynamic-slice_fusion), channel_id=1, source_target_pairs={{0,4},{2,6},{4,0},{6,2},{1,5},{3,7},{5,1},{7,3},{8,12},{10,14},{12... | collective-permute-start | bytes 49160 | tf_op jit(solution)/shard_map/ppermute | solution.py:16
  48.7 18.8 %collective-permute-start.2 = (bf16[32,256]{1,0:T(8,128)(2,1)S(1)}, bf16[32,256]{1,0:T(8,128)(2,1)S(1)}, u32[]{:S(2)}, u32[]{:S(2)}) collective-permute-start(bf16[32,256]{1,0:T(8,128)(2,1)S(1)} %constant_dynamic-slice_fusion), channel_id=1, source_target_pairs={{0,2},{2,4},{4,6},{6,0},{1,3},{3,5},{5,7},{7,1},{8,10},{10,12},{12... | collective-permute-start | bytes 49160 | tf_op jit(solution)/shard_map/ppermute | solution.py:16
  63.3 45.1 %all-to-all-start = ((bf16[4,4,128,256]{3,2,1,0:T(8,128)(2,1)}), bf16[4,4,128,256]{3,2,1,0:T(8,128)(2,1)S(1)}, u32[]{:S(2)}, u32[]{:S(2)}) async-start(bf16[4,4,128,256]{3,2,1,0:T(8,128)(2,1)} %bitcast.16), calls=%async_computation | async-start | bytes 2097152 | tf_op jit(solution)/shard_map/all_to_all | solution.py:110
  67.6 15.4 %collective-permute-start.4 = (bf16[4,32,256]{2,1,0:T(8,128)(2,1)S(1)}, bf16[4,32,256]{2,1,0:T(8,128)(2,1)S(1)}, u32[]{:S(2)}, u32[]{:S(2)}) collective-permute-start(bf16[4,32,256]{2,1,0:T(8,128)(2,1)S(1)} %get-tuple-element.12), channel_id=1, source_target_pairs={{0,16},{8,24},{16,0},{24,8},{1,17},{9,25},{17,1},{25,9},{2,18},{10... | collective-permute-start | bytes 196616 | tf_op jit(solution)/shard_map/ppermute | solution.py:16
  72.5 11.7 %collective-permute-start.5 = (bf16[4,32,256]{2,1,0:T(8,128)(2,1)S(1)}, bf16[4,32,256]{2,1,0:T(8,128)(2,1)S(1)}, u32[]{:S(2)}, u32[]{:S(2)}) collective-permute-start(bf16[4,32,256]{2,1,0:T(8,128)(2,1)S(1)} %get-tuple-element.12), channel_id=1, source_target_pairs={{0,8},{8,16},{16,24},{24,0},{1,9},{9,17},{17,25},{25,1},{2,10},{10... | collective-permute-start | bytes 196616 | tf_op jit(solution)/shard_map/ppermute | solution.py:16
  74.7 9.5 %collective-permute-start.3 = (bf16[4,32,256]{2,1,0:T(8,128)(2,1)S(1)}, bf16[4,32,256]{2,1,0:T(8,128)(2,1)S(1)}, u32[]{:S(2)}, u32[]{:S(2)}) collective-permute-start(bf16[4,32,256]{2,1,0:T(8,128)(2,1)S(1)} %get-tuple-element.12), channel_id=1, source_target_pairs={{0,24},{8,0},{16,8},{24,16},{1,25},{9,1},{17,9},{25,17},{2,26},{10... | collective-permute-start | bytes 196616 | tf_op jit(solution)/shard_map/ppermute | solution.py:16
  84.2 45.8 %copy-start.3 = (s32[128,2]{0,1:T(2,128)S(1)}, s32[128,2]{0,1:T(2,128)}, u32[]{:S(2)}) copy-start(s32[128,2]{0,1:T(2,128)} %param.9) | copy-start | bytes 3076
  84.2 9.4 %collective-permute-start.6 = (bf16[4,4,32,256]{3,2,1,0:T(8,128)(2,1)S(1)}, bf16[4,4,32,256]{3,2,1,0:T(8,128)(2,1)S(1)}, u32[]{:S(2)}, u32[]{:S(2)}) collective-permute-start(bf16[4,4,32,256]{3,2,1,0:T(8,128)(2,1)S(1)} %get-tuple-element.10), channel_id=1, source_target_pairs={{0,768},{256,0},{512,256},{768,512},{1,769},{257,1},{513,257},{769... | collective-permute-start | bytes 786440 | tf_op jit(solution)/shard_map/ppermute | solution.py:16
  88.6 9.0 %collective-permute-start.7 = (bf16[4,4,32,256]{3,2,1,0:T(8,128)(2,1)S(1)}, bf16[4,4,32,256]{3,2,1,0:T(8,128)(2,1)S(1)}, u32[]{:S(2)}, u32[]{:S(2)}) collective-permute-start(bf16[4,4,32,256]{3,2,1,0:T(8,128)(2,1)S(1)} %get-tuple-element.10), channel_id=1, source_target_pairs={{0,512},{256,768},{512,0},{768,256},{1,513},{257,769},{513,1},{769... | collective-permute-start | bytes 786440 | tf_op jit(solution)/shard_map/ppermute | solution.py:16
  91.1 13.8 %collective-permute-start.8 = (bf16[4,4,32,256]{3,2,1,0:T(8,128)(2,1)S(1)}, bf16[4,4,32,256]{3,2,1,0:T(8,128)(2,1)S(1)}, u32[]{:S(2)}, u32[]{:S(2)}) collective-permute-start(bf16[4,4,32,256]{3,2,1,0:T(8,128)(2,1)S(1)} %get-tuple-element.10), channel_id=1, source_target_pairs={{0,256},{256,512},{512,768},{768,0},{1,257},{257,513},{513,769},{7... | collective-permute-start | bytes 786440 | tf_op jit(solution)/shard_map/ppermute | solution.py:16
  105.0 56.7 %copy-start.1 = (bf16[4,4,4,32,256]{4,3,2,1,0:T(8,128)(2,1)}, bf16[4,4,4,32,256]{4,3,2,1,0:T(8,128)(2,1)S(1)}, u32[]{:S(2)}) copy-start(bf16[4,4,4,32,256]{4,3,2,1,0:T(8,128)(2,1)S(1)} %pad_maximum_fusion.own) | copy-start | bytes 3145732
  105.0 56.7 %collective-permute-start.9 = (bf16[4,4,4,32,256]{4,3,2,1,0:T(8,128)(2,1)S(1)}, bf16[4,4,4,32,256]{4,3,2,1,0:T(8,128)(2,1)S(1)}, u32[]{:S(2)}, u32[]{:S(2)}) collective-permute-start(bf16[4,4,4,32,256]{4,3,2,1,0:T(8,128)(2,1)S(1)} %pad_maximum_fusion.own), channel_id=1, source_target_pairs={{0,1},{1,0},{2,3},{3,2},{4,5},{5,4},{6,7},{7,6},{8,9},{9,8},{10,11... | collective-permute-start | bytes 3145736 | tf_op jit(solution)/shard_map/ppermute | solution.py:16
  108.7 21.4 %collective-permute-start.11 = (bf16[128,256]{1,0:T(8,128)(2,1)S(1)}, bf16[128,256]{1,0:T(8,128)(2,1)S(1)}, u32[]{:S(2)}, u32[]{:S(2)}) collective-permute-start(bf16[128,256]{1,0:T(8,128)(2,1)S(1)} %get-tuple-element.6), channel_id=1, source_target_pairs={{0,2},{2,4},{4,6},{6,0},{1,3},{3,5},{5,7},{7,1},{8,10},{10,12},{12... | collective-permute-start | bytes 196616 | tf_op jit(solution)/shard_map/ppermute | solution.py:16
  116.3 23.6 %collective-permute-start.12 = (bf16[128,256]{1,0:T(8,128)(2,1)S(1)}, bf16[128,256]{1,0:T(8,128)(2,1)S(1)}, u32[]{:S(2)}, u32[]{:S(2)}) collective-permute-start(bf16[128,256]{1,0:T(8,128)(2,1)S(1)} %get-tuple-element.8), channel_id=1, source_target_pairs={{0,4},{2,6},{4,0},{6,2},{1,5},{3,7},{5,1},{7,3},{8,12},{10,14},{12... | collective-permute-start | bytes 196616 | tf_op jit(solution)/shard_map/ppermute | solution.py:16
  124.2 32.7 %collective-permute-start.13 = (bf16[128,256]{1,0:T(8,128)(2,1)S(1)}, bf16[128,256]{1,0:T(8,128)(2,1)S(1)}, u32[]{:S(2)}, u32[]{:S(2)}) collective-permute-start(bf16[128,256]{1,0:T(8,128)(2,1)S(1)} %get-tuple-element.7), channel_id=1, source_target_pairs={{0,6},{2,0},{4,2},{6,4},{1,7},{3,1},{5,3},{7,5},{8,14},{10,8},{12,... | collective-permute-start | bytes 196616 | tf_op jit(solution)/shard_map/ppermute | solution.py:16
  157.8 15.4 %all-to-all-start.1 = ((bf16[32,4,256]{2,1,0:T(4,128)(2,1)}), bf16[32,4,256]{2,1,0:T(4,128)(2,1)S(1)}, u32[]{:S(2)}, u32[]{:S(2)}) async-start(bf16[32,4,256]{2,1,0:T(4,128)(2,1)} %reshape.17), calls=%async_computation.1 | async-start | bytes 131072 | tf_op jit(solution)/shard_map/all_to_all | solution.py:119
  161.7 1.0 copy-start.2

commit v2 on v0

v2 whole, which is shorter than its diff:
```python
import jax
import jax.numpy as jnp
from jax import lax
from jax.experimental import pallas as pl
from jax.experimental.pallas import tpu as pltpu
from jax.sharding import Mesh, PartitionSpec as P

SIZES = {"x": 4, "zl": 8, "y": 4, "zh": 4, "c": 2}
AXES = tuple(SIZES)
OUTER = ("x", "zl")
N_OUTER = 32
LIMIT = 448.0
F32, BF16 = jnp.float32, jnp.bfloat16


def limits(exponent):
    return jnp.left_shift(1, exponent + 16).astype(F32) * (LIMIT * 2.0**-16)


def grad_kernel(hid, og, exponent, out):
    bound = limits(exponent[...]).astype(BF16)
    acts = hid[...].T
    rows = lax.broadcasted_iota(jnp.int32, (16, 256), 0)
    lanes = lax.broadcasted_iota(jnp.int32, (16, 256), 1) // 128
    for block in range(8):
        pick = (rows == 2 * block + lanes).astype(BF16)
        limit = lax.dot_general(bound, pick, (((0,), (0,)), ((), ())), preferred_element_type=F32)
        local = jnp.dot(acts, og[:, 256 * block : 256 * (block + 1)], preferred_element_type=F32)
        out[block % 2, block // 2] = jnp.clip(local, -limit, limit).astype(BF16)


def local_grads(hidden, out_grad, exponent):
    return pl.pallas_call(
        grad_kernel,
        grid=(4,),
        in_specs=[
            pl.BlockSpec((192, 128), lambda y: (0, 0)),
            pl.BlockSpec((192, 2048), lambda y: (0, y)),
            pl.BlockSpec((16, 128), lambda y: (y, 0)),
        ],
        out_specs=pl.BlockSpec((2, 4, 128, 256), lambda y: (0, y, 0, 0)),
        out_shape=jax.ShapeDtypeStruct((2, 16, 128, 256), BF16),
        cost_estimate=pl.CostEstimate(flops=2 * 192 * 128 * 8192, bytes_accessed=5 << 20, transcendentals=0),
        name="local_grads",
    )(hidden, out_grad, exponent)


def hidden_kernel(core, og, own, oth, out, total):
    step, c = pl.program_id(0), core[0]

    @pl.when(step == 0)
    def _():
        total[...] = jnp.zeros_like(total)

    acc = total[...]
    for zh in range(4):
        for side, part in ((c, own), (1 - c, oth)):
            cols = og[:, pl.ds(pl.multiple_of(512 * zh + 256 * side, 256), 256)]
            rows = part[:, 0, zh].reshape(128, 256)
            acc += lax.dot_general(cols, rows, (((1,), (1,)), ((), ())), preferred_element_type=F32)
    total[...] = acc

    @pl.when(step == 3)
    def _():
        out[...] = acc.astype(BF16)


def hidden_grads(core, out_grad, own, oth):
    part = pl.BlockSpec((4, 1, 4, 32, 256), lambda y, core: (0, y, 0, 0, 0))
    return pl.pallas_call(
        hidden_kernel,
        grid_spec=pltpu.PrefetchScalarGridSpec(
            num_scalar_prefetch=1,
            grid=(4,),
            in_specs=[pl.BlockSpec((192, 2048), lambda y, core: (0, y)), part, part],
            out_specs=pl.BlockSpec((192, 128), lambda y, core: (0, 0)),
            scratch_shapes=[pltpu.VMEM((192, 128), F32)],
        ),
        out_shape=jax.ShapeDtypeStruct((192, 128), BF16),
        cost_estimate=pl.CostEstimate(flops=2 * 192 * 128 * 8192, bytes_accessed=5 << 20, transcendentals=0),
        name="hidden_grads",
    )(core, out_grad, own, oth)


def swap(value, axes):
    return lax.all_to_all(value, axes, 0, 0, tiled=True)


def after(value, *earlier):
    return lax.optimization_barrier((value, *earlier))[0]


def summed(parts):
    return parts.astype(F32).sum(0)


def per_device(out_grad, hidden, weight, e1, e2):
    x, c = lax.axis_index("x"), lax.axis_index("c")
    blocks = local_grads(hidden, out_grad, e1.T)
    pairs = summed(swap(blocks, "c")).astype(BF16)

    mine = after(lax.dynamic_slice_in_dim(weight, x * 32, 32, 0), blocks)
    quarter = swap(jnp.broadcast_to(mine, (4, 32, 256)), "zh")

    columns = swap(pairs.reshape(4, 4, 128, 256), "y")
    line = summed(columns).astype(BF16)
    group = summed(swap(line, "zh"))
    limit = jnp.repeat(limits(e2), 128, axis=1)
    again = jnp.clip(group, -limit, limit).astype(BF16)
    rows = swap(again.reshape(N_OUTER, -1, 256), OUTER)
    weight_grad = summed(rows)

    quarter = after(quarter, line)
    own = swap(jnp.broadcast_to(quarter, (16, 4, 32, 256)), ("x", "y")).reshape(4, 4, 4, 32, 256)
    oth = lax.ppermute(own, "c", [(0, 1), (1, 0)])
    hidden_grad = hidden_grads(c[None], out_grad, own, oth)
    return hidden_grad, weight_grad


def solution(mesh):
    fine = Mesh(mesh.devices.reshape(tuple(SIZES.values())), AXES)
    every, inner = P(AXES, None), ("y", "zh", "c")
    return jax.shard_map(
        per_device,
        mesh=fine,
        in_specs=(every, every, P(None, inner), every, P(OUTER, inner)),
        out_specs=(every, P(OUTER, inner)),
        check_vma=False,
    )
```

time: 832 us -> 166 us (0.20)
  the two profiles are of different devices: /device:TPU:1 before, /device:TPU:2 now
where the time goes in v2:
time: 166 us; the launch traced here: 165 us
  waiting for transfers between devices  75.1 us (45%)
  starting transfers between devices  49.5 us (30%)
  blocking collectives  24.3 us (15%)
  Pallas kernels  9.33 us (6%)
  other arithmetic  3.9 us (2%)
  local copies, waits for them, and re-layouts  2.22 us (1%)
    all_to_all x4, waiting for transfers between devices, swap(): return lax.all_to_all(value, axes, 0, 0, tiled=True)  75.1 us
    all_to_all x4, starting transfers between devices, swap(): return lax.all_to_all(value, axes, 0, 0, tiled=True)  47.6 us
    all_to_all x2, blocking collectives, swap(): return lax.all_to_all(value, axes, 0, 0, tiled=True)  24.3 us
    pallas_call x1, Pallas kernels, local_grads(): pl.pallas_call(grad_kernel, grid=(4,), in_specs=[pl.BlockSpec((192, 128),...  4.91 us
    pallas_call x1, Pallas kernels, hidden_grads(): pl.pallas_call(hidden_kernel, grid_spec=pltpu.PrefetchScalarGridSpec(num_...  4.42 us
  transfers between devices with their start and end apart: 5, of which 4 were waited for; matrix products, arithmetic and copies ran while one was open for 1% of the time, Pallas kernels for 3%

profile of v2, /device:TPU:2, one launch (start us, length us, event | category | flops | bytes accessed | tf_op | source)
XLA Modules:
  0.0 165.2 jit_solution(11405190011175146046)
XLA Ops:
  0.6 0.0 copy-start
  0.6 4.9 %local_grads.1 = bf16[2,16,128,256]{3,2,1,0:T(8,128)(2,1)} custom-call(bf16[192,128]{1,0:T(8,128)(2,1)} %hid.1, bf16[192,8192]{1,0:T(8,128)(2,1)} %og.3, s32[64,128]{1,0:T(8,128)} %bitcast.6), custom_call_target="tpu_custom_call" | custom-call | flops 402653184 | bytes 5242880 | tf_op jit(solution)/shard_map/local_grads/pallas_call | solution.py:33
  5.6 6.6 %all_to_all.30 = bf16[2,16,128,256]{3,2,1,0:T(8,128)(2,1)S(1)} all-to-all(bf16[2,16,128,256]{3,2,1,0:T(8,128)(2,1)} %local_grads.1), channel_id=1, replica_groups=mesh['x'=4,'zl'=8,'y'=4,'zh'=4,'c'=2] {'c'}, dimensions={0} | all-to-all | bytes 4194304 | tf_op jit(solution)/shard_map/all_to_all | solution.py:86
  12.2 1.6 reduce_sum.44
  13.8 4.5 %all-to-all-start.2 = ((bf16[4,4,128,256]{3,2,1,0:T(8,128)(2,1)}), bf16[4,4,128,256]{3,2,1,0:T(8,128)(2,1)S(1)}, u32[]{:S(2)}, u32[]{:S(2)}) async-start(bf16[4,4,128,256]{3,2,1,0:T(8,128)(2,1)} %bitcast.2), calls=%async_computation.2 | async-start | bytes 2097152 | tf_op jit(solution)/shard_map/all_to_all | solution.py:86
  18.3 0.0 copy-done
  18.3 15.4 %all-to-all-done.2 = bf16[4,4,128,256]{3,2,1,0:T(8,128)(2,1)S(1)} async-done(((bf16[4,4,128,256]{3,2,1,0:T(8,128)(2,1)}), bf16[4,4,128,256]{3,2,1,0:T(8,128)(2,1)S(1)}, u32[]{:S(2)}, u32[]{:S(2)}) %all-to-all-start.2) | async-done | bytes 1048608 | tf_op jit(solution)/shard_map/all_to_all | solution.py:86
  33.7 0.6 broadcast_in_dim.13
  34.3 28.3 %all-to-all-start = ((bf16[4,32,256]{2,1,0:T(8,128)(2,1)}), bf16[4,32,256]{2,1,0:T(8,128)(2,1)S(1)}, u32[]{:S(2)}, u32[]{:S(2)}) async-start(bf16[4,32,256]{2,1,0:T(8,128)(2,1)} %broadcast_in_dim.13), calls=%async_computation | async-start | bytes 131072 | tf_op jit(solution)/shard_map/all_to_all | solution.py:86
  62.6 0.9 reduce_sum.45
  63.6 0.0 copy-start.3
  63.6 21.7 %all-to-all-done = bf16[4,32,256]{2,1,0:T(8,128)(2,1)S(1)} async-done(((bf16[4,32,256]{2,1,0:T(8,128)(2,1)}), bf16[4,32,256]{2,1,0:T(8,128)(2,1)S(1)}, u32[]{:S(2)}, u32[]{:S(2)}) %all-to-all-start) | async-done | bytes 65568 | tf_op jit(solution)/shard_map/all_to_all | solution.py:86
  85.3 0.1 broadcast_in_dim.14
  85.4 17.7 %all_to_all.31 = bf16[16,4,32,256]{3,2,1,0:T(8,128)(2,1)S(1)} all-to-all(bf16[16,4,32,256]{3,2,1,0:T(8,128)(2,1)S(1)} %broadcast_in_dim.14), channel_id=1, replica_groups=mesh['x'=4,'zl'=8,'y'=4,'zh'=4,'c'=2] {'x','y'}, dimensions={0} | all-to-all | bytes 2097152 | tf_op jit(solution)/shard_map/all_to_all | solution.py:86
  103.1 0.0 copy-start.1
  103.1 3.4 %all-to-all-start.4 = ((bf16[4,128,256]{2,1,0:T(8,128)(2,1)}), bf16[4,128,256]{2,1,0:T(8,128)(2,1)S(1)}, u32[]{:S(2)}, u32[]{:S(2)}) async-start(bf16[4,128,256]{2,1,0:T(8,128)(2,1)} %reduce_sum.45), calls=%async_computation.4 | async-start | bytes 524288 | tf_op jit(solution)/shard_map/all_to_all | solution.py:86
  106.5 1.9 %collective-permute-start = (bf16[4,4,4,32,256]{4,3,2,1,0:T(8,128)(2,1)S(1)}, bf16[4,4,4,32,256]{4,3,2,1,0:T(8,128)(2,1)S(1)}, u32[]{:S(2)}, u32[]{:S(2)}) collective-permute-start(bf16[4,4,4,32,256]{4,3,2,1,0:T(8,128)(2,1)S(1)} %bitcast.4), channel_id=1, source_target_pairs={{0,1},{1,0},{2,3},{3,2},{4,5},{5,4},{6,7},{7,6},{8,9},{9,8},{10,11... | collective-permute-start | bytes 3145736 | tf_op jit(solution)/shard_map/ppermute | solution.py:115
  108.4 0.0 copy-done.3
  108.5 0.1 copy.19
  108.6 0.2 broadcast_in_dim.15
  108.8 0.1 reshape.18
  108.9 32.0 %all-to-all-done.4 = bf16[4,128,256]{2,1,0:T(8,128)(2,1)S(1)} async-done(((bf16[4,128,256]{2,1,0:T(8,128)(2,1)}), bf16[4,128,256]{2,1,0:T(8,128)(2,1)S(1)}, u32[]{:S(2)}, u32[]{:S(2)}) %all-to-all-start.4) | async-done | bytes 262176 | tf_op jit(solution)/shard_map/all_to_all | solution.py:86
  141.0 0.7 minimum_convert_fusion
  141.7 11.4 %all-to-all-start.5 = ((bf16[32,4,256]{2,1,0:T(4,128)(2,1)}), bf16[32,4,256]{2,1,0:T(4,128)(2,1)S(1)}, u32[]{:S(2)}, u32[]{:S(2)}) async-start(bf16[32,4,256]{2,1,0:T(4,128)(2,1)} %minimum_convert_fusion), calls=%async_computation.5 | async-start | bytes 131072 | tf_op jit(solution)/shard_map/all_to_all | solution.py:86
  153.1 0.0 collective-permute-done.oth
  153.1 0.0 copy-start.2
  153.1 0.0 copy-done.1
  153.1 1.0 copy-done.2
  154.1 4.4 %hidden_grads.1 = bf16[192,128]{1,0:T(8,128)(2,1)} custom-call(s32[1]{0:T(128)} %bitcast.core, bf16[192,8192]{1,0:T(8,128)(2,1)} %og.3, bf16[4,4,4,32,256]{4,3,2,1,0:T(8,128)(2,1)} %bitcast.5, bf16[4,4,4,32,256]{4,3,2,1,0:T(8,128)(2,1)} %copy-done.2), custom_call_target="tpu_custom_call" | custom-call | flops 402653184 | bytes 5242880 | tf_op jit(solution)/shard_map/hidden_grads/pallas_call | solution.py:70
  158.6 6.0 %all-to-all-done.5 = bf16[32,4,256]{2,1,0:T(4,128)(2,1)S(1)} async-done(((bf16[32,4,256]{2,1,0:T(4,128)(2,1)}), bf16[32,4,256]{2,1,0:T(4,128)(2,1)S(1)}, u32[]{:S(2)}, u32[]{:S(2)}) %all-to-all-start.5) | async-done | bytes 65568 | tf_op jit(solution)/shard_map/all_to_all | solution.py:86
  164.6 0.6 convert_reduce_fusion.1
  (4 shorter events, 0.1 us)
Async XLA Ops:
  0.6 17.7 %copy-start = (bf16[128,256]{1,0:T(8,128)(2,1)S(1)}, bf16[128,256]{1,0:T(8,128)(2,1)}, u32[]{:S(2)}) copy-start(bf16[128,256]{1,0:T(8,128)(2,1)} %param.7) | copy-start | bytes 196612
  13.8 19.9 %all-to-all-start.2 = ((bf16[4,4,128,256]{3,2,1,0:T(8,128)(2,1)}), bf16[4,4,128,256]{3,2,1,0:T(8,128)(2,1)S(1)}, u32[]{:S(2)}, u32[]{:S(2)}) async-start(bf16[4,4,128,256]{3,2,1,0:T(8,128)(2,1)} %bitcast.2), calls=%async_computation.2 | async-start | bytes 2097152 | tf_op jit(solution)/shard_map/all_to_all | solution.py:86
  34.3 51.0 %all-to-all-start = ((bf16[4,32,256]{2,1,0:T(8,128)(2,1)}), bf16[4,32,256]{2,1,0:T(8,128)(2,1)S(1)}, u32[]{:S(2)}, u32[]{:S(2)}) async-start(bf16[4,32,256]{2,1,0:T(8,128)(2,1)} %broadcast_in_dim.13), calls=%async_computation | async-start | bytes 131072 | tf_op jit(solution)/shard_map/all_to_all | solution.py:86
  63.6 44.9 %copy-start.3 = (s32[128,2]{0,1:T(2,128)S(1)}, s32[128,2]{0,1:T(2,128)}, u32[]{:S(2)}) copy-start(s32[128,2]{0,1:T(2,128)} %param.9) | copy-start | bytes 3076
  103.1 50.0 %copy-start.1 = (bf16[16,4,32,256]{3,2,1,0:T(8,128)(2,1)}, bf16[16,4,32,256]{3,2,1,0:T(8,128)(2,1)S(1)}, u32[]{:S(2)}) copy-start(bf16[16,4,32,256]{3,2,1,0:T(8,128)(2,1)S(1)} %all_to_all.31) | copy-start | bytes 3145732
  103.1 37.8 %all-to-all-start.4 = ((bf16[4,128,256]{2,1,0:T(8,128)(2,1)}), bf16[4,128,256]{2,1,0:T(8,128)(2,1)S(1)}, u32[]{:S(2)}, u32[]{:S(2)}) async-start(bf16[4,128,256]{2,1,0:T(8,128)(2,1)} %reduce_sum.45), calls=%async_computation.4 | async-start | bytes 524288 | tf_op jit(solution)/shard_map/all_to_all | solution.py:86
  106.5 46.6 %collective-permute-start = (bf16[4,4,4,32,256]{4,3,2,1,0:T(8,128)(2,1)S(1)}, bf16[4,4,4,32,256]{4,3,2,1,0:T(8,128)(2,1)S(1)}, u32[]{:S(2)}, u32[]{:S(2)}) collective-permute-start(bf16[4,4,4,32,256]{4,3,2,1,0:T(8,128)(2,1)S(1)} %bitcast.4), channel_id=1, source_target_pairs={{0,1},{1,0},{2,3},{3,2},{4,5},{5,4},{6,7},{7,6},{8,9},{9,8},{10,11... | collective-permute-start | bytes 3145736 | tf_op jit(solution)/shard_map/ppermute | solution.py:115
  141.7 22.9 %all-to-all-start.5 = ((bf16[32,4,256]{2,1,0:T(4,128)(2,1)}), bf16[32,4,256]{2,1,0:T(4,128)(2,1)S(1)}, u32[]{:S(2)}, u32[]{:S(2)}) async-start(bf16[32,4,256]{2,1,0:T(4,128)(2,1)} %minimum_convert_fusion), calls=%async_computation.5 | async-start | bytes 131072 | tf_op jit(solution)/shard_map/all_to_all | solution.py:86
  153.1 1.0 copy-start.2

commit v3 on v2

v3 whole, which is shorter than its diff:
```python
import jax
import jax.numpy as jnp
from jax import lax
from jax.experimental import pallas as pl
from jax.experimental.pallas import tpu as pltpu
from jax.sharding import Mesh, PartitionSpec as P

SIZES = {"x": 4, "zl": 8, "y": 4, "zh": 4, "c": 2}
AXES = tuple(SIZES)
OUTER = ("x", "zl")
N_OUTER = 32
LIMIT = 448.0
F32, BF16 = jnp.float32, jnp.bfloat16


def limits(exponent):
    return jnp.left_shift(1, exponent + 16).astype(F32) * (LIMIT * 2.0**-16)


def grad_kernel(core, hid, og0, og1, og2, og3, exponent, out):
    bound = limits(exponent[...]).astype(BF16)
    acts = hid[...].T
    rows = lax.broadcasted_iota(jnp.int32, (16, 256), 0)
    lanes = lax.broadcasted_iota(jnp.int32, (16, 256), 1) // 128 + 2 * core[0]
    for zh, og in enumerate((og0, og1, og2, og3)):
        pick = (rows == 4 * zh + lanes).astype(BF16)
        limit = lax.dot_general(bound, pick, (((0,), (0,)), ((), ())), preferred_element_type=F32)
        local = jnp.dot(acts, og[...], preferred_element_type=F32)
        out[zh] = jnp.clip(local, -limit, limit).astype(BF16)


def local_grads(core, hidden, out_grad, exponent):
    columns = [pl.BlockSpec((192, 256), lambda y, core, k=2 * zh: (0, 8 * y + k + core[0])) for zh in range(4)]
    return pl.pallas_call(
        grad_kernel,
        grid_spec=pltpu.PrefetchScalarGridSpec(
            num_scalar_prefetch=1,
            grid=(4,),
            in_specs=[
                pl.BlockSpec((192, 128), lambda y, core: (0, 0)),
                *columns,
                pl.BlockSpec((16, 128), lambda y, core: (y, 0)),
            ],
            out_specs=pl.BlockSpec((4, 128, 256), lambda y, core: (y, 0, 0)),
        ),
        out_shape=jax.ShapeDtypeStruct((16, 128, 256), BF16),
        cost_estimate=pl.CostEstimate(flops=192 * 128 * 8192, bytes_accessed=5 << 19, transcendentals=0),
        name="local_grads",
    )(core, hidden, out_grad, out_grad, out_grad, out_grad, exponent)


def hidden_kernel(pos, og, own, oth, out, wide, total):
    c, x, zh = pos[0], pos[1], pos[3]
    step = pl.program_id(0)

    @pl.when(step == 0)
    def _():
        total[...] = jnp.zeros_like(total)

    acc = total[...]
    for kz in range(4):
        at = lax.rem(zh + kz, 4) * 512
        for side, (core, part) in enumerate(((c, own), (1 - c, oth))):
            slot = 2 * kz + side
            for kx in range(4):
                row = pl.multiple_of(lax.rem(x + kx, 4) * 32, 32)
                wide[slot, pl.ds(row, 32), :] = part[kx, 0, kz]
            cols = og[:, pl.ds(pl.multiple_of(at + core * 256, 256), 256)]
            acc += lax.dot_general(cols, wide[slot], (((1,), (1,)), ((), ())), preferred_element_type=F32)
    total[...] = acc

    @pl.when(step == 3)
    def _():
        out[...] = acc.astype(BF16)


def hidden_grads(pos, out_grad, own, oth):
    part = pl.BlockSpec((4, 1, 4, 32, 256), lambda k, pos: (0, k, 0, 0, 0))
    return pl.pallas_call(
        hidden_kernel,
        grid_spec=pltpu.PrefetchScalarGridSpec(
            num_scalar_prefetch=1,
            grid=(4,),
            in_specs=[pl.BlockSpec((192, 2048), lambda k, pos: (0, lax.rem(pos[2] + k, 4))), part, part],
            out_specs=pl.BlockSpec((192, 128), lambda k, pos: (0, 0)),
            scratch_shapes=[pltpu.VMEM((8, 128, 256), BF16), pltpu.VMEM((192, 128), F32)],
        ),
        out_shape=jax.ShapeDtypeStruct((192, 128), BF16),
        cost_estimate=pl.CostEstimate(flops=2 * 192 * 128 * 8192, bytes_accessed=5 << 20, transcendentals=0),
        name="hidden_grads",
    )(pos, out_grad, own, oth)


def shifted(value, axis, k):
    n = SIZES[axis]
    return lax.ppermute(value, axis, [(i, (i - k) % n) for i in range(n)])


def gather(value, axis):
    return jnp.stack([value] + [shifted(value, axis, k) for k in (1, 2, 3)])


def swap(value, axes):
    return lax.all_to_all(value, axes, 0, 0, tiled=True)


def after(value, *earlier):
    return lax.optimization_barrier((value, *earlier))[0]


def summed(parts):
    return parts.astype(F32).sum(0)


def per_device(out_grad, hidden, weight, e1, e2):
    x, y, zh, c = (lax.axis_index(a) for a in ("x", "y", "zh", "c"))
    oth = local_grads(1 - c[None], hidden, out_grad, e1.T)
    got = shifted(oth, "c", 1)
    own = local_grads(after(c, oth)[None], hidden, out_grad, e1.T)
    pairs = (own.astype(F32) + got.astype(F32)).astype(BF16)
    columns = swap(pairs.reshape(4, 4, 128, 256), "y")

    part = after(lax.dynamic_slice_in_dim(weight, x * 32, 32, 0), pairs)
    part = gather(part, "zh")

    line = summed(columns).astype(BF16)
    group = summed(swap(line, "zh"))
    limit = jnp.repeat(limits(e2), 128, axis=1)
    again = jnp.clip(group, -limit, limit).astype(BF16)
    rows = swap(again.reshape(N_OUTER, -1, 256), OUTER)
    weight_grad = summed(rows)

    part = gather(after(part, line), "y")
    part = gather(part, "x")
    pos = jnp.stack([c, x, y, zh])
    hidden_grad = hidden_grads(pos, out_grad, part, shifted(part, "c", 1))
    return hidden_grad, weight_grad


def solution(mesh):
    fine = Mesh(mesh.devices.reshape(tuple(SIZES.values())), AXES)
    every, inner = P(AXES, None), ("y", "zh", "c")
    return jax.shard_map(
        per_device,
        mesh=fine,
        in_specs=(every, every, P(None, inner), every, P(OUTER, inner)),
        out_specs=(every, P(OUTER, inner)),
        check_vma=False,
    )
```

time: 166 us -> 164 us (0.988)
  the two profiles are of different devices: /device:TPU:2 before, /device:TPU:1 now
where the time goes in v3:
time: 164 us; the launch traced here: 163 us
  starting transfers between devices  110 us (67%)
  blocking collectives  17.4 us (11%)
  waiting for transfers between devices  15.1 us (9%)
  Pallas kernels  13.9 us (8%)
  other arithmetic  4.55 us (3%)
    ppermute x11, starting transfers between devices, shifted(): return lax.ppermute(value, axis, [(i, (i - k) % n) for i in range(n)])  81.6 us
    all_to_all x2, starting transfers between devices, swap(): return lax.all_to_all(value, axes, 0, 0, tiled=True)  28.2 us
    all_to_all x1, blocking collectives, swap(): return lax.all_to_all(value, axes, 0, 0, tiled=True)  17.4 us
    ppermute x11, waiting for transfers between devices, shifted(): return lax.ppermute(value, axis, [(i, (i - k) % n) for i in range(n)])  10.4 us
    pallas_call x2, Pallas kernels, local_grads(): pl.pallas_call(grad_kernel, grid_spec=pltpu.PrefetchScalarGridSpec(num_sc...  8.61 us
    pallas_call x1, Pallas kernels, hidden_grads(): pl.pallas_call(hidden_kernel, grid_spec=pltpu.PrefetchScalarGridSpec(num_...  5.26 us
    all_to_all x2, waiting for transfers between devices, swap(): return lax.all_to_all(value, axes, 0, 0, tiled=True)  4.72 us
  transfers between devices with their start and end apart: 13, of which 6 were waited for; matrix products, arithmetic and copies ran while one was open for 1% of the time, Pallas kernels for 6%

profile of v3, /device:TPU:1, one launch (start us, length us, event | category | flops | bytes accessed | tf_op | source)
XLA Modules:
  0.0 163.1 jit_solution(12446943414339010369)
XLA Ops:
  0.6 0.0 copy-start
  0.7 4.3 %local_grads.2 = bf16[16,128,256]{2,1,0:T(8,128)(2,1)} custom-call(s32[1]{0:T(128)S(6)} %sub.3.core, bf16[192,128]{1,0:T(8,128)(2,1)} %hid.3, bf16[192,8192]{1,0:T(8,128)(2,1)} %og.1, bf16[192,8192]{1,0:T(8,128)(2,1)} %og.1, bf16[192,8192]{1,0:T(8,128)(2,1)} %og.1, bf16[192,8192]{1,0:T(8,128)(2,1)} %og.1, s32[64,128]{1,0:T(8,128)} %bitcast.25), custom_call_target="tpu_custom_call" | custom-call | flops 201326592 | bytes 2621440 | tf_op jit(solution)/shard_map/local_grads/pallas_call | solution.py:34
  4.9 16.0 %collective-permute-start = (bf16[16,128,256]{2,1,0:T(8,128)(2,1)}, bf16[16,128,256]{2,1,0:T(8,128)(2,1)S(1)}, u32[]{:S(2)}, u32[]{:S(2)}) collective-permute-start(bf16[16,128,256]{2,1,0:T(8,128)(2,1)} %local_grads.2), channel_id=1, source_target_pairs={{0,1},{1,0},{2,3},{3,2},{4,5},{5,4},{6,7},{7,6},{8,9},{9,8},{10,11... | collective-permute-start | bytes 3145736 | tf_op jit(solution)/shard_map/ppermute | solution.py:96
  21.0 4.3 %local_grads.3 = bf16[16,128,256]{2,1,0:T(8,128)(2,1)} custom-call(s32[1]{0:T(128)} %bitcast.5.core, bf16[192,128]{1,0:T(8,128)(2,1)} %hid.3, bf16[192,8192]{1,0:T(8,128)(2,1)} %og.1, bf16[192,8192]{1,0:T(8,128)(2,1)} %og.1, bf16[192,8192]{1,0:T(8,128)(2,1)} %og.1, bf16[192,8192]{1,0:T(8,128)(2,1)} %og.1, s32[64,128]{1,0:T(8,128)} %bitcast.26), custom_call_target="tpu_custom_call" | custom-call | flops 201326592 | bytes 2621440 | tf_op jit(solution)/shard_map/local_grads/pallas_call | solution.py:34
  25.3 0.0 collective-permute-done
  25.3 1.5 add_convert_fusion
  26.9 17.4 %all_to_all.15 = bf16[4,4,128,256]{3,2,1,0:T(8,128)(2,1)S(1)} all-to-all(bf16[4,4,128,256]{3,2,1,0:T(8,128)(2,1)S(1)} %bitcast.20), channel_id=1, replica_groups=mesh['x'=4,'zl'=8,'y'=4,'zh'=4,'c'=2] {'y'}, dimensions={0} | all-to-all | bytes 2097152 | tf_op jit(solution)/shard_map/all_to_all | solution.py:104
  44.2 0.9 reduce_sum.32
  45.1 0.0 copy-start.3
  45.2 17.1 %all-to-all-start.1 = ((bf16[4,128,256]{2,1,0:T(8,128)(2,1)}), bf16[4,128,256]{2,1,0:T(8,128)(2,1)S(1)}, u32[]{:S(2)}, u32[]{:S(2)}) async-start(bf16[4,128,256]{2,1,0:T(8,128)(2,1)} %reduce_sum.32), calls=%async_computation.1 | async-start | bytes 524288 | tf_op jit(solution)/shard_map/all_to_all | solution.py:104
  62.2 0.0 copy-done
  62.2 12.1 %collective-permute-start.3 = (bf16[32,256]{1,0:T(8,128)(2,1)S(1)}, bf16[32,256]{1,0:T(8,128)(2,1)S(1)}, u32[]{:S(2)}, u32[]{:S(2)}) collective-permute-start(bf16[32,256]{1,0:T(8,128)(2,1)S(1)} %constant_dynamic-slice_fusion), channel_id=1, source_target_pairs={{0,2},{2,4},{4,6},{6,0},{1,3},{3,5},{5,7},{7,1},{8,10},{10,12},{12... | collective-permute-start | bytes 49160 | tf_op jit(solution)/shard_map/ppermute | solution.py:96
  74.3 11.8 %collective-permute-start.2 = (bf16[32,256]{1,0:T(8,128)(2,1)S(1)}, bf16[32,256]{1,0:T(8,128)(2,1)S(1)}, u32[]{:S(2)}, u32[]{:S(2)}) collective-permute-start(bf16[32,256]{1,0:T(8,128)(2,1)S(1)} %constant_dynamic-slice_fusion), channel_id=1, source_target_pairs={{0,4},{2,6},{4,0},{6,2},{1,5},{3,7},{5,1},{7,3},{8,12},{10,14},{12... | collective-permute-start | bytes 49160 | tf_op jit(solution)/shard_map/ppermute | solution.py:96
  86.1 11.8 %collective-permute-start.1 = (bf16[32,256]{1,0:T(8,128)(2,1)S(1)}, bf16[32,256]{1,0:T(8,128)(2,1)S(1)}, u32[]{:S(2)}, u32[]{:S(2)}) collective-permute-start(bf16[32,256]{1,0:T(8,128)(2,1)S(1)} %constant_dynamic-slice_fusion), channel_id=1, source_target_pairs={{0,6},{2,0},{4,2},{6,4},{1,7},{3,1},{5,3},{7,5},{8,14},{10,8},{12,... | collective-permute-start | bytes 49160 | tf_op jit(solution)/shard_map/ppermute | solution.py:96
  97.9 0.0 collective-permute-done.3
  97.9 3.4 %collective-permute-done.2 = bf16[32,256]{1,0:T(8,128)(2,1)S(1)} collective-permute-done((bf16[32,256]{1,0:T(8,128)(2,1)S(1)}, bf16[32,256]{1,0:T(8,128)(2,1)S(1)}, u32[]{:S(2)}, u32[]{:S(2)}) %collective-permute-start.2) | collective-permute-done | bytes 16416 | tf_op jit(solution)/shard_map/ppermute | solution.py:96
  101.4 0.0 collective-permute-done.1
  101.4 2.2 %collective-permute-start.6 = (bf16[4,32,256]{2,1,0:T(8,128)(2,1)S(1)}, bf16[4,32,256]{2,1,0:T(8,128)(2,1)S(1)}, u32[]{:S(2)}, u32[]{:S(2)}) collective-permute-start(bf16[4,32,256]{2,1,0:T(8,128)(2,1)S(1)} %pad_maximum_fusion.2), channel_id=1, source_target_pairs={{0,8},{8,16},{16,24},{24,0},{1,9},{9,17},{17,25},{25,1},{2,10},{10... | collective-permute-start | bytes 196616 | tf_op jit(solution)/shard_map/ppermute | solution.py:96
  103.6 3.7 %collective-permute-start.5 = (bf16[4,32,256]{2,1,0:T(8,128)(2,1)S(1)}, bf16[4,32,256]{2,1,0:T(8,128)(2,1)S(1)}, u32[]{:S(2)}, u32[]{:S(2)}) collective-permute-start(bf16[4,32,256]{2,1,0:T(8,128)(2,1)S(1)} %pad_maximum_fusion.2), channel_id=1, source_target_pairs={{0,16},{8,24},{16,0},{24,8},{1,17},{9,25},{17,1},{25,9},{2,18},{10... | collective-permute-start | bytes 196616 | tf_op jit(solution)/shard_map/ppermute | solution.py:96
  107.3 2.5 %collective-permute-start.4 = (bf16[4,32,256]{2,1,0:T(8,128)(2,1)S(1)}, bf16[4,32,256]{2,1,0:T(8,128)(2,1)S(1)}, u32[]{:S(2)}, u32[]{:S(2)}) collective-permute-start(bf16[4,32,256]{2,1,0:T(8,128)(2,1)S(1)} %pad_maximum_fusion.2), channel_id=1, source_target_pairs={{0,24},{8,0},{16,8},{24,16},{1,25},{9,1},{17,9},{25,17},{2,26},{10... | collective-permute-start | bytes 196616 | tf_op jit(solution)/shard_map/ppermute | solution.py:96
  109.8 0.0 collective-permute-done.6
  109.8 0.3 collective-permute-done.5
  110.1 2.2 %collective-permute-done.4 = bf16[4,32,256]{2,1,0:T(8,128)(2,1)S(1)} collective-permute-done((bf16[4,32,256]{2,1,0:T(8,128)(2,1)S(1)}, bf16[4,32,256]{2,1,0:T(8,128)(2,1)S(1)}, u32[]{:S(2)}, u32[]{:S(2)}) %collective-permute-start.4) | collective-permute-done | bytes 65568 | tf_op jit(solution)/shard_map/ppermute | solution.py:96
  112.3 3.1 %collective-permute-start.9 = (bf16[4,4,32,256]{3,2,1,0:T(8,128)(2,1)S(1)}, bf16[4,4,32,256]{3,2,1,0:T(8,128)(2,1)S(1)}, u32[]{:S(2)}, u32[]{:S(2)}) collective-permute-start(bf16[4,4,32,256]{3,2,1,0:T(8,128)(2,1)S(1)} %get-tuple-element.9), channel_id=1, source_target_pairs={{0,256},{256,512},{512,768},{768,0},{1,257},{257,513},{513,769},{7... | collective-permute-start | bytes 786440 | tf_op jit(solution)/shard_map/ppermute | solution.py:96
  115.5 4.4 %collective-permute-start.8 = (bf16[4,4,32,256]{3,2,1,0:T(8,128)(2,1)S(1)}, bf16[4,4,32,256]{3,2,1,0:T(8,128)(2,1)S(1)}, u32[]{:S(2)}, u32[]{:S(2)}) collective-permute-start(bf16[4,4,32,256]{3,2,1,0:T(8,128)(2,1)S(1)} %get-tuple-element.9), channel_id=1, source_target_pairs={{0,512},{256,768},{512,0},{768,256},{1,513},{257,769},{513,1},{769... | collective-permute-start | bytes 786440 | tf_op jit(solution)/shard_map/ppermute | solution.py:96
  119.9 2.9 %collective-permute-start.7 = (bf16[4,4,32,256]{3,2,1,0:T(8,128)(2,1)S(1)}, bf16[4,4,32,256]{3,2,1,0:T(8,128)(2,1)S(1)}, u32[]{:S(2)}, u32[]{:S(2)}) collective-permute-start(bf16[4,4,32,256]{3,2,1,0:T(8,128)(2,1)S(1)} %get-tuple-element.9), channel_id=1, source_target_pairs={{0,768},{256,0},{512,256},{768,512},{1,769},{257,1},{513,257},{769... | collective-permute-start | bytes 786440 | tf_op jit(solution)/shard_map/ppermute | solution.py:96
  122.8 0.0 collective-permute-done.9
  122.8 1.7 %collective-permute-done.8 = bf16[4,4,32,256]{3,2,1,0:T(8,128)(2,1)S(1)} collective-permute-done((bf16[4,4,32,256]{3,2,1,0:T(8,128)(2,1)S(1)}, bf16[4,4,32,256]{3,2,1,0:T(8,128)(2,1)S(1)}, u32[]{:S(2)}, u32[]{:S(2)}) %collective-permute-start.8) | collective-permute-done | bytes 262176 | tf_op jit(solution)/shard_map/ppermute | solution.py:96
  124.5 2.8 %collective-permute-done.7 = bf16[4,4,32,256]{3,2,1,0:T(8,128)(2,1)S(1)} collective-permute-done((bf16[4,4,32,256]{3,2,1,0:T(8,128)(2,1)S(1)}, bf16[4,4,32,256]{3,2,1,0:T(8,128)(2,1)S(1)}, u32[]{:S(2)}, u32[]{:S(2)}) %collective-permute-start.7) | collective-permute-done | bytes 262176 | tf_op jit(solution)/shard_map/ppermute | solution.py:96
  127.3 0.1 pad_maximum_fusion.own
  127.4 0.0 copy-start.1
  127.4 11.1 %collective-permute-start.10 = (bf16[4,4,4,32,256]{4,3,2,1,0:T(8,128)(2,1)S(1)}, bf16[4,4,4,32,256]{4,3,2,1,0:T(8,128)(2,1)S(1)}, u32[]{:S(2)}, u32[]{:S(2)}) collective-permute-start(bf16[4,4,4,32,256]{4,3,2,1,0:T(8,128)(2,1)S(1)} %pad_maximum_fusion.own), channel_id=1, source_target_pairs={{0,1},{1,0},{2,3},{3,2},{4,5},{5,4},{6,7},{7,6},{8,9},{9,8},{10,11... | collective-permute-start | bytes 3145736 | tf_op jit(solution)/shard_map/ppermute | solution.py:96
  138.5 0.0 copy-done.3
  138.6 0.1 copy.19
  138.7 0.2 broadcast_in_dim.8
  138.9 0.1 reshape.14
  139.0 0.0 all-to-all-done.1
  139.1 0.7 minimum_convert_fusion
  139.8 11.1 %all-to-all-start.2 = ((bf16[32,4,256]{2,1,0:T(4,128)(2,1)}), bf16[32,4,256]{2,1,0:T(4,128)(2,1)S(1)}, u32[]{:S(2)}, u32[]{:S(2)}) async-start(bf16[32,4,256]{2,1,0:T(4,128)(2,1)} %minimum_convert_fusion), calls=%async_computation.2 | async-start | bytes 131072 | tf_op jit(solution)/shard_map/all_to_all | solution.py:104
  150.9 0.6 pad_add_fusion.pos
  151.5 0.0 collective-permute-done.10.oth
  151.5 0.0 copy-done.1
  151.5 0.0 copy-start.2
  151.5 1.0 copy-done.2
  152.5 5.3 %hidden_grads.1 = bf16[192,128]{1,0:T(8,128)(2,1)} custom-call(s32[4]{0:T(128)} %pad_add_fusion.pos, bf16[192,8192]{1,0:T(8,128)(2,1)} %og.1, bf16[4,4,4,32,256]{4,3,2,1,0:T(8,128)(2,1)} %copy-done.1, bf16[4,4,4,32,256]{4,3,2,1,0:T(8,128)(2,1)} %copy-done.2), custom_call_target="tpu_custom_call" | custom-call | flops 402653184 | bytes 5242880 | tf_op jit(solution)/shard_map/hidden_grads/pallas_call | solution.py:79
  157.8 4.7 %all-to-all-done.2 = bf16[32,4,256]{2,1,0:T(4,128)(2,1)S(1)} async-done(((bf16[32,4,256]{2,1,0:T(4,128)(2,1)}), bf16[32,4,256]{2,1,0:T(4,128)(2,1)S(1)}, u32[]{:S(2)}, u32[]{:S(2)}) %all-to-all-start.2) | async-done | bytes 65568 | tf_op jit(solution)/shard_map/all_to_all | solution.py:104
  162.5 0.6 convert_reduce_fusion.1
  (6 shorter events, 0.1 us)
Async XLA Ops:
  0.6 61.6 %copy-start = (bf16[128,256]{1,0:T(8,128)(2,1)S(1)}, bf16[128,256]{1,0:T(8,128)(2,1)}, u32[]{:S(2)}) copy-start(bf16[128,256]{1,0:T(8,128)(2,1)} %param.7) | copy-start | bytes 196612
  4.9 20.4 %collective-permute-start = (bf16[16,128,256]{2,1,0:T(8,128)(2,1)}, bf16[16,128,256]{2,1,0:T(8,128)(2,1)S(1)}, u32[]{:S(2)}, u32[]{:S(2)}) collective-permute-start(bf16[16,128,256]{2,1,0:T(8,128)(2,1)} %local_grads.2), channel_id=1, source_target_pairs={{0,1},{1,0},{2,3},{3,2},{4,5},{5,4},{6,7},{7,6},{8,9},{9,8},{10,11... | collective-permute-start | bytes 3145736 | tf_op jit(solution)/shard_map/ppermute | solution.py:96
  45.1 93.4 %copy-start.3 = (s32[128,2]{0,1:T(2,128)S(1)}, s32[128,2]{0,1:T(2,128)}, u32[]{:S(2)}) copy-start(s32[128,2]{0,1:T(2,128)} %param.9) | copy-start | bytes 3076
  45.2 93.9 %all-to-all-start.1 = ((bf16[4,128,256]{2,1,0:T(8,128)(2,1)}), bf16[4,128,256]{2,1,0:T(8,128)(2,1)S(1)}, u32[]{:S(2)}, u32[]{:S(2)}) async-start(bf16[4,128,256]{2,1,0:T(8,128)(2,1)} %reduce_sum.32), calls=%async_computation.1 | async-start | bytes 524288 | tf_op jit(solution)/shard_map/all_to_all | solution.py:104
  62.2 35.7 %collective-permute-start.3 = (bf16[32,256]{1,0:T(8,128)(2,1)S(1)}, bf16[32,256]{1,0:T(8,128)(2,1)S(1)}, u32[]{:S(2)}, u32[]{:S(2)}) collective-permute-start(bf16[32,256]{1,0:T(8,128)(2,1)S(1)} %constant_dynamic-slice_fusion), channel_id=1, source_target_pairs={{0,2},{2,4},{4,6},{6,0},{1,3},{3,5},{5,7},{7,1},{8,10},{10,12},{12... | collective-permute-start | bytes 49160 | tf_op jit(solution)/shard_map/ppermute | solution.py:96
  74.3 27.1 %collective-permute-start.2 = (bf16[32,256]{1,0:T(8,128)(2,1)S(1)}, bf16[32,256]{1,0:T(8,128)(2,1)S(1)}, u32[]{:S(2)}, u32[]{:S(2)}) collective-permute-start(bf16[32,256]{1,0:T(8,128)(2,1)S(1)} %constant_dynamic-slice_fusion), channel_id=1, source_target_pairs={{0,4},{2,6},{4,0},{6,2},{1,5},{3,7},{5,1},{7,3},{8,12},{10,14},{12... | collective-permute-start | bytes 49160 | tf_op jit(solution)/shard_map/ppermute | solution.py:96
  86.1 15.2 %collective-permute-start.1 = (bf16[32,256]{1,0:T(8,128)(2,1)S(1)}, bf16[32,256]{1,0:T(8,128)(2,1)S(1)}, u32[]{:S(2)}, u32[]{:S(2)}) collective-permute-start(bf16[32,256]{1,0:T(8,128)(2,1)S(1)} %constant_dynamic-slice_fusion), channel_id=1, source_target_pairs={{0,6},{2,0},{4,2},{6,4},{1,7},{3,1},{5,3},{7,5},{8,14},{10,8},{12,... | collective-permute-start | bytes 49160 | tf_op jit(solution)/shard_map/ppermute | solution.py:96
  101.4 8.4 %collective-permute-start.6 = (bf16[4,32,256]{2,1,0:T(8,128)(2,1)S(1)}, bf16[4,32,256]{2,1,0:T(8,128)(2,1)S(1)}, u32[]{:S(2)}, u32[]{:S(2)}) collective-permute-start(bf16[4,32,256]{2,1,0:T(8,128)(2,1)S(1)} %pad_maximum_fusion.2), channel_id=1, source_target_pairs={{0,8},{8,16},{16,24},{24,0},{1,9},{9,17},{17,25},{25,1},{2,10},{10... | collective-permute-start | bytes 196616 | tf_op jit(solution)/shard_map/ppermute | solution.py:96
  103.6 6.5 %collective-permute-start.5 = (bf16[4,32,256]{2,1,0:T(8,128)(2,1)S(1)}, bf16[4,32,256]{2,1,0:T(8,128)(2,1)S(1)}, u32[]{:S(2)}, u32[]{:S(2)}) collective-permute-start(bf16[4,32,256]{2,1,0:T(8,128)(2,1)S(1)} %pad_maximum_fusion.2), channel_id=1, source_target_pairs={{0,16},{8,24},{16,0},{24,8},{1,17},{9,25},{17,1},{25,9},{2,18},{10... | collective-permute-start | bytes 196616 | tf_op jit(solution)/shard_map/ppermute | solution.py:96
  107.3 5.0 %collective-permute-start.4 = (bf16[4,32,256]{2,1,0:T(8,128)(2,1)S(1)}, bf16[4,32,256]{2,1,0:T(8,128)(2,1)S(1)}, u32[]{:S(2)}, u32[]{:S(2)}) collective-permute-start(bf16[4,32,256]{2,1,0:T(8,128)(2,1)S(1)} %pad_maximum_fusion.2), channel_id=1, source_target_pairs={{0,24},{8,0},{16,8},{24,16},{1,25},{9,1},{17,9},{25,17},{2,26},{10... | collective-permute-start | bytes 196616 | tf_op jit(solution)/shard_map/ppermute | solution.py:96
  112.3 10.4 %collective-permute-start.9 = (bf16[4,4,32,256]{3,2,1,0:T(8,128)(2,1)S(1)}, bf16[4,4,32,256]{3,2,1,0:T(8,128)(2,1)S(1)}, u32[]{:S(2)}, u32[]{:S(2)}) collective-permute-start(bf16[4,4,32,256]{3,2,1,0:T(8,128)(2,1)S(1)} %get-tuple-element.9), channel_id=1, source_target_pairs={{0,256},{256,512},{512,768},{768,0},{1,257},{257,513},{513,769},{7... | collective-permute-start | bytes 786440 | tf_op jit(solution)/shard_map/ppermute | solution.py:96
  115.5 9.0 %collective-permute-start.8 = (bf16[4,4,32,256]{3,2,1,0:T(8,128)(2,1)S(1)}, bf16[4,4,32,256]{3,2,1,0:T(8,128)(2,1)S(1)}, u32[]{:S(2)}, u32[]{:S(2)}) collective-permute-start(bf16[4,4,32,256]{3,2,1,0:T(8,128)(2,1)S(1)} %get-tuple-element.9), channel_id=1, source_target_pairs={{0,512},{256,768},{512,0},{768,256},{1,513},{257,769},{513,1},{769... | collective-permute-start | bytes 786440 | tf_op jit(solution)/shard_map/ppermute | solution.py:96
  119.9 7.4 %collective-permute-start.7 = (bf16[4,4,32,256]{3,2,1,0:T(8,128)(2,1)S(1)}, bf16[4,4,32,256]{3,2,1,0:T(8,128)(2,1)S(1)}, u32[]{:S(2)}, u32[]{:S(2)}) collective-permute-start(bf16[4,4,32,256]{3,2,1,0:T(8,128)(2,1)S(1)} %get-tuple-element.9), channel_id=1, source_target_pairs={{0,768},{256,0},{512,256},{768,512},{1,769},{257,1},{513,257},{769... | collective-permute-start | bytes 786440 | tf_op jit(solution)/shard_map/ppermute | solution.py:96
  127.4 24.1 %copy-start.1 = (bf16[4,4,4,32,256]{4,3,2,1,0:T(8,128)(2,1)}, bf16[4,4,4,32,256]{4,3,2,1,0:T(8,128)(2,1)S(1)}, u32[]{:S(2)}) copy-start(bf16[4,4,4,32,256]{4,3,2,1,0:T(8,128)(2,1)S(1)} %pad_maximum_fusion.own) | copy-start | bytes 3145732
  127.4 24.1 %collective-permute-start.10 = (bf16[4,4,4,32,256]{4,3,2,1,0:T(8,128)(2,1)S(1)}, bf16[4,4,4,32,256]{4,3,2,1,0:T(8,128)(2,1)S(1)}, u32[]{:S(2)}, u32[]{:S(2)}) collective-permute-start(bf16[4,4,4,32,256]{4,3,2,1,0:T(8,128)(2,1)S(1)} %pad_maximum_fusion.own), channel_id=1, source_target_pairs={{0,1},{1,0},{2,3},{3,2},{4,5},{5,4},{6,7},{7,6},{8,9},{9,8},{10,11... | collective-permute-start | bytes 3145736 | tf_op jit(solution)/shard_map/ppermute | solution.py:96
  139.8 22.7 %all-to-all-start.2 = ((bf16[32,4,256]{2,1,0:T(4,128)(2,1)}), bf16[32,4,256]{2,1,0:T(4,128)(2,1)S(1)}, u32[]{:S(2)}, u32[]{:S(2)}) async-start(bf16[32,4,256]{2,1,0:T(4,128)(2,1)} %minimum_convert_fusion), calls=%async_computation.2 | async-start | bytes 131072 | tf_op jit(solution)/shard_map/all_to_all | solution.py:104
  151.5 1.0 copy-start.2

commit v4 on v3

v4 whole, which is shorter than its diff:
```python
import jax
import jax.numpy as jnp
from jax import lax
from jax.experimental import pallas as pl
from jax.experimental.pallas import tpu as pltpu
from jax.sharding import Mesh, PartitionSpec as P

SIZES = {"x": 4, "zl": 8, "y": 4, "zh": 4, "c": 2}
AXES = tuple(SIZES)
OUTER = ("x", "zl")
N_OUTER = 32
LIMIT = 448.0
VMEM = 8 << 20
F32, BF16 = jnp.float32, jnp.bfloat16


def limits(exponent):
    return jnp.left_shift(1, exponent + 16).astype(F32) * (LIMIT * 2.0**-16)


def grad_kernel(core, hid, og, exponent, own, oth, acts):
    c = core[0]

    @pl.when(pl.program_id(0) == 0)
    def _():
        acts[...] = hid[...].T

    bound = limits(exponent[...])
    other = pltpu.roll(bound, 14, 0)
    for side, out in ((c, own), (1 - c, oth)):
        mine = jnp.where(side == 0, bound, other).T
        for zh in range(4):
            cols = og[:, pl.ds(pl.multiple_of(512 * zh + 256 * side, 256), 256)]
            local = jnp.dot(acts[...], cols, preferred_element_type=F32)
            for half in range(2):
                most = mine[:, 4 * zh + half : 4 * zh + half + 1]
                lanes = slice(128 * half, 128 * half + 128)
                out[zh, :, lanes] = jnp.clip(local[:, lanes], -most, most).astype(BF16)


def local_grads(core, hidden, out_grad, exponent):
    block = jax.ShapeDtypeStruct((16, 128, 256), BF16)
    return pl.pallas_call(
        grad_kernel,
        grid_spec=pltpu.PrefetchScalarGridSpec(
            num_scalar_prefetch=1,
            grid=(4,),
            in_specs=[
                pl.BlockSpec((192, 128), lambda y, core: (0, 0)),
                pl.BlockSpec((192, 2048), lambda y, core: (0, y)),
                pl.BlockSpec((16, 128), lambda y, core: (y, 0)),
            ],
            out_specs=[pl.BlockSpec((4, 128, 256), lambda y, core: (y, 0, 0))] * 2,
            scratch_shapes=[pltpu.VMEM((128, 192), BF16)],
        ),
        out_shape=[block, block],
        compiler_params=pltpu.CompilerParams(vmem_limit_bytes=VMEM),
        cost_estimate=pl.CostEstimate(flops=1 << 20, bytes_accessed=1 << 16, transcendentals=0),
        name="local_grads",
    )(core, hidden, out_grad, exponent)


def join_kernel(own, got, quarter, out):
    for zh in range(4):
        out[0, 128 * zh : 128 * (zh + 1)] = (own[zh].astype(F32) + got[zh].astype(F32)).astype(BF16)
    out[0, 512:] = quarter[...].reshape(128, 256)


def joined(own, got, quarter):
    block = pl.BlockSpec((4, 128, 256), lambda y: (y, 0, 0))
    return pl.pallas_call(
        join_kernel,
        grid=(4,),
        in_specs=[block, block, pl.BlockSpec((4, 32, 256), lambda y: (0, 0, 0))],
        out_specs=pl.BlockSpec((1, 640, 256), lambda y: (y, 0, 0)),
        out_shape=jax.ShapeDtypeStruct((4, 640, 256), BF16),
        compiler_params=pltpu.CompilerParams(vmem_limit_bytes=VMEM),
        cost_estimate=pl.CostEstimate(flops=1 << 20, bytes_accessed=13 << 18, transcendentals=0),
        name="joined",
    )(own, got, quarter)


def hidden_kernel(pos, og, own, oth, out, total):
    c, x = pos[0], pos[1]
    step = pl.program_id(0)

    @pl.when(step == 0)
    def _():
        total[...] = jnp.zeros_like(total)

    acc = total[...]
    for zh in range(4):
        for core, part in ((c, own), (1 - c, oth)):
            rows = part[:, 0, 32 * zh : 32 * (zh + 1)].reshape(128, 256)
            cols = og[:, pl.ds(pl.multiple_of(512 * zh + core * 256, 256), 256)]
            acc += lax.dot_general(cols, rows, (((1,), (1,)), ((), ())), preferred_element_type=F32)
    total[...] = acc

    @pl.when(step == 3)
    def _():
        out[...] = pltpu.roll(acc, 32 * x, 1).astype(BF16)


def hidden_grads(pos, out_grad, own, oth):
    part = pl.BlockSpec((4, 1, 128, 256), lambda y, pos: (0, y, 0, 0))
    return pl.pallas_call(
        hidden_kernel,
        grid_spec=pltpu.PrefetchScalarGridSpec(
            num_scalar_prefetch=1,
            grid=(4,),
            in_specs=[pl.BlockSpec((192, 2048), lambda y, pos: (0, y)), part, part],
            out_specs=pl.BlockSpec((192, 128), lambda y, pos: (0, 0)),
            scratch_shapes=[pltpu.VMEM((192, 128), F32)],
        ),
        out_shape=jax.ShapeDtypeStruct((192, 128), BF16),
        compiler_params=pltpu.CompilerParams(vmem_limit_bytes=VMEM),
        cost_estimate=pl.CostEstimate(flops=2 * 192 * 128 * 8192, bytes_accessed=5 << 20, transcendentals=0),
        name="hidden_grads",
    )(pos, out_grad, own, oth)


def shifted(value, axis, k):
    n = SIZES[axis]
    return lax.ppermute(value, axis, [(i, (i - k) % n) for i in range(n)])


def gather(value, axis):
    return jnp.stack([value] + [shifted(value, axis, k) for k in (1, 2, 3)])


def swap(value, axes):
    return lax.all_to_all(value, axes, 0, 0, tiled=True)


def after(value, *earlier):
    return lax.optimization_barrier((value, *earlier))[0]


def summed(parts):
    return parts.astype(F32).sum(0)


def per_device(out_grad, hidden, weight, e1, e2):
    x, c = lax.axis_index("x"), lax.axis_index("c")
    mine = lax.dynamic_slice_in_dim(weight, x * 32, 32, 0)
    quarter = swap(jnp.broadcast_to(mine, (4, 32, 256)), "zh")

    own, oth = local_grads(c[None], hidden, out_grad, e1.T)
    got = shifted(oth, "c", 1)
    columns = swap(joined(own, got, quarter), "y")

    line = summed(columns[:, :512].reshape(4, 4, 128, 256)).astype(BF16)
    group = summed(swap(line, "zh"))
    limit = jnp.repeat(limits(e2), 128, axis=1)
    again = jnp.clip(group, -limit, limit).astype(BF16)
    rows = swap(again.reshape(N_OUTER, -1, 256), OUTER)
    weight_grad = summed(rows)

    part = gather(after(columns[:, 512:], line), "x")
    hidden_grad = hidden_grads(jnp.stack([c, x]), out_grad, part, shifted(part, "c", 1))
    return hidden_grad, weight_grad


def solution(mesh):
    fine = Mesh(mesh.devices.reshape(tuple(SIZES.values())), AXES)
    every, inner = P(AXES, None), ("y", "zh", "c")
    return jax.shard_map(
        per_device,
        mesh=fine,
        in_specs=(every, every, P(None, inner), every, P(OUTER, inner)),
        out_specs=(every, P(OUTER, inner)),
        check_vma=False,
    )
```

time: 164 us -> 147 us (0.90)
  the two profiles are of different devices: /device:TPU:1 before, /device:TPU:2 now
where the time goes in v4:
time: 147 us
  blocking collectives  72.1 us (49%)
  starting transfers between devices  35.6 us (24%)
  waiting for transfers between devices  20.3 us (14%)
  Pallas kernels  7.32 us (5%)
  local copies, waits for them, and re-layouts  6.18 us (4%)
  other arithmetic  4.23 us (3%)
    all_to_all x2, blocking collectives, swap(): return lax.all_to_all(value, axes, 0, 0, tiled=True)  72.1 us
    all_to_all x2, starting transfers between devices, swap(): return lax.all_to_all(value, axes, 0, 0, tiled=True)  21.2 us
    ppermute x5, starting transfers between devices, shifted(): return lax.ppermute(value, axis, [(i, (i - k) % n) for i in range(n)])  14.4 us
    all_to_all x2, waiting for transfers between devices, swap(): return lax.all_to_all(value, axes, 0, 0, tiled=True)  13.3 us
    ppermute x5, waiting for transfers between devices, shifted(): return lax.ppermute(value, axis, [(i, (i - k) % n) for i in range(n)])  7.07 us
    pallas_call x1, Pallas kernels, hidden_grads(): pl.pallas_call(hidden_kernel, grid_spec=pltpu.PrefetchScalarGridSpec(num_...  4.67 us
    unnamed x12, local copies, waits for them, and re-layouts  3.49 us
  transfers between devices with their start and end apart: 7, of which 4 were waited for; matrix products, arithmetic and copies ran while one was open for 4% of the time, Pallas kernels for 3%

profile of v4, /device:TPU:2, one launch (start us, length us, event | category | flops | bytes accessed | tf_op | source)
XLA Modules:
  0.0 146.6 jit_solution(11543268573525926974)
XLA Ops:
  0.6 0.0 copy-start
  0.6 0.0 copy-start.1
  0.7 1.9 %copy-done.1 = bf16[192,8192]{1,0:T(8,128)(2,1)S(1)} copy-done((bf16[192,8192]{1,0:T(8,128)(2,1)S(1)}, bf16[192,8192]{1,0:T(8,128)(2,1)}, u32[]{:S(2)}) %copy-start.1) | copy-done | bytes 3145752
  2.6 0.0 copy-start.3
  2.6 0.8 copy-done.3
  3.4 0.0 copy-start.4
  3.4 0.8 copy-done.4
  4.1 2.3 %local_grads.1 = (bf16[16,128,256]{2,1,0:T(8,128)(2,1)S(1)}, bf16[16,128,256]{2,1,0:T(8,128)(2,1)S(1)}) custom-call(s32[1]{0:T(128)} %bitcast.core, bf16[192,128]{1,0:T(8,128)(2,1)S(1)} %copy-done.3, bf16[192,8192]{1,0:T(8,128)(2,1)S(1)} %copy-done.1, s32[64,128]{1,0:T(8,128)S(1)} %bitcast.8), custom_call_target="tpu_custom_call" | custom-call | flops 1048576 | bytes 65536 | tf_op jit(solution)/shard_map/local_grads/pallas_call | solution.py:43
  6.5 1.9 %collective-permute-start = (bf16[16,128,256]{2,1,0:T(8,128)(2,1)S(1)}, bf16[16,128,256]{2,1,0:T(8,128)(2,1)S(1)}, u32[]{:S(2)}, u32[]{:S(2)}) collective-permute-start(bf16[16,128,256]{2,1,0:T(8,128)(2,1)S(1)} %get-tuple-element.6), channel_id=1, source_target_pairs={{0,1},{1,0},{2,3},{3,2},{4,5},{5,4},{6,7},{7,6},{8,9},{9,8},{10,11... | collective-permute-start | bytes 3145736 | tf_op jit(solution)/shard_map/ppermute | solution.py:124
  8.4 0.0 copy-done
  8.5 51.4 %all_to_all.20.quarter = bf16[4,32,256]{2,1,0:T(8,128)(2,1)S(1)} all-to-all(bf16[4,32,256]{2,1,0:T(8,128)(2,1)S(1)} %broadcast_in_dim.7), channel_id=1, replica_groups=mesh['x'=4,'zl'=8,'y'=4,'zh'=4,'c'=2] {'zh'}, dimensions={0} | all-to-all | bytes 131072 | tf_op jit(solution)/shard_map/all_to_all | solution.py:132
  59.9 0.0 collective-permute-done.got
  59.9 0.3 joined.1
  60.2 20.8 %all_to_all.21 = bf16[4,640,256]{2,1,0:T(8,128)(2,1)S(1)} all-to-all(bf16[4,640,256]{2,1,0:T(8,128)(2,1)S(1)} %joined.1), channel_id=1, replica_groups=mesh['x'=4,'zl'=8,'y'=4,'zh'=4,'c'=2] {'y'}, dimensions={0} | all-to-all | bytes 2621440 | tf_op jit(solution)/shard_map/all_to_all | solution.py:132
  80.9 0.8 slice_reduce_fusion
  81.8 3.4 %all-to-all-start.2 = ((bf16[4,128,256]{2,1,0:T(8,128)(2,1)}), bf16[4,128,256]{2,1,0:T(8,128)(2,1)S(1)}, u32[]{:S(2)}, u32[]{:S(2)}) async-start(bf16[4,128,256]{2,1,0:T(8,128)(2,1)} %bitcast.3), calls=%async_computation.2 | async-start | bytes 524288 | tf_op jit(solution)/shard_map/all_to_all | solution.py:132
  85.2 0.0 copy-start.5
  85.2 3.4 %collective-permute-start.3 = (bf16[4,128,256]{2,1,0:T(8,128)(2,1)S(1)}, bf16[4,128,256]{2,1,0:T(8,128)(2,1)S(1)}, u32[]{:S(2)}, u32[]{:S(2)}) collective-permute-start(bf16[4,128,256]{2,1,0:T(8,128)(2,1)S(1)} %slice.8), channel_id=1, source_target_pairs={{0,256},{256,512},{512,768},{768,0},{1,257},{257,513},{513,769},{7... | collective-permute-start | bytes 786440 | tf_op jit(solution)/shard_map/ppermute | solution.py:124
  88.6 3.0 %collective-permute-start.2 = (bf16[4,128,256]{2,1,0:T(8,128)(2,1)S(1)}, bf16[4,128,256]{2,1,0:T(8,128)(2,1)S(1)}, u32[]{:S(2)}, u32[]{:S(2)}) collective-permute-start(bf16[4,128,256]{2,1,0:T(8,128)(2,1)S(1)} %slice.8), channel_id=1, source_target_pairs={{0,512},{256,768},{512,0},{768,256},{1,513},{257,769},{513,1},{769... | collective-permute-start | bytes 786440 | tf_op jit(solution)/shard_map/ppermute | solution.py:124
  91.6 4.1 %collective-permute-start.1 = (bf16[4,128,256]{2,1,0:T(8,128)(2,1)S(1)}, bf16[4,128,256]{2,1,0:T(8,128)(2,1)S(1)}, u32[]{:S(2)}, u32[]{:S(2)}) collective-permute-start(bf16[4,128,256]{2,1,0:T(8,128)(2,1)S(1)} %slice.8), channel_id=1, source_target_pairs={{0,768},{256,0},{512,256},{768,512},{1,769},{257,1},{513,257},{769... | collective-permute-start | bytes 786440 | tf_op jit(solution)/shard_map/ppermute | solution.py:124
  95.7 0.0 collective-permute-done.3
  95.7 4.4 %collective-permute-done.2 = bf16[4,128,256]{2,1,0:T(8,128)(2,1)S(1)} collective-permute-done((bf16[4,128,256]{2,1,0:T(8,128)(2,1)S(1)}, bf16[4,128,256]{2,1,0:T(8,128)(2,1)S(1)}, u32[]{:S(2)}, u32[]{:S(2)}) %collective-permute-start.2) | collective-permute-done | bytes 262176 | tf_op jit(solution)/shard_map/ppermute | solution.py:124
  100.1 2.7 %collective-permute-done.1 = bf16[4,128,256]{2,1,0:T(8,128)(2,1)S(1)} collective-permute-done((bf16[4,128,256]{2,1,0:T(8,128)(2,1)S(1)}, bf16[4,128,256]{2,1,0:T(8,128)(2,1)S(1)}, u32[]{:S(2)}, u32[]{:S(2)}) %collective-permute-start.1) | collective-permute-done | bytes 262176 | tf_op jit(solution)/shard_map/ppermute | solution.py:124
  102.8 0.0 copy-start.2
  102.8 1.1 pad_maximum_fusion.own
  103.9 2.0 %collective-permute-start.4 = (bf16[4,4,128,256]{3,2,1,0:T(8,128)(2,1)}, bf16[4,4,128,256]{3,2,1,0:T(8,128)(2,1)}, u32[]{:S(2)}, u32[]{:S(2)}) collective-permute-start(bf16[4,4,128,256]{3,2,1,0:T(8,128)(2,1)} %pad_maximum_fusion.own), channel_id=1, source_target_pairs={{0,1},{1,0},{2,3},{3,2},{4,5},{5,4},{6,7},{7,6},{8,9},{9,8},{10,11... | collective-permute-start | bytes 3145736 | tf_op jit(solution)/shard_map/ppermute | solution.py:124
  105.9 0.0 copy-done.5
  105.9 0.1 copy.19
  106.1 0.8 broadcast_in_dim.8
  106.9 1.7 %reshape.12 = f32[32,4,256]{2,1,0:T(4,128)} reshape(f32[128,2,128]{2,1,0:T(2,128)} %broadcast_in_dim.8) | data formatting | bytes 262144 | tf_op jit(solution)/shard_map/reshape | solution.py:154
  108.6 6.5 %all-to-all-done.2 = bf16[4,128,256]{2,1,0:T(8,128)(2,1)S(1)} async-done(((bf16[4,128,256]{2,1,0:T(8,128)(2,1)}), bf16[4,128,256]{2,1,0:T(8,128)(2,1)S(1)}, u32[]{:S(2)}, u32[]{:S(2)}) %all-to-all-start.2) | async-done | bytes 262176 | tf_op jit(solution)/shard_map/all_to_all | solution.py:132
  115.2 1.6 %minimum_convert_fusion = bf16[32,4,256]{2,1,0:T(4,128)(2,1)} fusion(f32[32,4,256]{2,1,0:T(4,128)} %reshape.12, bf16[32,4,256]{2,1,0:T(4,128)(2,1)S(1)} %reduce_sum.37), kind=kLoop, calls=%fused_computation.4 | loop fusion | flops 163840 | bytes 262144 | tf_op jit(solution)/shard_map/convert_element_type | solution.py:155
  116.7 17.8 %all-to-all-start.3 = ((bf16[32,4,256]{2,1,0:T(4,128)(2,1)}), bf16[32,4,256]{2,1,0:T(4,128)(2,1)S(1)}, u32[]{:S(2)}, u32[]{:S(2)}) async-start(bf16[32,4,256]{2,1,0:T(4,128)(2,1)} %minimum_convert_fusion), calls=%async_computation.3 | async-start | bytes 131072 | tf_op jit(solution)/shard_map/all_to_all | solution.py:132
  134.5 0.1 pad_add_fusion.pos
  134.6 0.0 collective-permute-done.4.oth
  134.6 0.0 copy-done.2
  134.6 4.7 %hidden_grads.1 = bf16[192,128]{1,0:T(8,128)(2,1)} custom-call(s32[2]{0:T(128)S(1)} %pad_add_fusion.pos, bf16[192,8192]{1,0:T(8,128)(2,1)S(1)} %copy-done.2, bf16[4,4,128,256]{3,2,1,0:T(8,128)(2,1)} %pad_maximum_fusion.own, bf16[4,4,128,256]{3,2,1,0:T(8,128)(2,1)} %collective-permute-done.4.oth), custom_call_target="tpu_custom_call" | custom-call | flops 402653184 | bytes 5242880 | tf_op jit(solution)/shard_map/hidden_grads/pallas_call | solution.py:106
  139.3 6.7 %all-to-all-done.3 = bf16[32,4,256]{2,1,0:T(4,128)(2,1)S(1)} async-done(((bf16[32,4,256]{2,1,0:T(4,128)(2,1)}), bf16[32,4,256]{2,1,0:T(4,128)(2,1)S(1)}, u32[]{:S(2)}, u32[]{:S(2)}) %all-to-all-start.3) | async-done | bytes 65568 | tf_op jit(solution)/shard_map/all_to_all | solution.py:132
  146.0 0.6 convert_reduce_fusion.1
  (6 shorter events, 0.1 us)
Async XLA Ops:
  0.6 7.8 %copy-start = (bf16[128,256]{1,0:T(8,128)(2,1)S(1)}, bf16[128,256]{1,0:T(8,128)(2,1)}, u32[]{:S(2)}) copy-start(bf16[128,256]{1,0:T(8,128)(2,1)} %param.7) | copy-start | bytes 196612
  0.6 1.9 %copy-start.1 = (bf16[192,8192]{1,0:T(8,128)(2,1)S(1)}, bf16[192,8192]{1,0:T(8,128)(2,1)}, u32[]{:S(2)}) copy-start(bf16[192,8192]{1,0:T(8,128)(2,1)} %og.3) | copy-start | bytes 9437188
  2.6 0.8 copy-start.3
  3.4 0.8 copy-start.4
  6.5 53.4 %collective-permute-start = (bf16[16,128,256]{2,1,0:T(8,128)(2,1)S(1)}, bf16[16,128,256]{2,1,0:T(8,128)(2,1)S(1)}, u32[]{:S(2)}, u32[]{:S(2)}) collective-permute-start(bf16[16,128,256]{2,1,0:T(8,128)(2,1)S(1)} %get-tuple-element.6), channel_id=1, source_target_pairs={{0,1},{1,0},{2,3},{3,2},{4,5},{5,4},{6,7},{7,6},{8,9},{9,8},{10,11... | collective-permute-start | bytes 3145736 | tf_op jit(solution)/shard_map/ppermute | solution.py:124
  81.8 33.4 %all-to-all-start.2 = ((bf16[4,128,256]{2,1,0:T(8,128)(2,1)}), bf16[4,128,256]{2,1,0:T(8,128)(2,1)S(1)}, u32[]{:S(2)}, u32[]{:S(2)}) async-start(bf16[4,128,256]{2,1,0:T(8,128)(2,1)} %bitcast.3), calls=%async_computation.2 | async-start | bytes 524288 | tf_op jit(solution)/shard_map/all_to_all | solution.py:132
  85.2 20.8 %copy-start.5 = (s32[128,2]{0,1:T(2,128)S(1)}, s32[128,2]{0,1:T(2,128)}, u32[]{:S(2)}) copy-start(s32[128,2]{0,1:T(2,128)} %param.9) | copy-start | bytes 3076
  85.2 10.5 %collective-permute-start.3 = (bf16[4,128,256]{2,1,0:T(8,128)(2,1)S(1)}, bf16[4,128,256]{2,1,0:T(8,128)(2,1)S(1)}, u32[]{:S(2)}, u32[]{:S(2)}) collective-permute-start(bf16[4,128,256]{2,1,0:T(8,128)(2,1)S(1)} %slice.8), channel_id=1, source_target_pairs={{0,256},{256,512},{512,768},{768,0},{1,257},{257,513},{513,769},{7... | collective-permute-start | bytes 786440 | tf_op jit(solution)/shard_map/ppermute | solution.py:124
  88.6 11.5 %collective-permute-start.2 = (bf16[4,128,256]{2,1,0:T(8,128)(2,1)S(1)}, bf16[4,128,256]{2,1,0:T(8,128)(2,1)S(1)}, u32[]{:S(2)}, u32[]{:S(2)}) collective-permute-start(bf16[4,128,256]{2,1,0:T(8,128)(2,1)S(1)} %slice.8), channel_id=1, source_target_pairs={{0,512},{256,768},{512,0},{768,256},{1,513},{257,769},{513,1},{769... | collective-permute-start | bytes 786440 | tf_op jit(solution)/shard_map/ppermute | solution.py:124
  91.6 11.1 %collective-permute-start.1 = (bf16[4,128,256]{2,1,0:T(8,128)(2,1)S(1)}, bf16[4,128,256]{2,1,0:T(8,128)(2,1)S(1)}, u32[]{:S(2)}, u32[]{:S(2)}) collective-permute-start(bf16[4,128,256]{2,1,0:T(8,128)(2,1)S(1)} %slice.8), channel_id=1, source_target_pairs={{0,768},{256,0},{512,256},{768,512},{1,769},{257,1},{513,257},{769... | collective-permute-start | bytes 786440 | tf_op jit(solution)/shard_map/ppermute | solution.py:124
  102.8 31.9 %copy-start.2 = (bf16[192,8192]{1,0:T(8,128)(2,1)S(1)}, bf16[192,8192]{1,0:T(8,128)(2,1)}, u32[]{:S(2)}) copy-start(bf16[192,8192]{1,0:T(8,128)(2,1)} %og.3) | copy-start | bytes 9437188
  103.9 30.8 %collective-permute-start.4 = (bf16[4,4,128,256]{3,2,1,0:T(8,128)(2,1)}, bf16[4,4,128,256]{3,2,1,0:T(8,128)(2,1)}, u32[]{:S(2)}, u32[]{:S(2)}) collective-permute-start(bf16[4,4,128,256]{3,2,1,0:T(8,128)(2,1)} %pad_maximum_fusion.own), channel_id=1, source_target_pairs={{0,1},{1,0},{2,3},{3,2},{4,5},{5,4},{6,7},{7,6},{8,9},{9,8},{10,11... | collective-permute-start | bytes 3145736 | tf_op jit(solution)/shard_map/ppermute | solution.py:124
  116.7 29.3 %all-to-all-start.3 = ((bf16[32,4,256]{2,1,0:T(4,128)(2,1)}), bf16[32,4,256]{2,1,0:T(4,128)(2,1)S(1)}, u32[]{:S(2)}, u32[]{:S(2)}) async-start(bf16[32,4,256]{2,1,0:T(4,128)(2,1)} %minimum_convert_fusion), calls=%async_computation.3 | async-start | bytes 131072 | tf_op jit(solution)/shard_map/all_to_all | solution.py:132

commit v5 on v4

--- a/solution.py
+++ b/solution.py
@@ -11,6 +11,7 @@
 N_OUTER = 32
 LIMIT = 448.0
 VMEM = 8 << 20
+ORDER = (0, 1, 3, 2)
 F32, BF16 = jnp.float32, jnp.bfloat16
 
 
@@ -60,28 +61,26 @@
     )(core, hidden, out_grad, exponent)
 
 
-def join_kernel(own, got, quarter, out):
-    for zh in range(4):
-        out[0, 128 * zh : 128 * (zh + 1)] = (own[zh].astype(F32) + got[zh].astype(F32)).astype(BF16)
-    out[0, 512:] = quarter[...].reshape(128, 256)
+def pair_kernel(own, got, out):
+    out[...] = (own[...].astype(F32) + got[...].astype(F32)).astype(BF16)
 
 
-def joined(own, got, quarter):
+def paired(own, got):
     block = pl.BlockSpec((4, 128, 256), lambda y: (y, 0, 0))
     return pl.pallas_call(
-        join_kernel,
+        pair_kernel,
         grid=(4,),
-        in_specs=[block, block, pl.BlockSpec((4, 32, 256), lambda y: (0, 0, 0))],
-        out_specs=pl.BlockSpec((1, 640, 256), lambda y: (y, 0, 0)),
-        out_shape=jax.ShapeDtypeStruct((4, 640, 256), BF16),
+        in_specs=[block, block],
+        out_specs=block,
+        out_shape=jax.ShapeDtypeStruct((16, 128, 256), BF16),
         compiler_params=pltpu.CompilerParams(vmem_limit_bytes=VMEM),
-        cost_estimate=pl.CostEstimate(flops=1 << 20, bytes_accessed=13 << 18, transcendentals=0),
-        name="joined",
-    )(own, got, quarter)
+        cost_estimate=pl.CostEstimate(flops=1 << 20, bytes_accessed=3 << 20, transcendentals=0),
+        name="paired",
+    )(own, got).reshape(4, 4, 128, 256)
 
 
 def hidden_kernel(pos, og, own, oth, out, total):
-    c, x = pos[0], pos[1]
+    c, x, zh = pos[0], pos[1], pos[3]
     step = pl.program_id(0)
 
     @pl.when(step == 0)
@@ -89,11 +88,11 @@
         total[...] = jnp.zeros_like(total)
 
     acc = total[...]
-    for zh in range(4):
+    for k, bits in enumerate(ORDER):
         for core, part in ((c, own), (1 - c, oth)):
-            rows = part[:, 0, 32 * zh : 32 * (zh + 1)].reshape(128, 256)
-            cols = og[:, pl.ds(pl.multiple_of(512 * zh + core * 256, 256), 256)]
-            acc += lax.dot_general(cols, rows, (((1,), (1,)), ((), ())), preferred_element_type=F32)
+            rows = part[:, 0, k].reshape(128, 256)
+            at = pl.multiple_of(512 * jnp.bitwise_xor(zh, bits) + core * 256, 256)
+            acc += lax.dot_general(og[:, pl.ds(at, 256)], rows, (((1,), (1,)), ((), ())), preferred_element_type=F32)
     total[...] = acc
 
     @pl.when(step == 3)
@@ -102,14 +101,14 @@
 
 
 def hidden_grads(pos, out_grad, own, oth):
-    part = pl.BlockSpec((4, 1, 128, 256), lambda y, pos: (0, y, 0, 0))
+    part = pl.BlockSpec((4, 1, 4, 32, 256), lambda k, pos: (0, k, 0, 0, 0))
     return pl.pallas_call(
         hidden_kernel,
         grid_spec=pltpu.PrefetchScalarGridSpec(
             num_scalar_prefetch=1,
             grid=(4,),
-            in_specs=[pl.BlockSpec((192, 2048), lambda y, pos: (0, y)), part, part],
-            out_specs=pl.BlockSpec((192, 128), lambda y, pos: (0, 0)),
+            in_specs=[pl.BlockSpec((192, 2048), lambda k, pos: (0, lax.rem(pos[2] + k, 4))), part, part],
+            out_specs=pl.BlockSpec((192, 128), lambda k, pos: (0, 0)),
             scratch_shapes=[pltpu.VMEM((192, 128), F32)],
         ),
         out_shape=jax.ShapeDtypeStruct((192, 128), BF16),
@@ -117,6 +116,10 @@
         cost_estimate=pl.CostEstimate(flops=2 * 192 * 128 * 8192, bytes_accessed=5 << 20, transcendentals=0),
         name="hidden_grads",
     )(pos, out_grad, own, oth)
+
+
+def exchanged(value, axis, bits):
+    return lax.ppermute(value, axis, [(i, i ^ bits) for i in range(SIZES[axis])])
 
 
 def shifted(value, axis, k):
@@ -141,23 +144,28 @@
 
 
 def per_device(out_grad, hidden, weight, e1, e2):
-    x, c = lax.axis_index("x"), lax.axis_index("c")
+    x, y, zh, c = (lax.axis_index(a) for a in ("x", "y", "zh", "c"))
     mine = lax.dynamic_slice_in_dim(weight, x * 32, 32, 0)
-    quarter = swap(jnp.broadcast_to(mine, (4, 32, 256)), "zh")
+    near = exchanged(mine, "zh", 1)
 
     own, oth = local_grads(c[None], hidden, out_grad, e1.T)
-    got = shifted(oth, "c", 1)
-    columns = swap(joined(own, got, quarter), "y")
+    got = shifted(after(oth, near), "c", 1)
+    pairs = paired(own, got)
+    columns = swap(pairs, "y")
+    line = summed(columns).astype(BF16)
 
-    line = summed(columns[:, :512].reshape(4, 4, 128, 256)).astype(BF16)
-    group = summed(swap(line, "zh"))
+    two = jnp.stack([mine, after(near, pairs)])
+    quarter = jnp.concatenate([two, exchanged(two, "zh", 3)])
+
+    group = summed(swap(after(line, quarter), "zh"))
     limit = jnp.repeat(limits(e2), 128, axis=1)
     again = jnp.clip(group, -limit, limit).astype(BF16)
     rows = swap(again.reshape(N_OUTER, -1, 256), OUTER)
     weight_grad = summed(rows)
 
-    part = gather(after(columns[:, 512:], line), "x")
-    hidden_grad = hidden_grads(jnp.stack([c, x]), out_grad, part, shifted(part, "c", 1))
+    part = gather(gather(after(quarter, line), "y"), "x")
+    pos = jnp.stack([c, x, y, zh])
+    hidden_grad = hidden_grads(pos, out_grad, part, shifted(part, "c", 1))
     return hidden_grad, weight_grad
 
 

time: 147 us -> 136 us (0.925)
  the two profiles are of different devices: /device:TPU:2 before, /device:TPU:8 now
where the time goes in v5:
time: 136 us; the launch traced here: 135 us
  starting transfers between devices  88.3 us (65%)
  waiting for transfers between devices  24.7 us (18%)
  Pallas kernels  8.73 us (6%)
  local copies, waits for them, and re-layouts  6.95 us (5%)
  other arithmetic  5.63 us (4%)
    all_to_all x3, starting transfers between devices, swap(): return lax.all_to_all(value, axes, 0, 0, tiled=True)  36.1 us
    ppermute x2, starting transfers between devices, exchanged(): lax.ppermute(value, axis, [(i, i ^ bits) for i in range(SIZES[axis])])  26.6 us
    ppermute x8, starting transfers between devices, shifted(): return lax.ppermute(value, axis, [(i, (i - k) % n) for i in range(n)])  25.6 us
    ppermute x8, waiting for transfers between devices, shifted(): return lax.ppermute(value, axis, [(i, (i - k) % n) for i in range(n)])  11.2 us
    all_to_all x3, waiting for transfers between devices, swap(): return lax.all_to_all(value, axes, 0, 0, tiled=True)  7.85 us
    ppermute x2, waiting for transfers between devices, exchanged(): lax.ppermute(value, axis, [(i, i ^ bits) for i in range(SIZES[axis])])  5.65 us
    pallas_call x1, Pallas kernels, hidden_grads(): pl.pallas_call(hidden_kernel, grid_spec=pltpu.PrefetchScalarGridSpec(num_...  4.71 us
    unnamed x12, local copies, waits for them, and re-layouts  4.28 us
  transfers between devices with their start and end apart: 13, of which 8 were waited for; matrix products, arithmetic and copies ran while one was open for 4% of the time, Pallas kernels for 5%

profile of v5, /device:TPU:8, one launch (start us, length us, event | category | flops | bytes accessed | tf_op | source)
XLA Modules:
  0.0 135.2 jit_solution(8047838948142696635)
XLA Ops:
  0.6 0.0 copy-start
  0.7 0.8 copy-done
  1.5 15.7 %collective-permute-start = (bf16[32,256]{1,0:T(8,128)(2,1)S(1)}, bf16[32,256]{1,0:T(8,128)(2,1)S(1)}, u32[]{:S(2)}, u32[]{:S(2)}) collective-permute-start(bf16[32,256]{1,0:T(8,128)(2,1)S(1)} %constant_dynamic-slice_fusion), channel_id=1, source_target_pairs={{0,2},{2,0},{4,6},{6,4},{1,3},{3,1},{5,7},{7,5},{8,10},{10,8},{12,... | collective-permute-start | bytes 49160 | tf_op jit(solution)/shard_map/ppermute | solution.py:122
  17.2 0.0 copy-start.1
  17.2 1.9 %copy-done.1 = bf16[192,8192]{1,0:T(8,128)(2,1)S(1)} copy-done((bf16[192,8192]{1,0:T(8,128)(2,1)S(1)}, bf16[192,8192]{1,0:T(8,128)(2,1)}, u32[]{:S(2)}) %copy-start.1) | copy-done | bytes 3145752
  19.1 0.0 copy-start.3
  19.1 0.8 copy-done.3
  19.9 0.0 copy-start.4
  19.9 0.8 copy-done.4
  20.6 2.3 %local_grads.1 = (bf16[16,128,256]{2,1,0:T(8,128)(2,1)S(1)}, bf16[16,128,256]{2,1,0:T(8,128)(2,1)S(1)}) custom-call(s32[1]{0:T(128)} %bitcast.core, bf16[192,128]{1,0:T(8,128)(2,1)S(1)} %copy-done.3, bf16[192,8192]{1,0:T(8,128)(2,1)S(1)} %copy-done.1, s32[64,128]{1,0:T(8,128)S(1)} %bitcast.18), custom_call_target="tpu_custom_call" | custom-call | flops 1048576 | bytes 65536 | tf_op jit(solution)/shard_map/local_grads/pallas_call | solution.py:44
  23.0 0.0 collective-permute-done
  23.0 1.9 %collective-permute-start.1 = (bf16[16,128,256]{2,1,0:T(8,128)(2,1)S(1)}, bf16[16,128,256]{2,1,0:T(8,128)(2,1)S(1)}, u32[]{:S(2)}, u32[]{:S(2)}) collective-permute-start(bf16[16,128,256]{2,1,0:T(8,128)(2,1)S(1)} %get-tuple-element.10), channel_id=1, source_target_pairs={{0,1},{1,0},{2,3},{3,2},{4,5},{5,4},{6,7},{7,6},{8,9},{9,8},{10,11... | collective-permute-start | bytes 3145736 | tf_op jit(solution)/shard_map/ppermute | solution.py:127
  24.9 2.6 %collective-permute-done.1.got = bf16[16,128,256]{2,1,0:T(8,128)(2,1)S(1)} collective-permute-done((bf16[16,128,256]{2,1,0:T(8,128)(2,1)S(1)}, bf16[16,128,256]{2,1,0:T(8,128)(2,1)S(1)}, u32[]{:S(2)}, u32[]{:S(2)}) %collective-permute-start.1) | collective-permute-done | bytes 1048608 | tf_op jit(solution)/shard_map/ppermute | solution.py:127
  27.6 1.7 %paired.1 = bf16[16,128,256]{2,1,0:T(8,128)(2,1)} custom-call(bf16[16,128,256]{2,1,0:T(8,128)(2,1)S(1)} %get-tuple-element.8.own, bf16[16,128,256]{2,1,0:T(8,128)(2,1)S(1)} %collective-permute-done.1.got), custom_call_target="tpu_custom_call" | custom-call | flops 1048576 | bytes 3145728 | tf_op jit(solution)/shard_map/paired/pallas_call | solution.py:70
  29.2 0.0 copy-start.5
  29.2 10.2 %all-to-all-start = ((bf16[4,4,128,256]{3,2,1,0:T(8,128)(2,1)}), bf16[4,4,128,256]{3,2,1,0:T(8,128)(2,1)}, u32[]{:S(2)}, u32[]{:S(2)}) async-start(bf16[4,4,128,256]{3,2,1,0:T(8,128)(2,1)} %bitcast.6), calls=%async_computation | async-start | bytes 2097152 | tf_op jit(solution)/shard_map/all_to_all | solution.py:135
  39.5 0.0 copy-start.2
  39.5 10.9 %collective-permute-start.2 = (bf16[2,32,256]{2,1,0:T(8,128)(2,1)S(1)}, bf16[2,32,256]{2,1,0:T(8,128)(2,1)S(1)}, u32[]{:S(2)}, u32[]{:S(2)}) collective-permute-start(bf16[2,32,256]{2,1,0:T(8,128)(2,1)S(1)} %pad_maximum_fusion.3), channel_id=1, source_target_pairs={{0,6},{2,4},{4,2},{6,0},{1,7},{3,5},{5,3},{7,1},{8,14},{10,12},{12... | collective-permute-start | bytes 98312 | tf_op jit(solution)/shard_map/ppermute | solution.py:122
  50.4 5.6 %collective-permute-done.2 = bf16[2,32,256]{2,1,0:T(8,128)(2,1)S(1)} collective-permute-done((bf16[2,32,256]{2,1,0:T(8,128)(2,1)S(1)}, bf16[2,32,256]{2,1,0:T(8,128)(2,1)S(1)}, u32[]{:S(2)}, u32[]{:S(2)}) %collective-permute-start.2) | collective-permute-done | bytes 32800 | tf_op jit(solution)/shard_map/ppermute | solution.py:122
  56.0 0.0 all-to-all-done
  56.0 2.2 %reduce_sum.32 = bf16[4,128,256]{2,1,0:T(8,128)(2,1)} reduce(bf16[4,4,128,256]{3,2,1,0:T(8,128)(2,1)} %all-to-all-done, bf16[]{:T(256)} %constant.26.clone.1), dimensions={0}, to_apply=%region_0.0 | reduce | flops 393216 | bytes 1310722 | tf_op jit(solution)/shard_map/reduce_sum | solution.py:143
  58.2 14.2 %all-to-all-start.1 = ((bf16[4,128,256]{2,1,0:T(8,128)(2,1)}), bf16[4,128,256]{2,1,0:T(8,128)(2,1)S(1)}, u32[]{:S(2)}, u32[]{:S(2)}) async-start(bf16[4,128,256]{2,1,0:T(8,128)(2,1)} %reduce_sum.32), calls=%async_computation.1 | async-start | bytes 524288 | tf_op jit(solution)/shard_map/all_to_all | solution.py:135
  72.4 3.4 %collective-permute-start.5 = (bf16[4,32,256]{2,1,0:T(8,128)(2,1)S(1)}, bf16[4,32,256]{2,1,0:T(8,128)(2,1)S(1)}, u32[]{:S(2)}, u32[]{:S(2)}) collective-permute-start(bf16[4,32,256]{2,1,0:T(8,128)(2,1)S(1)} %pad_maximum_fusion.2), channel_id=1, source_target_pairs={{0,8},{8,16},{16,24},{24,0},{1,9},{9,17},{17,25},{25,1},{2,10},{10... | collective-permute-start | bytes 196616 | tf_op jit(solution)/shard_map/ppermute | solution.py:127
  75.8 3.2 %collective-permute-start.4 = (bf16[4,32,256]{2,1,0:T(8,128)(2,1)S(1)}, bf16[4,32,256]{2,1,0:T(8,128)(2,1)S(1)}, u32[]{:S(2)}, u32[]{:S(2)}) collective-permute-start(bf16[4,32,256]{2,1,0:T(8,128)(2,1)S(1)} %pad_maximum_fusion.2), channel_id=1, source_target_pairs={{0,16},{8,24},{16,0},{24,8},{1,17},{9,25},{17,1},{25,9},{2,18},{10... | collective-permute-start | bytes 196616 | tf_op jit(solution)/shard_map/ppermute | solution.py:127
  79.0 3.9 %collective-permute-start.3 = (bf16[4,32,256]{2,1,0:T(8,128)(2,1)S(1)}, bf16[4,32,256]{2,1,0:T(8,128)(2,1)S(1)}, u32[]{:S(2)}, u32[]{:S(2)}) collective-permute-start(bf16[4,32,256]{2,1,0:T(8,128)(2,1)S(1)} %pad_maximum_fusion.2), channel_id=1, source_target_pairs={{0,24},{8,0},{16,8},{24,16},{1,25},{9,1},{17,9},{25,17},{2,26},{10... | collective-permute-start | bytes 196616 | tf_op jit(solution)/shard_map/ppermute | solution.py:127
  82.8 0.0 collective-permute-done.5
  82.8 0.6 collective-permute-done.4
  83.4 1.7 %collective-permute-done.3 = bf16[4,32,256]{2,1,0:T(8,128)(2,1)S(1)} collective-permute-done((bf16[4,32,256]{2,1,0:T(8,128)(2,1)S(1)}, bf16[4,32,256]{2,1,0:T(8,128)(2,1)S(1)}, u32[]{:S(2)}, u32[]{:S(2)}) %collective-permute-start.3) | collective-permute-done | bytes 65568 | tf_op jit(solution)/shard_map/ppermute | solution.py:127
  85.2 3.4 %collective-permute-start.8 = (bf16[4,4,32,256]{3,2,1,0:T(8,128)(2,1)S(1)}, bf16[4,4,32,256]{3,2,1,0:T(8,128)(2,1)S(1)}, u32[]{:S(2)}, u32[]{:S(2)}) collective-permute-start(bf16[4,4,32,256]{3,2,1,0:T(8,128)(2,1)S(1)} %get-tuple-element.15), channel_id=1, source_target_pairs={{0,256},{256,512},{512,768},{768,0},{1,257},{257,513},{513,769},{7... | collective-permute-start | bytes 786440 | tf_op jit(solution)/shard_map/ppermute | solution.py:127
  88.6 4.6 %collective-permute-start.7 = (bf16[4,4,32,256]{3,2,1,0:T(8,128)(2,1)S(1)}, bf16[4,4,32,256]{3,2,1,0:T(8,128)(2,1)S(1)}, u32[]{:S(2)}, u32[]{:S(2)}) collective-permute-start(bf16[4,4,32,256]{3,2,1,0:T(8,128)(2,1)S(1)} %get-tuple-element.15), channel_id=1, source_target_pairs={{0,512},{256,768},{512,0},{768,256},{1,513},{257,769},{513,1},{769... | collective-permute-start | bytes 786440 | tf_op jit(solution)/shard_map/ppermute | solution.py:127
  93.2 3.3 %collective-permute-start.6 = (bf16[4,4,32,256]{3,2,1,0:T(8,128)(2,1)S(1)}, bf16[4,4,32,256]{3,2,1,0:T(8,128)(2,1)S(1)}, u32[]{:S(2)}, u32[]{:S(2)}) collective-permute-start(bf16[4,4,32,256]{3,2,1,0:T(8,128)(2,1)S(1)} %get-tuple-element.15), channel_id=1, source_target_pairs={{0,768},{256,0},{512,256},{768,512},{1,769},{257,1},{513,257},{769... | collective-permute-start | bytes 786440 | tf_op jit(solution)/shard_map/ppermute | solution.py:127
  96.6 0.9 collective-permute-done.8
  97.5 2.9 %collective-permute-done.7 = bf16[4,4,32,256]{3,2,1,0:T(8,128)(2,1)S(1)} collective-permute-done((bf16[4,4,32,256]{3,2,1,0:T(8,128)(2,1)S(1)}, bf16[4,4,32,256]{3,2,1,0:T(8,128)(2,1)S(1)}, u32[]{:S(2)}, u32[]{:S(2)}) %collective-permute-start.7) | collective-permute-done | bytes 262176 | tf_op jit(solution)/shard_map/ppermute | solution.py:127
  100.4 2.5 %collective-permute-done.6 = bf16[4,4,32,256]{3,2,1,0:T(8,128)(2,1)S(1)} collective-permute-done((bf16[4,4,32,256]{3,2,1,0:T(8,128)(2,1)S(1)}, bf16[4,4,32,256]{3,2,1,0:T(8,128)(2,1)S(1)}, u32[]{:S(2)}, u32[]{:S(2)}) %collective-permute-start.6) | collective-permute-done | bytes 262176 | tf_op jit(solution)/shard_map/ppermute | solution.py:127
  102.9 1.1 pad_maximum_fusion.own
  104.0 1.9 %collective-permute-start.9 = (bf16[4,4,4,32,256]{4,3,2,1,0:T(8,128)(2,1)}, bf16[4,4,4,32,256]{4,3,2,1,0:T(8,128)(2,1)}, u32[]{:S(2)}, u32[]{:S(2)}) collective-permute-start(bf16[4,4,4,32,256]{4,3,2,1,0:T(8,128)(2,1)} %pad_maximum_fusion.own), channel_id=1, source_target_pairs={{0,1},{1,0},{2,3},{3,2},{4,5},{5,4},{6,7},{7,6},{8,9},{9,8},{10,11... | collective-permute-start | bytes 3145736 | tf_op jit(solution)/shard_map/ppermute | solution.py:127
  105.9 0.0 copy-done.5
  106.0 0.1 copy.19
  106.1 0.9 broadcast_in_dim.4
  106.9 1.7 %reshape.14 = f32[32,4,256]{2,1,0:T(4,128)} reshape(f32[128,2,128]{2,1,0:T(2,128)} %broadcast_in_dim.4) | data formatting | bytes 262144 | tf_op jit(solution)/shard_map/reshape | solution.py:161
  108.6 0.0 all-to-all-done.1
  108.7 1.6 %minimum_convert_fusion = bf16[32,4,256]{2,1,0:T(4,128)(2,1)} fusion(f32[32,4,256]{2,1,0:T(4,128)} %reshape.14, bf16[32,4,256]{2,1,0:T(4,128)(2,1)S(1)} %reduce_sum.34), kind=kLoop, calls=%fused_computation.4 | loop fusion | flops 163840 | bytes 262144 | tf_op jit(solution)/shard_map/convert_element_type | solution.py:162
  110.2 11.7 %all-to-all-start.2 = ((bf16[32,4,256]{2,1,0:T(4,128)(2,1)}), bf16[32,4,256]{2,1,0:T(4,128)(2,1)S(1)}, u32[]{:S(2)}, u32[]{:S(2)}) async-start(bf16[32,4,256]{2,1,0:T(4,128)(2,1)} %minimum_convert_fusion), calls=%async_computation.2 | async-start | bytes 131072 | tf_op jit(solution)/shard_map/all_to_all | solution.py:135
  122.0 0.1 pad_add_fusion.pos
  122.0 0.0 collective-permute-done.9.oth
  122.0 0.0 copy-done.2
  122.0 4.7 %hidden_grads.1 = bf16[192,128]{1,0:T(8,128)(2,1)} custom-call(s32[4]{0:T(128)S(1)} %pad_add_fusion.pos, bf16[192,8192]{1,0:T(8,128)(2,1)S(1)} %copy-done.2, bf16[4,4,4,32,256]{4,3,2,1,0:T(8,128)(2,1)} %pad_maximum_fusion.own, bf16[4,4,4,32,256]{4,3,2,1,0:T(8,128)(2,1)} %collective-permute-done.9.oth), custom_call_target="tpu_custom_call" | custom-call | flops 402653184 | bytes 5242880 | tf_op jit(solution)/shard_map/hidden_grads/pallas_call | solution.py:105
  126.7 7.8 %all-to-all-done.2 = bf16[32,4,256]{2,1,0:T(4,128)(2,1)S(1)} async-done(((bf16[32,4,256]{2,1,0:T(4,128)(2,1)}), bf16[32,4,256]{2,1,0:T(4,128)(2,1)S(1)}, u32[]{:S(2)}, u32[]{:S(2)}) %all-to-all-start.2) | async-done | bytes 65568 | tf_op jit(solution)/shard_map/all_to_all | solution.py:135
  134.6 0.6 convert_reduce_fusion.1
  (8 shorter events, 0.1 us)
Async XLA Ops:
  0.6 0.8 copy-start
  1.5 21.5 %collective-permute-start = (bf16[32,256]{1,0:T(8,128)(2,1)S(1)}, bf16[32,256]{1,0:T(8,128)(2,1)S(1)}, u32[]{:S(2)}, u32[]{:S(2)}) collective-permute-start(bf16[32,256]{1,0:T(8,128)(2,1)S(1)} %constant_dynamic-slice_fusion), channel_id=1, source_target_pairs={{0,2},{2,0},{4,6},{6,4},{1,3},{3,1},{5,7},{7,5},{8,10},{10,8},{12,... | collective-permute-start | bytes 49160 | tf_op jit(solution)/shard_map/ppermute | solution.py:122
  17.2 1.9 %copy-start.1 = (bf16[192,8192]{1,0:T(8,128)(2,1)S(1)}, bf16[192,8192]{1,0:T(8,128)(2,1)}, u32[]{:S(2)}) copy-start(bf16[192,8192]{1,0:T(8,128)(2,1)} %og.3) | copy-start | bytes 9437188
  19.1 0.8 copy-start.3
  19.9 0.8 copy-start.4
  23.0 4.6 %collective-permute-start.1 = (bf16[16,128,256]{2,1,0:T(8,128)(2,1)S(1)}, bf16[16,128,256]{2,1,0:T(8,128)(2,1)S(1)}, u32[]{:S(2)}, u32[]{:S(2)}) collective-permute-start(bf16[16,128,256]{2,1,0:T(8,128)(2,1)S(1)} %get-tuple-element.10), channel_id=1, source_target_pairs={{0,1},{1,0},{2,3},{3,2},{4,5},{5,4},{6,7},{7,6},{8,9},{9,8},{10,11... | collective-permute-start | bytes 3145736 | tf_op jit(solution)/shard_map/ppermute | solution.py:127
  29.2 76.7 %copy-start.5 = (s32[128,2]{0,1:T(2,128)S(1)}, s32[128,2]{0,1:T(2,128)}, u32[]{:S(2)}) copy-start(s32[128,2]{0,1:T(2,128)} %param.9) | copy-start | bytes 3076
  29.2 26.8 %all-to-all-start = ((bf16[4,4,128,256]{3,2,1,0:T(8,128)(2,1)}), bf16[4,4,128,256]{3,2,1,0:T(8,128)(2,1)}, u32[]{:S(2)}, u32[]{:S(2)}) async-start(bf16[4,4,128,256]{3,2,1,0:T(8,128)(2,1)} %bitcast.6), calls=%async_computation | async-start | bytes 2097152 | tf_op jit(solution)/shard_map/all_to_all | solution.py:135
  39.5 82.6 %copy-start.2 = (bf16[192,8192]{1,0:T(8,128)(2,1)S(1)}, bf16[192,8192]{1,0:T(8,128)(2,1)}, u32[]{:S(2)}) copy-start(bf16[192,8192]{1,0:T(8,128)(2,1)} %og.3) | copy-start | bytes 9437188
  39.5 16.5 %collective-permute-start.2 = (bf16[2,32,256]{2,1,0:T(8,128)(2,1)S(1)}, bf16[2,32,256]{2,1,0:T(8,128)(2,1)S(1)}, u32[]{:S(2)}, u32[]{:S(2)}) collective-permute-start(bf16[2,32,256]{2,1,0:T(8,128)(2,1)S(1)} %pad_maximum_fusion.3), channel_id=1, source_target_pairs={{0,6},{2,4},{4,2},{6,0},{1,7},{3,5},{5,3},{7,1},{8,14},{10,12},{12... | collective-permute-start | bytes 98312 | tf_op jit(solution)/shard_map/ppermute | solution.py:122
  58.2 50.4 %all-to-all-start.1 = ((bf16[4,128,256]{2,1,0:T(8,128)(2,1)}), bf16[4,128,256]{2,1,0:T(8,128)(2,1)S(1)}, u32[]{:S(2)}, u32[]{:S(2)}) async-start(bf16[4,128,256]{2,1,0:T(8,128)(2,1)} %reduce_sum.32), calls=%async_computation.1 | async-start | bytes 524288 | tf_op jit(solution)/shard_map/all_to_all | solution.py:135
  72.4 10.4 %collective-permute-start.5 = (bf16[4,32,256]{2,1,0:T(8,128)(2,1)S(1)}, bf16[4,32,256]{2,1,0:T(8,128)(2,1)S(1)}, u32[]{:S(2)}, u32[]{:S(2)}) collective-permute-start(bf16[4,32,256]{2,1,0:T(8,128)(2,1)S(1)} %pad_maximum_fusion.2), channel_id=1, source_target_pairs={{0,8},{8,16},{16,24},{24,0},{1,9},{9,17},{17,25},{25,1},{2,10},{10... | collective-permute-start | bytes 196616 | tf_op jit(solution)/shard_map/ppermute | solution.py:127
  75.8 7.7 %collective-permute-start.4 = (bf16[4,32,256]{2,1,0:T(8,128)(2,1)S(1)}, bf16[4,32,256]{2,1,0:T(8,128)(2,1)S(1)}, u32[]{:S(2)}, u32[]{:S(2)}) collective-permute-start(bf16[4,32,256]{2,1,0:T(8,128)(2,1)S(1)} %pad_maximum_fusion.2), channel_id=1, source_target_pairs={{0,16},{8,24},{16,0},{24,8},{1,17},{9,25},{17,1},{25,9},{2,18},{10... | collective-permute-start | bytes 196616 | tf_op jit(solution)/shard_map/ppermute | solution.py:127
  79.0 6.2 %collective-permute-start.3 = (bf16[4,32,256]{2,1,0:T(8,128)(2,1)S(1)}, bf16[4,32,256]{2,1,0:T(8,128)(2,1)S(1)}, u32[]{:S(2)}, u32[]{:S(2)}) collective-permute-start(bf16[4,32,256]{2,1,0:T(8,128)(2,1)S(1)} %pad_maximum_fusion.2), channel_id=1, source_target_pairs={{0,24},{8,0},{16,8},{24,16},{1,25},{9,1},{17,9},{25,17},{2,26},{10... | collective-permute-start | bytes 196616 | tf_op jit(solution)/shard_map/ppermute | solution.py:127
  85.2 12.3 %collective-permute-start.8 = (bf16[4,4,32,256]{3,2,1,0:T(8,128)(2,1)S(1)}, bf16[4,4,32,256]{3,2,1,0:T(8,128)(2,1)S(1)}, u32[]{:S(2)}, u32[]{:S(2)}) collective-permute-start(bf16[4,4,32,256]{3,2,1,0:T(8,128)(2,1)S(1)} %get-tuple-element.15), channel_id=1, source_target_pairs={{0,256},{256,512},{512,768},{768,0},{1,257},{257,513},{513,769},{7... | collective-permute-start | bytes 786440 | tf_op jit(solution)/shard_map/ppermute | solution.py:127
  88.6 11.8 %collective-permute-start.7 = (bf16[4,4,32,256]{3,2,1,0:T(8,128)(2,1)S(1)}, bf16[4,4,32,256]{3,2,1,0:T(8,128)(2,1)S(1)}, u32[]{:S(2)}, u32[]{:S(2)}) collective-permute-start(bf16[4,4,32,256]{3,2,1,0:T(8,128)(2,1)S(1)} %get-tuple-element.15), channel_id=1, source_target_pairs={{0,512},{256,768},{512,0},{768,256},{1,513},{257,769},{513,1},{769... | collective-permute-start | bytes 786440 | tf_op jit(solution)/shard_map/ppermute | solution.py:127
  93.2 9.7 %collective-permute-start.6 = (bf16[4,4,32,256]{3,2,1,0:T(8,128)(2,1)S(1)}, bf16[4,4,32,256]{3,2,1,0:T(8,128)(2,1)S(1)}, u32[]{:S(2)}, u32[]{:S(2)}) collective-permute-start(bf16[4,4,32,256]{3,2,1,0:T(8,128)(2,1)S(1)} %get-tuple-element.15), channel_id=1, source_target_pairs={{0,768},{256,0},{512,256},{768,512},{1,769},{257,1},{513,257},{769... | collective-permute-start | bytes 786440 | tf_op jit(solution)/shard_map/ppermute | solution.py:127
  104.0 18.0 %collective-permute-start.9 = (bf16[4,4,4,32,256]{4,3,2,1,0:T(8,128)(2,1)}, bf16[4,4,4,32,256]{4,3,2,1,0:T(8,128)(2,1)}, u32[]{:S(2)}, u32[]{:S(2)}) collective-permute-start(bf16[4,4,4,32,256]{4,3,2,1,0:T(8,128)(2,1)} %pad_maximum_fusion.own), channel_id=1, source_target_pairs={{0,1},{1,0},{2,3},{3,2},{4,5},{5,4},{6,7},{7,6},{8,9},{9,8},{10,11... | collective-permute-start | bytes 3145736 | tf_op jit(solution)/shard_map/ppermute | solution.py:127
  110.2 24.4 %all-to-all-start.2 = ((bf16[32,4,256]{2,1,0:T(4,128)(2,1)}), bf16[32,4,256]{2,1,0:T(4,128)(2,1)S(1)}, u32[]{:S(2)}, u32[]{:S(2)}) async-start(bf16[32,4,256]{2,1,0:T(4,128)(2,1)} %minimum_convert_fusion), calls=%async_computation.2 | async-start | bytes 131072 | tf_op jit(solution)/shard_map/all_to_all | solution.py:135

commit v6 on v5

--- a/solution.py
+++ b/solution.py
@@ -90,7 +90,7 @@
     acc = total[...]
     for k, bits in enumerate(ORDER):
         for core, part in ((c, own), (1 - c, oth)):
-            rows = part[:, 0, k].reshape(128, 256)
+            rows = part[0, :, k].reshape(128, 256)
             at = pl.multiple_of(512 * jnp.bitwise_xor(zh, bits) + core * 256, 256)
             acc += lax.dot_general(og[:, pl.ds(at, 256)], rows, (((1,), (1,)), ((), ())), preferred_element_type=F32)
     total[...] = acc
@@ -101,7 +101,7 @@
 
 
 def hidden_grads(pos, out_grad, own, oth):
-    part = pl.BlockSpec((4, 1, 4, 32, 256), lambda k, pos: (0, k, 0, 0, 0))
+    part = pl.BlockSpec((1, 4, 4, 32, 256), lambda k, pos: (k, 0, 0, 0, 0))
     return pl.pallas_call(
         hidden_kernel,
         grid_spec=pltpu.PrefetchScalarGridSpec(
@@ -118,6 +118,42 @@
     )(pos, out_grad, own, oth)
 
 
+def line_kernel(parts, out):
+    out[0] = parts[:, 0].astype(F32).sum(0).astype(BF16)
+
+
+def lined(parts):
+    return pl.pallas_call(
+        line_kernel,
+        grid=(4,),
+        in_specs=[pl.BlockSpec((4, 1, 128, 256), lambda zh: (0, zh, 0, 0))],
+        out_specs=pl.BlockSpec((1, 128, 256), lambda zh: (zh, 0, 0)),
+        out_shape=jax.ShapeDtypeStruct((4, 128, 256), BF16),
+        compiler_params=pltpu.CompilerParams(vmem_limit_bytes=VMEM),
+        cost_estimate=pl.CostEstimate(flops=1 << 19, bytes_accessed=5 << 18, transcendentals=0),
+        name="lined",
+    )(parts)
+
+
+def again_kernel(parts, exponent, out):
+    bound = limits(exponent[...]).T
+    for half in range(2):
+        lanes = slice(128 * half, 128 * half + 128)
+        group = parts[:, :, lanes].astype(F32).sum(0)
+        most = bound[:, half : half + 1]
+        out[:, lanes] = jnp.clip(group, -most, most).astype(BF16)
+
+
+def requantized(parts, exponent):
+    return pl.pallas_call(
+        again_kernel,
+        out_shape=jax.ShapeDtypeStruct((128, 256), BF16),
+        compiler_params=pltpu.CompilerParams(vmem_limit_bytes=VMEM),
+        cost_estimate=pl.CostEstimate(flops=1 << 17, bytes_accessed=5 << 16, transcendentals=0),
+        name="requantized",
+    )(parts, exponent)
+
+
 def exchanged(value, axis, bits):
     return lax.ppermute(value, axis, [(i, i ^ bits) for i in range(SIZES[axis])])
 
@@ -127,8 +163,8 @@
     return lax.ppermute(value, axis, [(i, (i - k) % n) for i in range(n)])
 
 
-def gather(value, axis):
-    return jnp.stack([value] + [shifted(value, axis, k) for k in (1, 2, 3)])
+def pieces(value, axis):
+    return [value] + [shifted(value, axis, k) for k in (1, 2, 3)]
 
 
 def swap(value, axes):
@@ -152,21 +188,18 @@
     got = shifted(after(oth, near), "c", 1)
     pairs = paired(own, got)
     columns = swap(pairs, "y")
-    line = summed(columns).astype(BF16)
-
     two = jnp.stack([mine, after(near, pairs)])
     quarter = jnp.concatenate([two, exchanged(two, "zh", 3)])
 
-    group = summed(swap(after(line, quarter), "zh"))
-    limit = jnp.repeat(limits(e2), 128, axis=1)
-    again = jnp.clip(group, -limit, limit).astype(BF16)
+    line = lined(columns)
+    again = requantized(swap(after(line, quarter), "zh"), e2.T)
     rows = swap(again.reshape(N_OUTER, -1, 256), OUTER)
-    weight_grad = summed(rows)
-
-    part = gather(gather(after(quarter, line), "y"), "x")
+
+    part = jnp.stack(pieces(after(quarter, line), "x"))
+    part = jnp.stack([after(piece, again) for piece in pieces(part, "y")])
     pos = jnp.stack([c, x, y, zh])
     hidden_grad = hidden_grads(pos, out_grad, part, shifted(part, "c", 1))
-    return hidden_grad, weight_grad
+    return hidden_grad, summed(after(rows, hidden_grad))
 
 
 def solution(mesh):

time: 136 us -> 141 us (1.037)
  the two profiles are of different devices: /device:TPU:8 before, /device:TPU:1 now
where the time goes in v6:
time: 141 us
  starting transfers between devices  96.3 us (68%)
  waiting for transfers between devices  22.5 us (16%)
  Pallas kernels  12.2 us (9%)
  local copies, waits for them, and re-layouts  4.95 us (4%)
  other arithmetic  3.8 us (3%)
    all_to_all x3, starting transfers between devices, swap(): return lax.all_to_all(value, axes, 0, 0, tiled=True)  35.3 us
    ppermute x8, starting transfers between devices, shifted(): return lax.ppermute(value, axis, [(i, (i - k) % n) for i in range(n)])  34.4 us
    ppermute x2, starting transfers between devices, exchanged(): lax.ppermute(value, axis, [(i, i ^ bits) for i in range(SIZES[axis])])  26.6 us
    ppermute x8, waiting for transfers between devices, shifted(): return lax.ppermute(value, axis, [(i, (i - k) % n) for i in range(n)])  11.2 us
    all_to_all x3, waiting for transfers between devices, swap(): return lax.all_to_all(value, axes, 0, 0, tiled=True)  7.94 us
    pallas_call x1, Pallas kernels, hidden_grads(): pl.pallas_call(hidden_kernel, grid_spec=pltpu.PrefetchScalarGridSpec(num_...  4.69 us
    unnamed x12, local copies, waits for them, and re-layouts  4.28 us
    ppermute x2, waiting for transfers between devices, exchanged(): lax.ppermute(value, axis, [(i, i ^ bits) for i in range(SIZES[axis])])  3.39 us
  transfers between devices with their start and end apart: 13, of which 7 were waited for; matrix products, arithmetic and copies ran while one was open for 1% of the time, Pallas kernels for 5%

profile of v6, /device:TPU:1, one launch (start us, length us, event | category | flops | bytes accessed | tf_op | source)
XLA Modules:
  0.0 140.6 jit_solution(10504915400601263053)
XLA Ops:
  0.6 0.0 copy-start
  0.7 0.8 copy-done
  1.5 16.3 %collective-permute-start = (bf16[32,256]{1,0:T(8,128)(2,1)S(1)}, bf16[32,256]{1,0:T(8,128)(2,1)S(1)}, u32[]{:S(2)}, u32[]{:S(2)}) collective-permute-start(bf16[32,256]{1,0:T(8,128)(2,1)S(1)} %constant_dynamic-slice_fusion), channel_id=1, source_target_pairs={{0,2},{2,0},{4,6},{6,4},{1,3},{3,1},{5,7},{7,5},{8,10},{10,8},{12,... | collective-permute-start | bytes 49160 | tf_op jit(solution)/shard_map/ppermute | solution.py:158
  17.7 0.0 copy-start.1
  17.8 1.9 %copy-done.1 = bf16[192,8192]{1,0:T(8,128)(2,1)S(1)} copy-done((bf16[192,8192]{1,0:T(8,128)(2,1)S(1)}, bf16[192,8192]{1,0:T(8,128)(2,1)}, u32[]{:S(2)}) %copy-start.1) | copy-done | bytes 3145752
  19.6 0.0 copy-start.3
  19.6 0.8 copy-done.3
  20.4 0.0 copy-start.4
  20.4 0.8 copy-done.4
  21.2 2.3 %local_grads.1 = (bf16[16,128,256]{2,1,0:T(8,128)(2,1)S(1)}, bf16[16,128,256]{2,1,0:T(8,128)(2,1)S(1)}) custom-call(s32[1]{0:T(128)} %bitcast.core, bf16[192,128]{1,0:T(8,128)(2,1)S(1)} %copy-done.3, bf16[192,8192]{1,0:T(8,128)(2,1)S(1)} %copy-done.1, s32[64,128]{1,0:T(8,128)S(1)} %bitcast.18), custom_call_target="tpu_custom_call" | custom-call | flops 1048576 | bytes 65536 | tf_op jit(solution)/shard_map/local_grads/pallas_call | solution.py:44
  23.6 0.0 collective-permute-done
  23.6 8.3 %collective-permute-start.1 = (bf16[16,128,256]{2,1,0:T(8,128)(2,1)S(1)}, bf16[16,128,256]{2,1,0:T(8,128)(2,1)S(1)}, u32[]{:S(2)}, u32[]{:S(2)}) collective-permute-start(bf16[16,128,256]{2,1,0:T(8,128)(2,1)S(1)} %get-tuple-element.15), channel_id=1, source_target_pairs={{0,1},{1,0},{2,3},{3,2},{4,5},{5,4},{6,7},{7,6},{8,9},{9,8},{10,11... | collective-permute-start | bytes 3145736 | tf_op jit(solution)/shard_map/ppermute | solution.py:163
  31.9 2.3 %collective-permute-done.1.got = bf16[16,128,256]{2,1,0:T(8,128)(2,1)S(1)} collective-permute-done((bf16[16,128,256]{2,1,0:T(8,128)(2,1)S(1)}, bf16[16,128,256]{2,1,0:T(8,128)(2,1)S(1)}, u32[]{:S(2)}, u32[]{:S(2)}) %collective-permute-start.1) | collective-permute-done | bytes 1048608 | tf_op jit(solution)/shard_map/ppermute | solution.py:163
  34.1 0.0 copy-start.5
  34.1 1.7 %paired.1 = bf16[16,128,256]{2,1,0:T(8,128)(2,1)} custom-call(bf16[16,128,256]{2,1,0:T(8,128)(2,1)S(1)} %get-tuple-element.13.own, bf16[16,128,256]{2,1,0:T(8,128)(2,1)S(1)} %collective-permute-done.1.got), custom_call_target="tpu_custom_call" | custom-call | flops 1048576 | bytes 3145728 | tf_op jit(solution)/shard_map/paired/pallas_call | solution.py:70
  35.8 4.2 %all-to-all-start = ((bf16[4,4,128,256]{3,2,1,0:T(8,128)(2,1)}), bf16[4,4,128,256]{3,2,1,0:T(8,128)(2,1)}, u32[]{:S(2)}, u32[]{:S(2)}) async-start(bf16[4,4,128,256]{3,2,1,0:T(8,128)(2,1)} %bitcast.6), calls=%async_computation | async-start | bytes 2097152 | tf_op jit(solution)/shard_map/all_to_all | solution.py:171
  40.1 0.0 copy-start.2
  40.1 10.3 %collective-permute-start.2 = (bf16[2,32,256]{2,1,0:T(8,128)(2,1)S(1)}, bf16[2,32,256]{2,1,0:T(8,128)(2,1)S(1)}, u32[]{:S(2)}, u32[]{:S(2)}) collective-permute-start(bf16[2,32,256]{2,1,0:T(8,128)(2,1)S(1)} %pad_maximum_fusion.3), channel_id=1, source_target_pairs={{0,6},{2,4},{4,2},{6,0},{1,7},{3,5},{5,3},{7,1},{8,14},{10,12},{12... | collective-permute-start | bytes 98312 | tf_op jit(solution)/shard_map/ppermute | solution.py:158
  50.4 3.4 %collective-permute-done.2 = bf16[2,32,256]{2,1,0:T(8,128)(2,1)S(1)} collective-permute-done((bf16[2,32,256]{2,1,0:T(8,128)(2,1)S(1)}, bf16[2,32,256]{2,1,0:T(8,128)(2,1)S(1)}, u32[]{:S(2)}, u32[]{:S(2)}) %collective-permute-start.2) | collective-permute-done | bytes 32800 | tf_op jit(solution)/shard_map/ppermute | solution.py:158
  53.8 1.1 all-to-all-done.parts
  55.0 3.2 %lined.1 = bf16[4,128,256]{2,1,0:T(8,128)(2,1)} custom-call(bf16[4,4,128,256]{3,2,1,0:T(8,128)(2,1)} %all-to-all-done.parts), custom_call_target="tpu_custom_call" | custom-call | flops 524288 | bytes 1310720 | tf_op jit(solution)/shard_map/lined/pallas_call | solution.py:126
  58.2 15.1 %all-to-all-start.1 = ((bf16[4,128,256]{2,1,0:T(8,128)(2,1)}), bf16[4,128,256]{2,1,0:T(8,128)(2,1)S(1)}, u32[]{:S(2)}, u32[]{:S(2)}) async-start(bf16[4,128,256]{2,1,0:T(8,128)(2,1)} %lined.1), calls=%async_computation.1 | async-start | bytes 524288 | tf_op jit(solution)/shard_map/all_to_all | solution.py:171
  73.3 3.1 %collective-permute-start.5 = (bf16[4,32,256]{2,1,0:T(8,128)(2,1)S(1)}, bf16[4,32,256]{2,1,0:T(8,128)(2,1)S(1)}, u32[]{:S(2)}, u32[]{:S(2)}) collective-permute-start(bf16[4,32,256]{2,1,0:T(8,128)(2,1)S(1)} %pad_maximum_fusion.2), channel_id=1, source_target_pairs={{0,256},{256,512},{512,768},{768,0},{1,257},{257,513},{513,769},{7... | collective-permute-start | bytes 196616 | tf_op jit(solution)/shard_map/ppermute | solution.py:163
  76.4 4.4 %collective-permute-start.4 = (bf16[4,32,256]{2,1,0:T(8,128)(2,1)S(1)}, bf16[4,32,256]{2,1,0:T(8,128)(2,1)S(1)}, u32[]{:S(2)}, u32[]{:S(2)}) collective-permute-start(bf16[4,32,256]{2,1,0:T(8,128)(2,1)S(1)} %pad_maximum_fusion.2), channel_id=1, source_target_pairs={{0,512},{256,768},{512,0},{768,256},{1,513},{257,769},{513,1},{769... | collective-permute-start | bytes 196616 | tf_op jit(solution)/shard_map/ppermute | solution.py:163
  80.8 3.1 %collective-permute-start.3 = (bf16[4,32,256]{2,1,0:T(8,128)(2,1)S(1)}, bf16[4,32,256]{2,1,0:T(8,128)(2,1)S(1)}, u32[]{:S(2)}, u32[]{:S(2)}) collective-permute-start(bf16[4,32,256]{2,1,0:T(8,128)(2,1)S(1)} %pad_maximum_fusion.2), channel_id=1, source_target_pairs={{0,768},{256,0},{512,256},{768,512},{1,769},{257,1},{513,257},{769... | collective-permute-start | bytes 196616 | tf_op jit(solution)/shard_map/ppermute | solution.py:163
  83.9 0.0 collective-permute-done.5
  83.9 0.0 collective-permute-done.4
  83.9 2.2 %collective-permute-done.3 = bf16[4,32,256]{2,1,0:T(8,128)(2,1)S(1)} collective-permute-done((bf16[4,32,256]{2,1,0:T(8,128)(2,1)S(1)}, bf16[4,32,256]{2,1,0:T(8,128)(2,1)S(1)}, u32[]{:S(2)}, u32[]{:S(2)}) %collective-permute-start.3) | collective-permute-done | bytes 65568 | tf_op jit(solution)/shard_map/ppermute | solution.py:163
  86.1 0.8 pad_maximum_fusion.1
  86.9 2.4 %collective-permute-start.8 = (bf16[4,4,32,256]{3,2,1,0:T(8,128)(2,1)}, bf16[4,4,32,256]{3,2,1,0:T(8,128)(2,1)}, u32[]{:S(2)}, u32[]{:S(2)}) collective-permute-start(bf16[4,4,32,256]{3,2,1,0:T(8,128)(2,1)} %pad_maximum_fusion.1), channel_id=1, source_target_pairs={{0,8},{8,16},{16,24},{24,0},{1,9},{9,17},{17,25},{25,1},{2,10},{10... | collective-permute-start | bytes 786440 | tf_op jit(solution)/shard_map/ppermute | solution.py:163
  89.3 4.5 %collective-permute-start.7 = (bf16[4,4,32,256]{3,2,1,0:T(8,128)(2,1)}, bf16[4,4,32,256]{3,2,1,0:T(8,128)(2,1)}, u32[]{:S(2)}, u32[]{:S(2)}) collective-permute-start(bf16[4,4,32,256]{3,2,1,0:T(8,128)(2,1)} %pad_maximum_fusion.1), channel_id=1, source_target_pairs={{0,16},{8,24},{16,0},{24,8},{1,17},{9,25},{17,1},{25,9},{2,18},{10... | collective-permute-start | bytes 786440 | tf_op jit(solution)/shard_map/ppermute | solution.py:163
  93.8 2.9 %collective-permute-start.6 = (bf16[4,4,32,256]{3,2,1,0:T(8,128)(2,1)}, bf16[4,4,32,256]{3,2,1,0:T(8,128)(2,1)}, u32[]{:S(2)}, u32[]{:S(2)}) collective-permute-start(bf16[4,4,32,256]{3,2,1,0:T(8,128)(2,1)} %pad_maximum_fusion.1), channel_id=1, source_target_pairs={{0,24},{8,0},{16,8},{24,16},{1,25},{9,1},{17,9},{25,17},{2,26},{10... | collective-permute-start | bytes 786440 | tf_op jit(solution)/shard_map/ppermute | solution.py:163
  96.7 0.0 all-to-all-done.1.parts
  96.7 0.0 copy-done.5
  96.7 0.2 requantized.1
  97.0 0.0 collective-permute-done.8
  97.0 3.5 %collective-permute-done.7 = bf16[4,4,32,256]{3,2,1,0:T(8,128)(2,1)} collective-permute-done((bf16[4,4,32,256]{3,2,1,0:T(8,128)(2,1)}, bf16[4,4,32,256]{3,2,1,0:T(8,128)(2,1)}, u32[]{:S(2)}, u32[]{:S(2)}) %collective-permute-start.7) | collective-permute-done | bytes 262176 | tf_op jit(solution)/shard_map/ppermute | solution.py:163
  100.5 3.2 %collective-permute-done.6 = bf16[4,4,32,256]{3,2,1,0:T(8,128)(2,1)} collective-permute-done((bf16[4,4,32,256]{3,2,1,0:T(8,128)(2,1)}, bf16[4,4,32,256]{3,2,1,0:T(8,128)(2,1)}, u32[]{:S(2)}, u32[]{:S(2)}) %collective-permute-start.6) | collective-permute-done | bytes 262176 | tf_op jit(solution)/shard_map/ppermute | solution.py:163
  103.7 2.3 %pad_maximum_fusion.own = bf16[4,4,4,32,256]{4,3,2,1,0:T(8,128)(2,1)} fusion(bf16[1,4,4,32,256]{4,3,2,1,0:T(8,128)(2,1)} %bitcast.16, bf16[1,4,4,32,256]{4,3,2,1,0:T(8,128)(2,1)} %bitcast.15, bf16[1,4,4,32,256]{4,3,2,1,0:T(8,128)(2,1)} %bitcast.14, bf16[1,4,4,32,256]{4,3,2,1,0:T(8,128)(2,1)} %bitcast.13), kind=kLoop, calls=%fused_computation | loop fusion | flops 1572864 | bytes 2097152 | tf_op jit(solution)/shard_map/stack | solution.py:199
  106.0 5.7 %collective-permute-start.9 = (bf16[4,4,4,32,256]{4,3,2,1,0:T(8,128)(2,1)}, bf16[4,4,4,32,256]{4,3,2,1,0:T(8,128)(2,1)}, u32[]{:S(2)}, u32[]{:S(2)}) collective-permute-start(bf16[4,4,4,32,256]{4,3,2,1,0:T(8,128)(2,1)} %pad_maximum_fusion.own), channel_id=1, source_target_pairs={{0,1},{1,0},{2,3},{3,2},{4,5},{5,4},{6,7},{7,6},{8,9},{9,8},{10,11... | collective-permute-start | bytes 3145736 | tf_op jit(solution)/shard_map/ppermute | solution.py:163
  111.8 0.7 reshape.11
  112.4 15.9 %all-to-all-start.2 = ((bf16[32,4,256]{2,1,0:T(4,128)(2,1)}), bf16[32,4,256]{2,1,0:T(4,128)(2,1)S(1)}, u32[]{:S(2)}, u32[]{:S(2)}) async-start(bf16[32,4,256]{2,1,0:T(4,128)(2,1)} %reshape.11), calls=%async_computation.2 | async-start | bytes 131072 | tf_op jit(solution)/shard_map/all_to_all | solution.py:171
  128.3 0.1 pad_add_fusion.pos
  128.4 0.0 collective-permute-done.9.oth
  128.4 0.0 copy-done.2
  128.4 4.7 %hidden_grads.1 = bf16[192,128]{1,0:T(8,128)(2,1)} custom-call(s32[4]{0:T(128)S(1)} %pad_add_fusion.pos, bf16[192,8192]{1,0:T(8,128)(2,1)S(1)} %copy-done.2, bf16[4,4,4,32,256]{4,3,2,1,0:T(8,128)(2,1)} %pad_maximum_fusion.own, bf16[4,4,4,32,256]{4,3,2,1,0:T(8,128)(2,1)} %collective-permute-done.9.oth), custom_call_target="tpu_custom_call" | custom-call | flops 402653184 | bytes 5242880 | tf_op jit(solution)/shard_map/hidden_grads/pallas_call | solution.py:105
  133.1 6.8 %all-to-all-done.2 = bf16[32,4,256]{2,1,0:T(4,128)(2,1)S(1)} async-done(((bf16[32,4,256]{2,1,0:T(4,128)(2,1)}), bf16[32,4,256]{2,1,0:T(4,128)(2,1)S(1)}, u32[]{:S(2)}, u32[]{:S(2)}) %all-to-all-start.2) | async-done | bytes 65568 | tf_op jit(solution)/shard_map/all_to_all | solution.py:171
  139.9 0.6 convert_reduce_fusion
  (4 shorter events, 0.0 us)
Async XLA Ops:
  0.6 0.8 copy-start
  1.5 22.1 %collective-permute-start = (bf16[32,256]{1,0:T(8,128)(2,1)S(1)}, bf16[32,256]{1,0:T(8,128)(2,1)S(1)}, u32[]{:S(2)}, u32[]{:S(2)}) collective-permute-start(bf16[32,256]{1,0:T(8,128)(2,1)S(1)} %constant_dynamic-slice_fusion), channel_id=1, source_target_pairs={{0,2},{2,0},{4,6},{6,4},{1,3},{3,1},{5,7},{7,5},{8,10},{10,8},{12,... | collective-permute-start | bytes 49160 | tf_op jit(solution)/shard_map/ppermute | solution.py:158
  17.7 1.9 %copy-start.1 = (bf16[192,8192]{1,0:T(8,128)(2,1)S(1)}, bf16[192,8192]{1,0:T(8,128)(2,1)}, u32[]{:S(2)}) copy-start(bf16[192,8192]{1,0:T(8,128)(2,1)} %og.3) | copy-start | bytes 9437188
  19.6 0.8 copy-start.3
  20.4 0.8 copy-start.4
  23.6 10.6 %collective-permute-start.1 = (bf16[16,128,256]{2,1,0:T(8,128)(2,1)S(1)}, bf16[16,128,256]{2,1,0:T(8,128)(2,1)S(1)}, u32[]{:S(2)}, u32[]{:S(2)}) collective-permute-start(bf16[16,128,256]{2,1,0:T(8,128)(2,1)S(1)} %get-tuple-element.15), channel_id=1, source_target_pairs={{0,1},{1,0},{2,3},{3,2},{4,5},{5,4},{6,7},{7,6},{8,9},{9,8},{10,11... | collective-permute-start | bytes 3145736 | tf_op jit(solution)/shard_map/ppermute | solution.py:163
  34.1 62.6 %copy-start.5 = (s32[128,2]{0,1:T(2,128)S(1)}, s32[128,2]{0,1:T(2,128)}, u32[]{:S(2)}) copy-start(s32[128,2]{0,1:T(2,128)} %param.9) | copy-start | bytes 3076
  35.8 19.2 %all-to-all-start = ((bf16[4,4,128,256]{3,2,1,0:T(8,128)(2,1)}), bf16[4,4,128,256]{3,2,1,0:T(8,128)(2,1)}, u32[]{:S(2)}, u32[]{:S(2)}) async-start(bf16[4,4,128,256]{3,2,1,0:T(8,128)(2,1)} %bitcast.6), calls=%async_computation | async-start | bytes 2097152 | tf_op jit(solution)/shard_map/all_to_all | solution.py:171
  40.1 88.4 %copy-start.2 = (bf16[192,8192]{1,0:T(8,128)(2,1)S(1)}, bf16[192,8192]{1,0:T(8,128)(2,1)}, u32[]{:S(2)}) copy-start(bf16[192,8192]{1,0:T(8,128)(2,1)} %og.3) | copy-start | bytes 9437188
  40.1 13.7 %collective-permute-start.2 = (bf16[2,32,256]{2,1,0:T(8,128)(2,1)S(1)}, bf16[2,32,256]{2,1,0:T(8,128)(2,1)S(1)}, u32[]{:S(2)}, u32[]{:S(2)}) collective-permute-start(bf16[2,32,256]{2,1,0:T(8,128)(2,1)S(1)} %pad_maximum_fusion.3), channel_id=1, source_target_pairs={{0,6},{2,4},{4,2},{6,0},{1,7},{3,5},{5,3},{7,1},{8,14},{10,12},{12... | collective-permute-start | bytes 98312 | tf_op jit(solution)/shard_map/ppermute | solution.py:158
  58.2 38.5 %all-to-all-start.1 = ((bf16[4,128,256]{2,1,0:T(8,128)(2,1)}), bf16[4,128,256]{2,1,0:T(8,128)(2,1)S(1)}, u32[]{:S(2)}, u32[]{:S(2)}) async-start(bf16[4,128,256]{2,1,0:T(8,128)(2,1)} %lined.1), calls=%async_computation.1 | async-start | bytes 524288 | tf_op jit(solution)/shard_map/all_to_all | solution.py:171
  73.3 10.6 %collective-permute-start.5 = (bf16[4,32,256]{2,1,0:T(8,128)(2,1)S(1)}, bf16[4,32,256]{2,1,0:T(8,128)(2,1)S(1)}, u32[]{:S(2)}, u32[]{:S(2)}) collective-permute-start(bf16[4,32,256]{2,1,0:T(8,128)(2,1)S(1)} %pad_maximum_fusion.2), channel_id=1, source_target_pairs={{0,256},{256,512},{512,768},{768,0},{1,257},{257,513},{513,769},{7... | collective-permute-start | bytes 196616 | tf_op jit(solution)/shard_map/ppermute | solution.py:163
  76.4 7.4 %collective-permute-start.4 = (bf16[4,32,256]{2,1,0:T(8,128)(2,1)S(1)}, bf16[4,32,256]{2,1,0:T(8,128)(2,1)S(1)}, u32[]{:S(2)}, u32[]{:S(2)}) collective-permute-start(bf16[4,32,256]{2,1,0:T(8,128)(2,1)S(1)} %pad_maximum_fusion.2), channel_id=1, source_target_pairs={{0,512},{256,768},{512,0},{768,256},{1,513},{257,769},{513,1},{769... | collective-permute-start | bytes 196616 | tf_op jit(solution)/shard_map/ppermute | solution.py:163
  80.8 5.3 %collective-permute-start.3 = (bf16[4,32,256]{2,1,0:T(8,128)(2,1)S(1)}, bf16[4,32,256]{2,1,0:T(8,128)(2,1)S(1)}, u32[]{:S(2)}, u32[]{:S(2)}) collective-permute-start(bf16[4,32,256]{2,1,0:T(8,128)(2,1)S(1)} %pad_maximum_fusion.2), channel_id=1, source_target_pairs={{0,768},{256,0},{512,256},{768,512},{1,769},{257,1},{513,257},{769... | collective-permute-start | bytes 196616 | tf_op jit(solution)/shard_map/ppermute | solution.py:163
  86.9 10.1 %collective-permute-start.8 = (bf16[4,4,32,256]{3,2,1,0:T(8,128)(2,1)}, bf16[4,4,32,256]{3,2,1,0:T(8,128)(2,1)}, u32[]{:S(2)}, u32[]{:S(2)}) collective-permute-start(bf16[4,4,32,256]{3,2,1,0:T(8,128)(2,1)} %pad_maximum_fusion.1), channel_id=1, source_target_pairs={{0,8},{8,16},{16,24},{24,0},{1,9},{9,17},{17,25},{25,1},{2,10},{10... | collective-permute-start | bytes 786440 | tf_op jit(solution)/shard_map/ppermute | solution.py:163
  89.3 11.2 %collective-permute-start.7 = (bf16[4,4,32,256]{3,2,1,0:T(8,128)(2,1)}, bf16[4,4,32,256]{3,2,1,0:T(8,128)(2,1)}, u32[]{:S(2)}, u32[]{:S(2)}) collective-permute-start(bf16[4,4,32,256]{3,2,1,0:T(8,128)(2,1)} %pad_maximum_fusion.1), channel_id=1, source_target_pairs={{0,16},{8,24},{16,0},{24,8},{1,17},{9,25},{17,1},{25,9},{2,18},{10... | collective-permute-start | bytes 786440 | tf_op jit(solution)/shard_map/ppermute | solution.py:163
  93.8 9.9 %collective-permute-start.6 = (bf16[4,4,32,256]{3,2,1,0:T(8,128)(2,1)}, bf16[4,4,32,256]{3,2,1,0:T(8,128)(2,1)}, u32[]{:S(2)}, u32[]{:S(2)}) collective-permute-start(bf16[4,4,32,256]{3,2,1,0:T(8,128)(2,1)} %pad_maximum_fusion.1), channel_id=1, source_target_pairs={{0,24},{8,0},{16,8},{24,16},{1,25},{9,1},{17,9},{25,17},{2,26},{10... | collective-permute-start | bytes 786440 | tf_op jit(solution)/shard_map/ppermute | solution.py:163
  106.0 22.4 %collective-permute-start.9 = (bf16[4,4,4,32,256]{4,3,2,1,0:T(8,128)(2,1)}, bf16[4,4,4,32,256]{4,3,2,1,0:T(8,128)(2,1)}, u32[]{:S(2)}, u32[]{:S(2)}) collective-permute-start(bf16[4,4,4,32,256]{4,3,2,1,0:T(8,128)(2,1)} %pad_maximum_fusion.own), channel_id=1, source_target_pairs={{0,1},{1,0},{2,3},{3,2},{4,5},{5,4},{6,7},{7,6},{8,9},{9,8},{10,11... | collective-permute-start | bytes 3145736 | tf_op jit(solution)/shard_map/ppermute | solution.py:163
  112.4 27.5 %all-to-all-start.2 = ((bf16[32,4,256]{2,1,0:T(4,128)(2,1)}), bf16[32,4,256]{2,1,0:T(4,128)(2,1)S(1)}, u32[]{:S(2)}, u32[]{:S(2)}) async-start(bf16[32,4,256]{2,1,0:T(4,128)(2,1)} %reshape.11), calls=%async_computation.2 | async-start | bytes 131072 | tf_op jit(solution)/shard_map/all_to_all | solution.py:171

commit v7 on v6

--- a/solution.py
+++ b/solution.py
@@ -10,7 +10,8 @@
 OUTER = ("x", "zl")
 N_OUTER = 32
 LIMIT = 448.0
-VMEM = 8 << 20
+VMEM = 3 << 20
+VMEM_LOCAL, VMEM_HIDDEN = 64_980_000, 64_500_000
 ORDER = (0, 1, 3, 2)
 F32, BF16 = jnp.float32, jnp.bfloat16
 
@@ -55,7 +56,7 @@
             scratch_shapes=[pltpu.VMEM((128, 192), BF16)],
         ),
         out_shape=[block, block],
-        compiler_params=pltpu.CompilerParams(vmem_limit_bytes=VMEM),
+        compiler_params=pltpu.CompilerParams(vmem_limit_bytes=VMEM_LOCAL),
         cost_estimate=pl.CostEstimate(flops=1 << 20, bytes_accessed=1 << 16, transcendentals=0),
         name="local_grads",
     )(core, hidden, out_grad, exponent)
@@ -112,7 +113,7 @@
             scratch_shapes=[pltpu.VMEM((192, 128), F32)],
         ),
         out_shape=jax.ShapeDtypeStruct((192, 128), BF16),
-        compiler_params=pltpu.CompilerParams(vmem_limit_bytes=VMEM),
+        compiler_params=pltpu.CompilerParams(vmem_limit_bytes=VMEM_HIDDEN),
         cost_estimate=pl.CostEstimate(flops=2 * 192 * 128 * 8192, bytes_accessed=5 << 20, transcendentals=0),
         name="hidden_grads",
     )(pos, out_grad, own, oth)

time: 141 us -> 139 us (0.986)
  starting transfers between devices: 96.3 us -> 99.1 us
  other arithmetic: 3.8 us -> 1.5 us
  local copies, waits for them, and re-layouts: 4.95 us -> 2.72 us
  waiting for transfers between devices: 22.5 us -> 20.3 us
    pallas_call x1, Pallas kernels: 2.35 us -> 4.98 us  [local_grads(): pl.pallas_call(grad_kernel, grid_spec=pltpu.PrefetchScalarGridSpec(num_sc...]
    unnamed x12 -> x8, local copies, waits for them, and re-layouts: 4.28 us -> 2.06 us
    another operation x1, other arithmetic: 2.31 us -> 0.13 us  [per_device(): part = jnp.stack([after(piece, again) for piece in pieces(part, 'y')])]
    ppermute x8, starting transfers between devices: 34.4 us -> 36.5 us  [shifted(): return lax.ppermute(value, axis, [(i, (i - k) % n) for i in range(n)])]
    pallas_call x1, Pallas kernels: 3.25 us -> 1.45 us  [lined(): pl.pallas_call(line_kernel, grid=(4,), in_specs=[pl.BlockSpec((4, 1, 128,...]
  transfers between devices with their start and end apart: 13 -> 13, of which waited for: 7 -> 8; matrix products, arithmetic and copies ran while one was open for 1% -> 1% of each run, Pallas kernels for 5% -> 8%
where the time goes in v7:
time: 139 us; the launch traced here: 138 us
  starting transfers between devices  99.1 us (71%)
  waiting for transfers between devices  20.3 us (15%)
  Pallas kernels  13.5 us (10%)
  local copies, waits for them, and re-layouts  2.72 us (2%)
  other arithmetic  1.5 us (1%)
    ppermute x8, starting transfers between devices, shifted(): return lax.ppermute(value, axis, [(i, (i - k) % n) for i in range(n)])  36.5 us
    all_to_all x3, starting transfers between devices, swap(): return lax.all_to_all(value, axes, 0, 0, tiled=True)  35.6 us
    ppermute x2, starting transfers between devices, exchanged(): lax.ppermute(value, axis, [(i, i ^ bits) for i in range(SIZES[axis])])  27 us
    ppermute x8, waiting for transfers between devices, shifted(): return lax.ppermute(value, axis, [(i, (i - k) % n) for i in range(n)])  10 us
    all_to_all x3, waiting for transfers between devices, swap(): return lax.all_to_all(value, axes, 0, 0, tiled=True)  7.47 us
    pallas_call x1, Pallas kernels, hidden_grads(): pl.pallas_call(hidden_kernel, grid_spec=pltpu.PrefetchScalarGridSpec(num_...  5.18 us
    pallas_call x1, Pallas kernels, local_grads(): pl.pallas_call(grad_kernel, grid_spec=pltpu.PrefetchScalarGridSpec(num_sc...  4.98 us
    ppermute x2, waiting for transfers between devices, exchanged(): lax.ppermute(value, axis, [(i, i ^ bits) for i in range(SIZES[axis])])  2.81 us
  transfers between devices with their start and end apart: 13, of which 8 were waited for; matrix products, arithmetic and copies ran while one was open for 1% of the time, Pallas kernels for 8%

profile of v7, /device:TPU:1, one launch (start us, length us, event | category | flops | bytes accessed | tf_op | source)
XLA Modules:
  0.0 137.9 jit_solution(14684952282358322396)
XLA Ops:
  0.6 0.0 copy-start
  0.7 0.8 copy-done
  1.5 16.3 %collective-permute-start = (bf16[32,256]{1,0:T(8,128)(2,1)S(1)}, bf16[32,256]{1,0:T(8,128)(2,1)S(1)}, u32[]{:S(2)}, u32[]{:S(2)}) collective-permute-start(bf16[32,256]{1,0:T(8,128)(2,1)S(1)} %constant_dynamic-slice_fusion), channel_id=1, source_target_pairs={{0,2},{2,0},{4,6},{6,4},{1,3},{3,1},{5,7},{7,5},{8,10},{10,8},{12,... | collective-permute-start | bytes 49160 | tf_op jit(solution)/shard_map/ppermute | solution.py:159
  17.7 5.0 %local_grads.1 = (bf16[16,128,256]{2,1,0:T(8,128)(2,1)}, bf16[16,128,256]{2,1,0:T(8,128)(2,1)}) custom-call(s32[1]{0:T(128)} %bitcast.core, bf16[192,128]{1,0:T(8,128)(2,1)} %hid.1, bf16[192,8192]{1,0:T(8,128)(2,1)} %og.3, s32[64,128]{1,0:T(8,128)} %bitcast.29), custom_call_target="tpu_custom_call" | custom-call | flops 1048576 | bytes 65536 | tf_op jit(solution)/shard_map/local_grads/pallas_call | solution.py:45
  22.7 0.0 collective-permute-done
  22.7 9.1 %collective-permute-start.1 = (bf16[16,128,256]{2,1,0:T(8,128)(2,1)}, bf16[16,128,256]{2,1,0:T(8,128)(2,1)S(1)}, u32[]{:S(2)}, u32[]{:S(2)}) collective-permute-start(bf16[16,128,256]{2,1,0:T(8,128)(2,1)} %get-tuple-element.15), channel_id=1, source_target_pairs={{0,1},{1,0},{2,3},{3,2},{4,5},{5,4},{6,7},{7,6},{8,9},{9,8},{10,11... | collective-permute-start | bytes 3145736 | tf_op jit(solution)/shard_map/ppermute | solution.py:164
  31.9 2.5 %collective-permute-done.1.got = bf16[16,128,256]{2,1,0:T(8,128)(2,1)S(1)} collective-permute-done((bf16[16,128,256]{2,1,0:T(8,128)(2,1)}, bf16[16,128,256]{2,1,0:T(8,128)(2,1)S(1)}, u32[]{:S(2)}, u32[]{:S(2)}) %collective-permute-start.1) | collective-permute-done | bytes 1048608 | tf_op jit(solution)/shard_map/ppermute | solution.py:164
  34.3 0.0 copy-start.1
  34.3 1.2 copy-done.1
  35.6 0.0 copy-start.2
  35.6 1.6 %paired.1 = bf16[16,128,256]{2,1,0:T(8,128)(2,1)} custom-call(bf16[16,128,256]{2,1,0:T(8,128)(2,1)S(1)} %copy-done.1, bf16[16,128,256]{2,1,0:T(8,128)(2,1)S(1)} %collective-permute-done.1.got), custom_call_target="tpu_custom_call" | custom-call | flops 1048576 | bytes 3145728 | tf_op jit(solution)/shard_map/paired/pallas_call | solution.py:71
  37.2 3.5 %all-to-all-start = ((bf16[4,4,128,256]{3,2,1,0:T(8,128)(2,1)}), bf16[4,4,128,256]{3,2,1,0:T(8,128)(2,1)S(1)}, u32[]{:S(2)}, u32[]{:S(2)}) async-start(bf16[4,4,128,256]{3,2,1,0:T(8,128)(2,1)} %bitcast.6), calls=%async_computation | async-start | bytes 2097152 | tf_op jit(solution)/shard_map/all_to_all | solution.py:172
  40.8 10.7 %collective-permute-start.2 = (bf16[2,32,256]{2,1,0:T(8,128)(2,1)S(1)}, bf16[2,32,256]{2,1,0:T(8,128)(2,1)S(1)}, u32[]{:S(2)}, u32[]{:S(2)}) collective-permute-start(bf16[2,32,256]{2,1,0:T(8,128)(2,1)S(1)} %pad_maximum_fusion.3), channel_id=1, source_target_pairs={{0,6},{2,4},{4,2},{6,0},{1,7},{3,5},{5,3},{7,1},{8,14},{10,12},{12... | collective-permute-start | bytes 98312 | tf_op jit(solution)/shard_map/ppermute | solution.py:159
  51.5 2.8 %collective-permute-done.2 = bf16[2,32,256]{2,1,0:T(8,128)(2,1)S(1)} collective-permute-done((bf16[2,32,256]{2,1,0:T(8,128)(2,1)S(1)}, bf16[2,32,256]{2,1,0:T(8,128)(2,1)S(1)}, u32[]{:S(2)}, u32[]{:S(2)}) %collective-permute-start.2) | collective-permute-done | bytes 32800 | tf_op jit(solution)/shard_map/ppermute | solution.py:159
  54.3 1.2 all-to-all-done.parts
  55.5 1.5 %lined.1 = bf16[4,128,256]{2,1,0:T(8,128)(2,1)} custom-call(bf16[4,4,128,256]{3,2,1,0:T(8,128)(2,1)S(1)} %all-to-all-done.parts), custom_call_target="tpu_custom_call" | custom-call | flops 524288 | bytes 1310720 | tf_op jit(solution)/shard_map/lined/pallas_call | solution.py:127
  57.0 15.8 %all-to-all-start.1 = ((bf16[4,128,256]{2,1,0:T(8,128)(2,1)}), bf16[4,128,256]{2,1,0:T(8,128)(2,1)S(1)}, u32[]{:S(2)}, u32[]{:S(2)}) async-start(bf16[4,128,256]{2,1,0:T(8,128)(2,1)} %lined.1), calls=%async_computation.1 | async-start | bytes 524288 | tf_op jit(solution)/shard_map/all_to_all | solution.py:172
  72.8 3.1 %collective-permute-start.5 = (bf16[4,32,256]{2,1,0:T(8,128)(2,1)S(1)}, bf16[4,32,256]{2,1,0:T(8,128)(2,1)S(1)}, u32[]{:S(2)}, u32[]{:S(2)}) collective-permute-start(bf16[4,32,256]{2,1,0:T(8,128)(2,1)S(1)} %pad_maximum_fusion.2), channel_id=1, source_target_pairs={{0,256},{256,512},{512,768},{768,0},{1,257},{257,513},{513,769},{7... | collective-permute-start | bytes 196616 | tf_op jit(solution)/shard_map/ppermute | solution.py:164
  75.9 4.4 %collective-permute-start.4 = (bf16[4,32,256]{2,1,0:T(8,128)(2,1)S(1)}, bf16[4,32,256]{2,1,0:T(8,128)(2,1)S(1)}, u32[]{:S(2)}, u32[]{:S(2)}) collective-permute-start(bf16[4,32,256]{2,1,0:T(8,128)(2,1)S(1)} %pad_maximum_fusion.2), channel_id=1, source_target_pairs={{0,512},{256,768},{512,0},{768,256},{1,513},{257,769},{513,1},{769... | collective-permute-start | bytes 196616 | tf_op jit(solution)/shard_map/ppermute | solution.py:164
  80.3 3.1 %collective-permute-start.3 = (bf16[4,32,256]{2,1,0:T(8,128)(2,1)S(1)}, bf16[4,32,256]{2,1,0:T(8,128)(2,1)S(1)}, u32[]{:S(2)}, u32[]{:S(2)}) collective-permute-start(bf16[4,32,256]{2,1,0:T(8,128)(2,1)S(1)} %pad_maximum_fusion.2), channel_id=1, source_target_pairs={{0,768},{256,0},{512,256},{768,512},{1,769},{257,1},{513,257},{769... | collective-permute-start | bytes 196616 | tf_op jit(solution)/shard_map/ppermute | solution.py:164
  83.3 0.0 collective-permute-done.5
  83.3 0.0 collective-permute-done.4
  83.3 2.2 %collective-permute-done.3 = bf16[4,32,256]{2,1,0:T(8,128)(2,1)S(1)} collective-permute-done((bf16[4,32,256]{2,1,0:T(8,128)(2,1)S(1)}, bf16[4,32,256]{2,1,0:T(8,128)(2,1)S(1)}, u32[]{:S(2)}, u32[]{:S(2)}) %collective-permute-start.3) | collective-permute-done | bytes 65568 | tf_op jit(solution)/shard_map/ppermute | solution.py:164
  85.6 2.3 %collective-permute-start.8 = (bf16[4,4,32,256]{3,2,1,0:T(8,128)(2,1)S(1)}, bf16[4,4,32,256]{3,2,1,0:T(8,128)(2,1)S(1)}, u32[]{:S(2)}, u32[]{:S(2)}) collective-permute-start(bf16[4,4,32,256]{3,2,1,0:T(8,128)(2,1)S(1)} %pad_maximum_fusion.1), channel_id=1, source_target_pairs={{0,8},{8,16},{16,24},{24,0},{1,9},{9,17},{17,25},{25,1},{2,10},{10... | collective-permute-start | bytes 786440 | tf_op jit(solution)/shard_map/ppermute | solution.py:164
  87.9 4.3 %collective-permute-start.7 = (bf16[4,4,32,256]{3,2,1,0:T(8,128)(2,1)S(1)}, bf16[4,4,32,256]{3,2,1,0:T(8,128)(2,1)S(1)}, u32[]{:S(2)}, u32[]{:S(2)}) collective-permute-start(bf16[4,4,32,256]{3,2,1,0:T(8,128)(2,1)S(1)} %pad_maximum_fusion.1), channel_id=1, source_target_pairs={{0,16},{8,24},{16,0},{24,8},{1,17},{9,25},{17,1},{25,9},{2,18},{10... | collective-permute-start | bytes 786440 | tf_op jit(solution)/shard_map/ppermute | solution.py:164
  92.2 3.1 %collective-permute-start.6 = (bf16[4,4,32,256]{3,2,1,0:T(8,128)(2,1)S(1)}, bf16[4,4,32,256]{3,2,1,0:T(8,128)(2,1)S(1)}, u32[]{:S(2)}, u32[]{:S(2)}) collective-permute-start(bf16[4,4,32,256]{3,2,1,0:T(8,128)(2,1)S(1)} %pad_maximum_fusion.1), channel_id=1, source_target_pairs={{0,24},{8,0},{16,8},{24,16},{1,25},{9,1},{17,9},{25,17},{2,26},{10... | collective-permute-start | bytes 786440 | tf_op jit(solution)/shard_map/ppermute | solution.py:164
  95.3 0.5 all-to-all-done.1.parts
  95.8 0.0 copy-done.2
  95.8 0.2 requantized.1
  96.0 0.0 collective-permute-done.8
  96.0 2.4 %collective-permute-done.7 = bf16[4,4,32,256]{3,2,1,0:T(8,128)(2,1)S(1)} collective-permute-done((bf16[4,4,32,256]{3,2,1,0:T(8,128)(2,1)S(1)}, bf16[4,4,32,256]{3,2,1,0:T(8,128)(2,1)S(1)}, u32[]{:S(2)}, u32[]{:S(2)}) %collective-permute-start.7) | collective-permute-done | bytes 262176 | tf_op jit(solution)/shard_map/ppermute | solution.py:164
  98.5 2.9 %collective-permute-done.6 = bf16[4,4,32,256]{3,2,1,0:T(8,128)(2,1)S(1)} collective-permute-done((bf16[4,4,32,256]{3,2,1,0:T(8,128)(2,1)S(1)}, bf16[4,4,32,256]{3,2,1,0:T(8,128)(2,1)S(1)}, u32[]{:S(2)}, u32[]{:S(2)}) %collective-permute-start.6) | collective-permute-done | bytes 262176 | tf_op jit(solution)/shard_map/ppermute | solution.py:164
  101.4 0.1 pad_maximum_fusion.own
  101.5 0.0 copy-start.3
  101.5 7.2 %collective-permute-start.9 = (bf16[4,4,4,32,256]{4,3,2,1,0:T(8,128)(2,1)S(1)}, bf16[4,4,4,32,256]{4,3,2,1,0:T(8,128)(2,1)}, u32[]{:S(2)}, u32[]{:S(2)}) collective-permute-start(bf16[4,4,4,32,256]{4,3,2,1,0:T(8,128)(2,1)S(1)} %pad_maximum_fusion.own), channel_id=1, source_target_pairs={{0,1},{1,0},{2,3},{3,2},{4,5},{5,4},{6,7},{7,6},{8,9},{9,8},{10,11... | collective-permute-start | bytes 3145736 | tf_op jit(solution)/shard_map/ppermute | solution.py:164
  108.7 0.6 reshape.11
  109.3 16.3 %all-to-all-start.2 = ((bf16[32,4,256]{2,1,0:T(4,128)(2,1)}), bf16[32,4,256]{2,1,0:T(4,128)(2,1)S(1)}, u32[]{:S(2)}, u32[]{:S(2)}) async-start(bf16[32,4,256]{2,1,0:T(4,128)(2,1)} %reshape.11), calls=%async_computation.2 | async-start | bytes 131072 | tf_op jit(solution)/shard_map/all_to_all | solution.py:172
  125.6 0.7 pad_add_fusion.pos
  126.3 0.0 collective-permute-done.9.oth
  126.3 0.0 copy-done.3
  126.3 5.2 %hidden_grads.1 = bf16[192,128]{1,0:T(8,128)(2,1)} custom-call(s32[4]{0:T(128)} %pad_add_fusion.pos, bf16[192,8192]{1,0:T(8,128)(2,1)} %og.3, bf16[4,4,4,32,256]{4,3,2,1,0:T(8,128)(2,1)} %copy-done.3, bf16[4,4,4,32,256]{4,3,2,1,0:T(8,128)(2,1)} %collective-permute-done.9.oth), custom_call_target="tpu_custom_call" | custom-call | flops 402653184 | bytes 5242880 | tf_op jit(solution)/shard_map/hidden_grads/pallas_call | solution.py:106
  131.5 5.7 %all-to-all-done.2 = bf16[32,4,256]{2,1,0:T(4,128)(2,1)S(1)} async-done(((bf16[32,4,256]{2,1,0:T(4,128)(2,1)}), bf16[32,4,256]{2,1,0:T(4,128)(2,1)S(1)}, u32[]{:S(2)}, u32[]{:S(2)}) %all-to-all-start.2) | async-done | bytes 65568 | tf_op jit(solution)/shard_map/all_to_all | solution.py:172
  137.2 0.6 convert_reduce_fusion
  (5 shorter events, 0.1 us)
Async XLA Ops:
  0.6 0.8 copy-start
  1.5 21.3 %collective-permute-start = (bf16[32,256]{1,0:T(8,128)(2,1)S(1)}, bf16[32,256]{1,0:T(8,128)(2,1)S(1)}, u32[]{:S(2)}, u32[]{:S(2)}) collective-permute-start(bf16[32,256]{1,0:T(8,128)(2,1)S(1)} %constant_dynamic-slice_fusion), channel_id=1, source_target_pairs={{0,2},{2,0},{4,6},{6,4},{1,3},{3,1},{5,7},{7,5},{8,10},{10,8},{12,... | collective-permute-start | bytes 49160 | tf_op jit(solution)/shard_map/ppermute | solution.py:159
  22.7 11.6 %collective-permute-start.1 = (bf16[16,128,256]{2,1,0:T(8,128)(2,1)}, bf16[16,128,256]{2,1,0:T(8,128)(2,1)S(1)}, u32[]{:S(2)}, u32[]{:S(2)}) collective-permute-start(bf16[16,128,256]{2,1,0:T(8,128)(2,1)} %get-tuple-element.15), channel_id=1, source_target_pairs={{0,1},{1,0},{2,3},{3,2},{4,5},{5,4},{6,7},{7,6},{8,9},{9,8},{10,11... | collective-permute-start | bytes 3145736 | tf_op jit(solution)/shard_map/ppermute | solution.py:164
  34.3 1.2 copy-start.1
  35.6 60.2 %copy-start.2 = (s32[128,2]{0,1:T(2,128)S(1)}, s32[128,2]{0,1:T(2,128)}, u32[]{:S(2)}) copy-start(s32[128,2]{0,1:T(2,128)} %param.9) | copy-start | bytes 3076
  37.2 18.3 %all-to-all-start = ((bf16[4,4,128,256]{3,2,1,0:T(8,128)(2,1)}), bf16[4,4,128,256]{3,2,1,0:T(8,128)(2,1)S(1)}, u32[]{:S(2)}, u32[]{:S(2)}) async-start(bf16[4,4,128,256]{3,2,1,0:T(8,128)(2,1)} %bitcast.6), calls=%async_computation | async-start | bytes 2097152 | tf_op jit(solution)/shard_map/all_to_all | solution.py:172
  40.8 13.5 %collective-permute-start.2 = (bf16[2,32,256]{2,1,0:T(8,128)(2,1)S(1)}, bf16[2,32,256]{2,1,0:T(8,128)(2,1)S(1)}, u32[]{:S(2)}, u32[]{:S(2)}) collective-permute-start(bf16[2,32,256]{2,1,0:T(8,128)(2,1)S(1)} %pad_maximum_fusion.3), channel_id=1, source_target_pairs={{0,6},{2,4},{4,2},{6,0},{1,7},{3,5},{5,3},{7,1},{8,14},{10,12},{12... | collective-permute-start | bytes 98312 | tf_op jit(solution)/shard_map/ppermute | solution.py:159
  57.0 38.8 %all-to-all-start.1 = ((bf16[4,128,256]{2,1,0:T(8,128)(2,1)}), bf16[4,128,256]{2,1,0:T(8,128)(2,1)S(1)}, u32[]{:S(2)}, u32[]{:S(2)}) async-start(bf16[4,128,256]{2,1,0:T(8,128)(2,1)} %lined.1), calls=%async_computation.1 | async-start | bytes 524288 | tf_op jit(solution)/shard_map/all_to_all | solution.py:172
  72.8 10.6 %collective-permute-start.5 = (bf16[4,32,256]{2,1,0:T(8,128)(2,1)S(1)}, bf16[4,32,256]{2,1,0:T(8,128)(2,1)S(1)}, u32[]{:S(2)}, u32[]{:S(2)}) collective-permute-start(bf16[4,32,256]{2,1,0:T(8,128)(2,1)S(1)} %pad_maximum_fusion.2), channel_id=1, source_target_pairs={{0,256},{256,512},{512,768},{768,0},{1,257},{257,513},{513,769},{7... | collective-permute-start | bytes 196616 | tf_op jit(solution)/shard_map/ppermute | solution.py:164
  75.9 7.4 %collective-permute-start.4 = (bf16[4,32,256]{2,1,0:T(8,128)(2,1)S(1)}, bf16[4,32,256]{2,1,0:T(8,128)(2,1)S(1)}, u32[]{:S(2)}, u32[]{:S(2)}) collective-permute-start(bf16[4,32,256]{2,1,0:T(8,128)(2,1)S(1)} %pad_maximum_fusion.2), channel_id=1, source_target_pairs={{0,512},{256,768},{512,0},{768,256},{1,513},{257,769},{513,1},{769... | collective-permute-start | bytes 196616 | tf_op jit(solution)/shard_map/ppermute | solution.py:164
  80.3 5.3 %collective-permute-start.3 = (bf16[4,32,256]{2,1,0:T(8,128)(2,1)S(1)}, bf16[4,32,256]{2,1,0:T(8,128)(2,1)S(1)}, u32[]{:S(2)}, u32[]{:S(2)}) collective-permute-start(bf16[4,32,256]{2,1,0:T(8,128)(2,1)S(1)} %pad_maximum_fusion.2), channel_id=1, source_target_pairs={{0,768},{256,0},{512,256},{768,512},{1,769},{257,1},{513,257},{769... | collective-permute-start | bytes 196616 | tf_op jit(solution)/shard_map/ppermute | solution.py:164
  85.6 10.4 %collective-permute-start.8 = (bf16[4,4,32,256]{3,2,1,0:T(8,128)(2,1)S(1)}, bf16[4,4,32,256]{3,2,1,0:T(8,128)(2,1)S(1)}, u32[]{:S(2)}, u32[]{:S(2)}) collective-permute-start(bf16[4,4,32,256]{3,2,1,0:T(8,128)(2,1)S(1)} %pad_maximum_fusion.1), channel_id=1, source_target_pairs={{0,8},{8,16},{16,24},{24,0},{1,9},{9,17},{17,25},{25,1},{2,10},{10... | collective-permute-start | bytes 786440 | tf_op jit(solution)/shard_map/ppermute | solution.py:164
  87.9 10.6 %collective-permute-start.7 = (bf16[4,4,32,256]{3,2,1,0:T(8,128)(2,1)S(1)}, bf16[4,4,32,256]{3,2,1,0:T(8,128)(2,1)S(1)}, u32[]{:S(2)}, u32[]{:S(2)}) collective-permute-start(bf16[4,4,32,256]{3,2,1,0:T(8,128)(2,1)S(1)} %pad_maximum_fusion.1), channel_id=1, source_target_pairs={{0,16},{8,24},{16,0},{24,8},{1,17},{9,25},{17,1},{25,9},{2,18},{10... | collective-permute-start | bytes 786440 | tf_op jit(solution)/shard_map/ppermute | solution.py:164
  92.2 9.2 %collective-permute-start.6 = (bf16[4,4,32,256]{3,2,1,0:T(8,128)(2,1)S(1)}, bf16[4,4,32,256]{3,2,1,0:T(8,128)(2,1)S(1)}, u32[]{:S(2)}, u32[]{:S(2)}) collective-permute-start(bf16[4,4,32,256]{3,2,1,0:T(8,128)(2,1)S(1)} %pad_maximum_fusion.1), channel_id=1, source_target_pairs={{0,24},{8,0},{16,8},{24,16},{1,25},{9,1},{17,9},{25,17},{2,26},{10... | collective-permute-start | bytes 786440 | tf_op jit(solution)/shard_map/ppermute | solution.py:164
  101.5 24.8 %copy-start.3 = (bf16[4,4,4,32,256]{4,3,2,1,0:T(8,128)(2,1)}, bf16[4,4,4,32,256]{4,3,2,1,0:T(8,128)(2,1)S(1)}, u32[]{:S(2)}) copy-start(bf16[4,4,4,32,256]{4,3,2,1,0:T(8,128)(2,1)S(1)} %pad_maximum_fusion.own) | copy-start | bytes 3145732
  101.5 24.8 %collective-permute-start.9 = (bf16[4,4,4,32,256]{4,3,2,1,0:T(8,128)(2,1)S(1)}, bf16[4,4,4,32,256]{4,3,2,1,0:T(8,128)(2,1)}, u32[]{:S(2)}, u32[]{:S(2)}) collective-permute-start(bf16[4,4,4,32,256]{4,3,2,1,0:T(8,128)(2,1)S(1)} %pad_maximum_fusion.own), channel_id=1, source_target_pairs={{0,1},{1,0},{2,3},{3,2},{4,5},{5,4},{6,7},{7,6},{8,9},{9,8},{10,11... | collective-permute-start | bytes 3145736 | tf_op jit(solution)/shard_map/ppermute | solution.py:164
  109.3 27.9 %all-to-all-start.2 = ((bf16[32,4,256]{2,1,0:T(4,128)(2,1)}), bf16[32,4,256]{2,1,0:T(4,128)(2,1)S(1)}, u32[]{:S(2)}, u32[]{:S(2)}) async-start(bf16[32,4,256]{2,1,0:T(4,128)(2,1)} %reshape.11), calls=%async_computation.2 | async-start | bytes 131072 | tf_op jit(solution)/shard_map/all_to_all | solution.py:172

commit v8 on v7

--- a/solution.py
+++ b/solution.py
@@ -11,7 +11,7 @@
 N_OUTER = 32
 LIMIT = 448.0
 VMEM = 3 << 20
-VMEM_LOCAL, VMEM_HIDDEN = 64_980_000, 64_500_000
+VMEM_LOCAL, VMEM_HIDDEN = 3 << 20, 65_500_000
 ORDER = (0, 1, 3, 2)
 F32, BF16 = jnp.float32, jnp.bfloat16
 

time: 139 us -> 137 us (0.986)
  Pallas kernels: 13.5 us -> 10.8 us
  local copies, waits for them, and re-layouts: 2.72 us -> 4.95 us
    pallas_call x1, Pallas kernels: 4.98 us -> 2.35 us  [local_grads(): pl.pallas_call(grad_kernel, grid_spec=pltpu.PrefetchScalarGridSpec(num_sc...]
    unnamed x8 -> x12, local copies, waits for them, and re-layouts: 2.06 us -> 4.28 us
  transfers between devices with their start and end apart: 13 -> 13, of which waited for: 8 -> 8; matrix products, arithmetic and copies ran while one was open for 1% -> 1% of each run, Pallas kernels for 8% -> 6%
where the time goes in v8:
time: 137 us; the launch traced here: 136 us
  starting transfers between devices  98.2 us (72%)
  waiting for transfers between devices  20.2 us (15%)
  Pallas kernels  10.8 us (8%)
  local copies, waits for them, and re-layouts  4.95 us (4%)
  other arithmetic  1.44 us (1%)
    ppermute x8, starting transfers between devices, shifted(): return lax.ppermute(value, axis, [(i, (i - k) % n) for i in range(n)])  35.7 us
    all_to_all x3, starting transfers between devices, swap(): return lax.all_to_all(value, axes, 0, 0, tiled=True)  35.6 us
    ppermute x2, starting transfers between devices, exchanged(): lax.ppermute(value, axis, [(i, i ^ bits) for i in range(SIZES[axis])])  27 us
    ppermute x8, waiting for transfers between devices, shifted(): return lax.ppermute(value, axis, [(i, (i - k) % n) for i in range(n)])  9.83 us
    all_to_all x3, waiting for transfers between devices, swap(): return lax.all_to_all(value, axes, 0, 0, tiled=True)  7.53 us
    pallas_call x1, Pallas kernels, hidden_grads(): pl.pallas_call(hidden_kernel, grid_spec=pltpu.PrefetchScalarGridSpec(num_...  5.17 us
    unnamed x12, local copies, waits for them, and re-layouts  4.28 us
    ppermute x2, waiting for transfers between devices, exchanged(): lax.ppermute(value, axis, [(i, i ^ bits) for i in range(SIZES[axis])])  2.82 us
  transfers between devices with their start and end apart: 13, of which 8 were waited for; matrix products, arithmetic and copies ran while one was open for 1% of the time, Pallas kernels for 6%

profile of v8, /device:TPU:1, one launch (start us, length us, event | category | flops | bytes accessed | tf_op | source)
XLA Modules:
  0.0 136.4 jit_solution(12927270926666535327)
XLA Ops:
  0.6 0.0 copy-start
  0.7 0.8 copy-done
  1.5 16.3 %collective-permute-start = (bf16[32,256]{1,0:T(8,128)(2,1)S(1)}, bf16[32,256]{1,0:T(8,128)(2,1)S(1)}, u32[]{:S(2)}, u32[]{:S(2)}) collective-permute-start(bf16[32,256]{1,0:T(8,128)(2,1)S(1)} %constant_dynamic-slice_fusion), channel_id=1, source_target_pairs={{0,2},{2,0},{4,6},{6,4},{1,3},{3,1},{5,7},{7,5},{8,10},{10,8},{12,... | collective-permute-start | bytes 49160 | tf_op jit(solution)/shard_map/ppermute | solution.py:159
  17.7 0.0 copy-start.1
  17.8 1.9 %copy-done.1 = bf16[192,8192]{1,0:T(8,128)(2,1)S(1)} copy-done((bf16[192,8192]{1,0:T(8,128)(2,1)S(1)}, bf16[192,8192]{1,0:T(8,128)(2,1)}, u32[]{:S(2)}) %copy-start.1) | copy-done | bytes 3145752
  19.6 0.0 copy-start.2
  19.6 0.8 copy-done.2
  20.4 0.0 copy-start.3
  20.4 0.8 copy-done.3
  21.2 2.3 %local_grads.1 = (bf16[16,128,256]{2,1,0:T(8,128)(2,1)S(1)}, bf16[16,128,256]{2,1,0:T(8,128)(2,1)S(1)}) custom-call(s32[1]{0:T(128)} %bitcast.core, bf16[192,128]{1,0:T(8,128)(2,1)S(1)} %copy-done.2, bf16[192,8192]{1,0:T(8,128)(2,1)S(1)} %copy-done.1, s32[64,128]{1,0:T(8,128)S(1)} %bitcast.18), custom_call_target="tpu_custom_call" | custom-call | flops 1048576 | bytes 65536 | tf_op jit(solution)/shard_map/local_grads/pallas_call | solution.py:45
  23.6 0.0 collective-permute-done
  23.6 8.3 %collective-permute-start.1 = (bf16[16,128,256]{2,1,0:T(8,128)(2,1)S(1)}, bf16[16,128,256]{2,1,0:T(8,128)(2,1)S(1)}, u32[]{:S(2)}, u32[]{:S(2)}) collective-permute-start(bf16[16,128,256]{2,1,0:T(8,128)(2,1)S(1)} %get-tuple-element.15), channel_id=1, source_target_pairs={{0,1},{1,0},{2,3},{3,2},{4,5},{5,4},{6,7},{7,6},{8,9},{9,8},{10,11... | collective-permute-start | bytes 3145736 | tf_op jit(solution)/shard_map/ppermute | solution.py:164
  31.9 2.3 %collective-permute-done.1.got = bf16[16,128,256]{2,1,0:T(8,128)(2,1)S(1)} collective-permute-done((bf16[16,128,256]{2,1,0:T(8,128)(2,1)S(1)}, bf16[16,128,256]{2,1,0:T(8,128)(2,1)S(1)}, u32[]{:S(2)}, u32[]{:S(2)}) %collective-permute-start.1) | collective-permute-done | bytes 1048608 | tf_op jit(solution)/shard_map/ppermute | solution.py:164
  34.1 0.0 copy-start.4
  34.1 1.6 %paired.1 = bf16[16,128,256]{2,1,0:T(8,128)(2,1)} custom-call(bf16[16,128,256]{2,1,0:T(8,128)(2,1)S(1)} %get-tuple-element.13.own, bf16[16,128,256]{2,1,0:T(8,128)(2,1)S(1)} %collective-permute-done.1.got), custom_call_target="tpu_custom_call" | custom-call | flops 1048576 | bytes 3145728 | tf_op jit(solution)/shard_map/paired/pallas_call | solution.py:71
  35.8 3.5 %all-to-all-start = ((bf16[4,4,128,256]{3,2,1,0:T(8,128)(2,1)}), bf16[4,4,128,256]{3,2,1,0:T(8,128)(2,1)S(1)}, u32[]{:S(2)}, u32[]{:S(2)}) async-start(bf16[4,4,128,256]{3,2,1,0:T(8,128)(2,1)} %bitcast.6), calls=%async_computation | async-start | bytes 2097152 | tf_op jit(solution)/shard_map/all_to_all | solution.py:172
  39.3 10.7 %collective-permute-start.2 = (bf16[2,32,256]{2,1,0:T(8,128)(2,1)S(1)}, bf16[2,32,256]{2,1,0:T(8,128)(2,1)S(1)}, u32[]{:S(2)}, u32[]{:S(2)}) collective-permute-start(bf16[2,32,256]{2,1,0:T(8,128)(2,1)S(1)} %pad_maximum_fusion.3), channel_id=1, source_target_pairs={{0,6},{2,4},{4,2},{6,0},{1,7},{3,5},{5,3},{7,1},{8,14},{10,12},{12... | collective-permute-start | bytes 98312 | tf_op jit(solution)/shard_map/ppermute | solution.py:159
  50.0 2.8 %collective-permute-done.2 = bf16[2,32,256]{2,1,0:T(8,128)(2,1)S(1)} collective-permute-done((bf16[2,32,256]{2,1,0:T(8,128)(2,1)S(1)}, bf16[2,32,256]{2,1,0:T(8,128)(2,1)S(1)}, u32[]{:S(2)}, u32[]{:S(2)}) %collective-permute-start.2) | collective-permute-done | bytes 32800 | tf_op jit(solution)/shard_map/ppermute | solution.py:159
  52.9 1.2 all-to-all-done.parts
  54.1 1.5 %lined.1 = bf16[4,128,256]{2,1,0:T(8,128)(2,1)} custom-call(bf16[4,4,128,256]{3,2,1,0:T(8,128)(2,1)S(1)} %all-to-all-done.parts), custom_call_target="tpu_custom_call" | custom-call | flops 524288 | bytes 1310720 | tf_op jit(solution)/shard_map/lined/pallas_call | solution.py:127
  55.5 15.8 %all-to-all-start.1 = ((bf16[4,128,256]{2,1,0:T(8,128)(2,1)}), bf16[4,128,256]{2,1,0:T(8,128)(2,1)S(1)}, u32[]{:S(2)}, u32[]{:S(2)}) async-start(bf16[4,128,256]{2,1,0:T(8,128)(2,1)} %lined.1), calls=%async_computation.1 | async-start | bytes 524288 | tf_op jit(solution)/shard_map/all_to_all | solution.py:172
  71.3 3.1 %collective-permute-start.5 = (bf16[4,32,256]{2,1,0:T(8,128)(2,1)S(1)}, bf16[4,32,256]{2,1,0:T(8,128)(2,1)S(1)}, u32[]{:S(2)}, u32[]{:S(2)}) collective-permute-start(bf16[4,32,256]{2,1,0:T(8,128)(2,1)S(1)} %pad_maximum_fusion.2), channel_id=1, source_target_pairs={{0,256},{256,512},{512,768},{768,0},{1,257},{257,513},{513,769},{7... | collective-permute-start | bytes 196616 | tf_op jit(solution)/shard_map/ppermute | solution.py:164
  74.4 4.4 %collective-permute-start.4 = (bf16[4,32,256]{2,1,0:T(8,128)(2,1)S(1)}, bf16[4,32,256]{2,1,0:T(8,128)(2,1)S(1)}, u32[]{:S(2)}, u32[]{:S(2)}) collective-permute-start(bf16[4,32,256]{2,1,0:T(8,128)(2,1)S(1)} %pad_maximum_fusion.2), channel_id=1, source_target_pairs={{0,512},{256,768},{512,0},{768,256},{1,513},{257,769},{513,1},{769... | collective-permute-start | bytes 196616 | tf_op jit(solution)/shard_map/ppermute | solution.py:164
  78.8 3.1 %collective-permute-start.3 = (bf16[4,32,256]{2,1,0:T(8,128)(2,1)S(1)}, bf16[4,32,256]{2,1,0:T(8,128)(2,1)S(1)}, u32[]{:S(2)}, u32[]{:S(2)}) collective-permute-start(bf16[4,32,256]{2,1,0:T(8,128)(2,1)S(1)} %pad_maximum_fusion.2), channel_id=1, source_target_pairs={{0,768},{256,0},{512,256},{768,512},{1,769},{257,1},{513,257},{769... | collective-permute-start | bytes 196616 | tf_op jit(solution)/shard_map/ppermute | solution.py:164
  81.9 0.0 collective-permute-done.5
  81.9 0.0 collective-permute-done.4
  81.9 2.2 %collective-permute-done.3 = bf16[4,32,256]{2,1,0:T(8,128)(2,1)S(1)} collective-permute-done((bf16[4,32,256]{2,1,0:T(8,128)(2,1)S(1)}, bf16[4,32,256]{2,1,0:T(8,128)(2,1)S(1)}, u32[]{:S(2)}, u32[]{:S(2)}) %collective-permute-start.3) | collective-permute-done | bytes 65568 | tf_op jit(solution)/shard_map/ppermute | solution.py:164
  84.2 2.3 %collective-permute-start.8 = (bf16[4,4,32,256]{3,2,1,0:T(8,128)(2,1)S(1)}, bf16[4,4,32,256]{3,2,1,0:T(8,128)(2,1)S(1)}, u32[]{:S(2)}, u32[]{:S(2)}) collective-permute-start(bf16[4,4,32,256]{3,2,1,0:T(8,128)(2,1)S(1)} %pad_maximum_fusion.1), channel_id=1, source_target_pairs={{0,8},{8,16},{16,24},{24,0},{1,9},{9,17},{17,25},{25,1},{2,10},{10... | collective-permute-start | bytes 786440 | tf_op jit(solution)/shard_map/ppermute | solution.py:164
  86.5 4.3 %collective-permute-start.7 = (bf16[4,4,32,256]{3,2,1,0:T(8,128)(2,1)S(1)}, bf16[4,4,32,256]{3,2,1,0:T(8,128)(2,1)S(1)}, u32[]{:S(2)}, u32[]{:S(2)}) collective-permute-start(bf16[4,4,32,256]{3,2,1,0:T(8,128)(2,1)S(1)} %pad_maximum_fusion.1), channel_id=1, source_target_pairs={{0,16},{8,24},{16,0},{24,8},{1,17},{9,25},{17,1},{25,9},{2,18},{10... | collective-permute-start | bytes 786440 | tf_op jit(solution)/shard_map/ppermute | solution.py:164
  90.8 3.1 %collective-permute-start.6 = (bf16[4,4,32,256]{3,2,1,0:T(8,128)(2,1)S(1)}, bf16[4,4,32,256]{3,2,1,0:T(8,128)(2,1)S(1)}, u32[]{:S(2)}, u32[]{:S(2)}) collective-permute-start(bf16[4,4,32,256]{3,2,1,0:T(8,128)(2,1)S(1)} %pad_maximum_fusion.1), channel_id=1, source_target_pairs={{0,24},{8,0},{16,8},{24,16},{1,25},{9,1},{17,9},{25,17},{2,26},{10... | collective-permute-start | bytes 786440 | tf_op jit(solution)/shard_map/ppermute | solution.py:164
  93.9 0.5 all-to-all-done.1.parts
  94.4 0.0 copy-done.4
  94.4 0.2 requantized.1
  94.6 0.0 collective-permute-done.8
  94.6 2.4 %collective-permute-done.7 = bf16[4,4,32,256]{3,2,1,0:T(8,128)(2,1)S(1)} collective-permute-done((bf16[4,4,32,256]{3,2,1,0:T(8,128)(2,1)S(1)}, bf16[4,4,32,256]{3,2,1,0:T(8,128)(2,1)S(1)}, u32[]{:S(2)}, u32[]{:S(2)}) %collective-permute-start.7) | collective-permute-done | bytes 262176 | tf_op jit(solution)/shard_map/ppermute | solution.py:164
  97.0 2.9 %collective-permute-done.6 = bf16[4,4,32,256]{3,2,1,0:T(8,128)(2,1)S(1)} collective-permute-done((bf16[4,4,32,256]{3,2,1,0:T(8,128)(2,1)S(1)}, bf16[4,4,32,256]{3,2,1,0:T(8,128)(2,1)S(1)}, u32[]{:S(2)}, u32[]{:S(2)}) %collective-permute-start.6) | collective-permute-done | bytes 262176 | tf_op jit(solution)/shard_map/ppermute | solution.py:164
  99.9 0.1 pad_maximum_fusion.own
  100.1 0.0 copy-start.5
  100.1 7.2 %collective-permute-start.9 = (bf16[4,4,4,32,256]{4,3,2,1,0:T(8,128)(2,1)S(1)}, bf16[4,4,4,32,256]{4,3,2,1,0:T(8,128)(2,1)}, u32[]{:S(2)}, u32[]{:S(2)}) collective-permute-start(bf16[4,4,4,32,256]{4,3,2,1,0:T(8,128)(2,1)S(1)} %pad_maximum_fusion.own), channel_id=1, source_target_pairs={{0,1},{1,0},{2,3},{3,2},{4,5},{5,4},{6,7},{7,6},{8,9},{9,8},{10,11... | collective-permute-start | bytes 3145736 | tf_op jit(solution)/shard_map/ppermute | solution.py:164
  107.3 0.7 reshape.11
  107.9 16.3 %all-to-all-start.2 = ((bf16[32,4,256]{2,1,0:T(4,128)(2,1)}), bf16[32,4,256]{2,1,0:T(4,128)(2,1)S(1)}, u32[]{:S(2)}, u32[]{:S(2)}) async-start(bf16[32,4,256]{2,1,0:T(4,128)(2,1)} %reshape.11), calls=%async_computation.2 | async-start | bytes 131072 | tf_op jit(solution)/shard_map/all_to_all | solution.py:172
  124.2 0.6 pad_add_fusion.pos
  124.8 0.0 collective-permute-done.9.oth
  124.8 0.0 copy-done.5
  124.8 5.2 %hidden_grads.1 = bf16[192,128]{1,0:T(8,128)(2,1)} custom-call(s32[4]{0:T(128)} %pad_add_fusion.pos, bf16[192,8192]{1,0:T(8,128)(2,1)} %og.3, bf16[4,4,4,32,256]{4,3,2,1,0:T(8,128)(2,1)} %copy-done.5, bf16[4,4,4,32,256]{4,3,2,1,0:T(8,128)(2,1)} %collective-permute-done.9.oth), custom_call_target="tpu_custom_call" | custom-call | flops 402653184 | bytes 5242880 | tf_op jit(solution)/shard_map/hidden_grads/pallas_call | solution.py:106
  130.0 5.8 %all-to-all-done.2 = bf16[32,4,256]{2,1,0:T(4,128)(2,1)S(1)} async-done(((bf16[32,4,256]{2,1,0:T(4,128)(2,1)}), bf16[32,4,256]{2,1,0:T(4,128)(2,1)S(1)}, u32[]{:S(2)}, u32[]{:S(2)}) %all-to-all-start.2) | async-done | bytes 65568 | tf_op jit(solution)/shard_map/all_to_all | solution.py:172
  135.8 0.6 convert_reduce_fusion
  (5 shorter events, 0.1 us)
Async XLA Ops:
  0.6 0.8 copy-start
  1.5 22.1 %collective-permute-start = (bf16[32,256]{1,0:T(8,128)(2,1)S(1)}, bf16[32,256]{1,0:T(8,128)(2,1)S(1)}, u32[]{:S(2)}, u32[]{:S(2)}) collective-permute-start(bf16[32,256]{1,0:T(8,128)(2,1)S(1)} %constant_dynamic-slice_fusion), channel_id=1, source_target_pairs={{0,2},{2,0},{4,6},{6,4},{1,3},{3,1},{5,7},{7,5},{8,10},{10,8},{12,... | collective-permute-start | bytes 49160 | tf_op jit(solution)/shard_map/ppermute | solution.py:159
  17.7 1.9 %copy-start.1 = (bf16[192,8192]{1,0:T(8,128)(2,1)S(1)}, bf16[192,8192]{1,0:T(8,128)(2,1)}, u32[]{:S(2)}) copy-start(bf16[192,8192]{1,0:T(8,128)(2,1)} %og.3) | copy-start | bytes 9437188
  19.6 0.8 copy-start.2
  20.4 0.8 copy-start.3
  23.6 10.6 %collective-permute-start.1 = (bf16[16,128,256]{2,1,0:T(8,128)(2,1)S(1)}, bf16[16,128,256]{2,1,0:T(8,128)(2,1)S(1)}, u32[]{:S(2)}, u32[]{:S(2)}) collective-permute-start(bf16[16,128,256]{2,1,0:T(8,128)(2,1)S(1)} %get-tuple-element.15), channel_id=1, source_target_pairs={{0,1},{1,0},{2,3},{3,2},{4,5},{5,4},{6,7},{7,6},{8,9},{9,8},{10,11... | collective-permute-start | bytes 3145736 | tf_op jit(solution)/shard_map/ppermute | solution.py:164
  34.1 60.2 %copy-start.4 = (s32[128,2]{0,1:T(2,128)S(1)}, s32[128,2]{0,1:T(2,128)}, u32[]{:S(2)}) copy-start(s32[128,2]{0,1:T(2,128)} %param.9) | copy-start | bytes 3076
  35.8 18.3 %all-to-all-start = ((bf16[4,4,128,256]{3,2,1,0:T(8,128)(2,1)}), bf16[4,4,128,256]{3,2,1,0:T(8,128)(2,1)S(1)}, u32[]{:S(2)}, u32[]{:S(2)}) async-start(bf16[4,4,128,256]{3,2,1,0:T(8,128)(2,1)} %bitcast.6), calls=%async_computation | async-start | bytes 2097152 | tf_op jit(solution)/shard_map/all_to_all | solution.py:172
  39.3 13.5 %collective-permute-start.2 = (bf16[2,32,256]{2,1,0:T(8,128)(2,1)S(1)}, bf16[2,32,256]{2,1,0:T(8,128)(2,1)S(1)}, u32[]{:S(2)}, u32[]{:S(2)}) collective-permute-start(bf16[2,32,256]{2,1,0:T(8,128)(2,1)S(1)} %pad_maximum_fusion.3), channel_id=1, source_target_pairs={{0,6},{2,4},{4,2},{6,0},{1,7},{3,5},{5,3},{7,1},{8,14},{10,12},{12... | collective-permute-start | bytes 98312 | tf_op jit(solution)/shard_map/ppermute | solution.py:159
  55.5 38.8 %all-to-all-start.1 = ((bf16[4,128,256]{2,1,0:T(8,128)(2,1)}), bf16[4,128,256]{2,1,0:T(8,128)(2,1)S(1)}, u32[]{:S(2)}, u32[]{:S(2)}) async-start(bf16[4,128,256]{2,1,0:T(8,128)(2,1)} %lined.1), calls=%async_computation.1 | async-start | bytes 524288 | tf_op jit(solution)/shard_map/all_to_all | solution.py:172
  71.3 10.6 %collective-permute-start.5 = (bf16[4,32,256]{2,1,0:T(8,128)(2,1)S(1)}, bf16[4,32,256]{2,1,0:T(8,128)(2,1)S(1)}, u32[]{:S(2)}, u32[]{:S(2)}) collective-permute-start(bf16[4,32,256]{2,1,0:T(8,128)(2,1)S(1)} %pad_maximum_fusion.2), channel_id=1, source_target_pairs={{0,256},{256,512},{512,768},{768,0},{1,257},{257,513},{513,769},{7... | collective-permute-start | bytes 196616 | tf_op jit(solution)/shard_map/ppermute | solution.py:164
  74.4 7.4 %collective-permute-start.4 = (bf16[4,32,256]{2,1,0:T(8,128)(2,1)S(1)}, bf16[4,32,256]{2,1,0:T(8,128)(2,1)S(1)}, u32[]{:S(2)}, u32[]{:S(2)}) collective-permute-start(bf16[4,32,256]{2,1,0:T(8,128)(2,1)S(1)} %pad_maximum_fusion.2), channel_id=1, source_target_pairs={{0,512},{256,768},{512,0},{768,256},{1,513},{257,769},{513,1},{769... | collective-permute-start | bytes 196616 | tf_op jit(solution)/shard_map/ppermute | solution.py:164
  78.8 5.3 %collective-permute-start.3 = (bf16[4,32,256]{2,1,0:T(8,128)(2,1)S(1)}, bf16[4,32,256]{2,1,0:T(8,128)(2,1)S(1)}, u32[]{:S(2)}, u32[]{:S(2)}) collective-permute-start(bf16[4,32,256]{2,1,0:T(8,128)(2,1)S(1)} %pad_maximum_fusion.2), channel_id=1, source_target_pairs={{0,768},{256,0},{512,256},{768,512},{1,769},{257,1},{513,257},{769... | collective-permute-start | bytes 196616 | tf_op jit(solution)/shard_map/ppermute | solution.py:164
  84.2 10.4 %collective-permute-start.8 = (bf16[4,4,32,256]{3,2,1,0:T(8,128)(2,1)S(1)}, bf16[4,4,32,256]{3,2,1,0:T(8,128)(2,1)S(1)}, u32[]{:S(2)}, u32[]{:S(2)}) collective-permute-start(bf16[4,4,32,256]{3,2,1,0:T(8,128)(2,1)S(1)} %pad_maximum_fusion.1), channel_id=1, source_target_pairs={{0,8},{8,16},{16,24},{24,0},{1,9},{9,17},{17,25},{25,1},{2,10},{10... | collective-permute-start | bytes 786440 | tf_op jit(solution)/shard_map/ppermute | solution.py:164
  86.5 10.6 %collective-permute-start.7 = (bf16[4,4,32,256]{3,2,1,0:T(8,128)(2,1)S(1)}, bf16[4,4,32,256]{3,2,1,0:T(8,128)(2,1)S(1)}, u32[]{:S(2)}, u32[]{:S(2)}) collective-permute-start(bf16[4,4,32,256]{3,2,1,0:T(8,128)(2,1)S(1)} %pad_maximum_fusion.1), channel_id=1, source_target_pairs={{0,16},{8,24},{16,0},{24,8},{1,17},{9,25},{17,1},{25,9},{2,18},{10... | collective-permute-start | bytes 786440 | tf_op jit(solution)/shard_map/ppermute | solution.py:164
  90.8 9.2 %collective-permute-start.6 = (bf16[4,4,32,256]{3,2,1,0:T(8,128)(2,1)S(1)}, bf16[4,4,32,256]{3,2,1,0:T(8,128)(2,1)S(1)}, u32[]{:S(2)}, u32[]{:S(2)}) collective-permute-start(bf16[4,4,32,256]{3,2,1,0:T(8,128)(2,1)S(1)} %pad_maximum_fusion.1), channel_id=1, source_target_pairs={{0,24},{8,0},{16,8},{24,16},{1,25},{9,1},{17,9},{25,17},{2,26},{10... | collective-permute-start | bytes 786440 | tf_op jit(solution)/shard_map/ppermute | solution.py:164
  100.1 24.8 %copy-start.5 = (bf16[4,4,4,32,256]{4,3,2,1,0:T(8,128)(2,1)}, bf16[4,4,4,32,256]{4,3,2,1,0:T(8,128)(2,1)S(1)}, u32[]{:S(2)}) copy-start(bf16[4,4,4,32,256]{4,3,2,1,0:T(8,128)(2,1)S(1)} %pad_maximum_fusion.own) | copy-start | bytes 3145732
  100.1 24.7 %collective-permute-start.9 = (bf16[4,4,4,32,256]{4,3,2,1,0:T(8,128)(2,1)S(1)}, bf16[4,4,4,32,256]{4,3,2,1,0:T(8,128)(2,1)}, u32[]{:S(2)}, u32[]{:S(2)}) collective-permute-start(bf16[4,4,4,32,256]{4,3,2,1,0:T(8,128)(2,1)S(1)} %pad_maximum_fusion.own), channel_id=1, source_target_pairs={{0,1},{1,0},{2,3},{3,2},{4,5},{5,4},{6,7},{7,6},{8,9},{9,8},{10,11... | collective-permute-start | bytes 3145736 | tf_op jit(solution)/shard_map/ppermute | solution.py:164
  107.9 27.9 %all-to-all-start.2 = ((bf16[32,4,256]{2,1,0:T(4,128)(2,1)}), bf16[32,4,256]{2,1,0:T(4,128)(2,1)S(1)}, u32[]{:S(2)}, u32[]{:S(2)}) async-start(bf16[32,4,256]{2,1,0:T(4,128)(2,1)} %reshape.11), calls=%async_computation.2 | async-start | bytes 131072 | tf_op jit(solution)/shard_map/all_to_all | solution.py:172
